TPU v7x, 256 devices: a whole 4x4x8 slice. The times are simulated.
256 devices in a mesh: rep: 4 (over x_hi, core), fsdp: 64 (over y, x_lo, z).
Axes of the slice: x: 4 (x_hi: 2, x_lo: 2; x = x_hi * 2 + x_lo), y: 4, z: 8, core: 2. Of those that a mesh axis runs over, the one named last changes fastest.
Arguments:
- acts: bfloat16 [4, 16384, 8192], P('rep', 'fsdp'), may hold values from -16 to 16
- out_grad: bfloat16 [4, 16384, 512], P('rep', 'fsdp'), may hold values from -6 to 6
- weights: bfloat16 [4, 8192, 512], P('rep', 'fsdp'), may hold values from -0.0625 to 0.0625
- anchor: float32 [8192, 512], P('fsdp', 'rep'), may hold values from -0.0625 to 0.0625
- momentum: float32 [8192, 512], P('fsdp', 'rep'), may hold values from -0.078125 to 0.078125
- plan: int32 [4], replicated, may hold values 0 or 1
Outputs:
- values: bfloat16 [4, 16384, 512], P('rep', 'fsdp')
- act_grad: bfloat16 [4, 16384, 8192], P('rep', 'fsdp')
- new_weights: bfloat16 [4, 8192, 512], P('rep', 'fsdp')
- new_momentum: float32 [8192, 512], P('fsdp', 'rep')
All inputs are finite; a program needn't handle non-finite values.
Results may differ from a plain program's by a relative error of at most 0.001.
Values may be sent and summed in bfloat16 or wider, within the bound.
No kernel may reach another device: no remote copies, remote signals or barrier semaphores. Data moves between devices by JAX's collectives and lax.ppermute only.
A program may use at most 128 MiB of HBM per device.

v0:
```python
import math

import jax
import jax.numpy as jnp
from jax import lax
from jax.sharding import PartitionSpec as P

outer_rate = 0.7
momentum_coef = 0.9


def local(acts, out_grad, weights, anchor, momentum, plan):
    tokens = acts[0]
    grads_out = out_grad[0]
    local_weight = weights[0]
    total_tokens = tokens.shape[0] * lax.axis_size("fsdp")
    inner_rate = 1.0 / math.sqrt(total_tokens * tokens.shape[1])
    full_weight = lax.all_gather(local_weight, "fsdp", axis=0, tiled=True)
    values = jnp.dot(tokens, full_weight, preferred_element_type=jnp.float32).astype(jnp.bfloat16)
    act_grad = lax.dot_general(
        grads_out, full_weight, (((1,), (1,)), ((), ())), preferred_element_type=jnp.float32
    ).astype(jnp.bfloat16)
    weight_grad = lax.psum_scatter(
        lax.dot_general(
            tokens, grads_out, (((0,), (0,)), ((), ())), preferred_element_type=jnp.float32
        ),
        "fsdp",
        scatter_dimension=0,
        tiled=True,
    )
    inner_weight = local_weight.astype(jnp.float32) - inner_rate * weight_grad
    head_dim = local_weight.shape[1] // plan.shape[0]
    col_mask = jnp.repeat(plan, head_dim) > 0
    block_width = anchor.shape[1]
    offset = lax.axis_index("rep") * block_width
    group_count = lax.axis_size("rep")
    group_total = lax.psum(inner_weight, "rep")
    mom_all, anchor_all = (
        lax.all_gather(momentum, "rep", axis=1, tiled=True),
        lax.all_gather(anchor, "rep", axis=1, tiled=True),
    )
    group_mean = group_total / group_count
    pseudo_grad = anchor_all - group_mean
    mom_full = momentum_coef * mom_all + pseudo_grad
    outer_all = (anchor_all - outer_rate * (pseudo_grad + momentum_coef * mom_full)).astype(
        jnp.bfloat16
    )
    mom_next = lax.dynamic_slice_in_dim(mom_full, offset, block_width, 1)
    block_mask = lax.dynamic_slice_in_dim(col_mask, offset, block_width, 0)
    new_weight = jnp.where(col_mask[None, :], outer_all, inner_weight.astype(jnp.bfloat16))
    new_momentum = jnp.where(block_mask[None, :], mom_next, momentum)
    return (values[None], act_grad[None], new_weight[None], new_momentum)


def solution(mesh):
    placed = (
        P("rep", "fsdp", None),
        P("rep", "fsdp", None),
        P("rep", "fsdp", None),
        P("fsdp", "rep"),
        P("fsdp", "rep"),
        P(),
    )
    return jax.shard_map(
        local,
        mesh=mesh,
        in_specs=placed,
        out_specs=(
            P("rep", "fsdp", None),
            P("rep", "fsdp", None),
            P("rep", "fsdp", None),
            P("fsdp", "rep"),
        ),
        check_vma=False,
    )
```

profile of v0, /device:TPU:1, one launch (start us, length us, event | category | flops | bytes accessed | tf_op | source)
XLA Modules:
  0.0 731.3 jit_solution(17964136372567556638)
XLA Ops:
  7.2 0.0 copy-start
  7.2 0.0 all-gather.3.cloned.1.call-start
  7.2 0.7 all-gather.3.cloned.1.call-update
  7.9 0.0 reduce-scatter.2.cloned.1.call-start
  8.0 0.2 copy-done
  8.1 10.3 %fusion.4 = f32[8192,512]{1,0:T(8,128)} fusion(bf16[1,256,8192]{2,1,0:T(8,128)(2,1)} %param.6, bf16[1,256,512]{2,1,0:T(8,128)(2,1)S(1)} %copy-done), kind=kOutput, calls=%fused_computation.5 | convolution fusion | flops 2147483648 | bytes 21233664 | tf_op jit(solution)/shard_map/dot_general | solution.py:24
  18.4 0.0 reduce-scatter.2.cloned.1.call-update
  18.5 0.0 all-reduce.2.cloned.1.call-start
  18.5 0.6 copy-done.5
  19.1 0.1 broadcast_bitcast_fusion
  19.2 0.1 dynamic_slice.6
  19.2 0.0 copy-done.4
  19.3 10.4 %all_gather.10 = f32[128,512]{1,0:T(8,128)S(1)} all-gather(f32[128,128]{1,0:T(8,128)S(1)} %copy-done.4), channel_id=1, replica_groups=mesh['rep'=4,'fsdp'=64] {'rep'}, dimensions={1}, use_global_device_ids=true | all-gather | bytes 327680 | tf_op jit(solution)/shard_map/all_gather | solution.py:40
  29.6 8.6 %all_gather.11 = f32[128,512]{1,0:T(8,128)S(1)} all-gather(f32[128,128]{1,0:T(8,128)S(1)} %copy-done.3), channel_id=1, replica_groups=mesh['rep'=4,'fsdp'=64] {'rep'}, dimensions={1}, use_global_device_ids=true | all-gather | bytes 327680 | tf_op jit(solution)/shard_map/all_gather | solution.py:39
  38.2 248.9 %all-gather.3.cloned.1.call-done = bf16[1,8192,512]{2,1,0:T(8,128)(2,1)} async-done(((bf16[1,128,512]{2,1,0:T(8,128)(2,1)}), bf16[1,8192,512]{2,1,0:T(8,128)(2,1)}) %all-gather.3.cloned.1.call-update) | async-done | bytes 8388624 | tf_op jit(solution)/shard_map/all_gather | solution.py:18
  287.1 7.7 %fusion.12 = bf16[1,256,512]{2,1,0:T(8,128)(2,1)} fusion(bf16[1,8192,512]{2,1,0:T(8,128)(2,1)} %all-gather.3.cloned.1.call-done, bf16[1,256,8192]{2,1,0:T(8,128)(2,1)} %param.6), kind=kOutput, calls=%fused_computation.9 | convolution fusion | flops 2147614720 | bytes 12845056 | tf_op jit(solution)/shard_map/dot_general | solution.py:19
  294.8 335.4 %reduce-scatter.2.cloned.1.call-done = f32[128,512]{1,0:T(8,128)} async-done(((f32[8192,512]{1,0:T(8,128)}), f32[128,512]{1,0:T(8,128)}) %reduce-scatter.2.cloned.1.call-update) | async-done | bytes 262160 | tf_op jit(solution)/shard_map/reduce_scatter | solution.py:23
  630.2 1.7 convert_subtract_fusion
  631.9 0.0 all-reduce.2.cloned.1.call-update
  632.0 7.8 %fusion = bf16[1,256,8192]{2,1,0:T(8,128)(2,1)} fusion(bf16[1,8192,512]{2,1,0:T(8,128)(2,1)} %all-gather.3.cloned.1.call-done, bf16[1,256,512]{2,1,0:T(8,128)(2,1)S(1)} %copy-done), kind=kOutput, calls=%fused_computation.1 | convolution fusion | flops 2149580800 | bytes 12845056 | tf_op jit(solution)/shard_map/dot_general | solution.py:20
  639.8 81.6 %all-reduce.2.cloned.1.call-done = f32[128,512]{1,0:T(8,128)} async-done(((f32[128,512]{1,0:T(8,128)}), f32[128,512]{1,0:T(8,128)}) %all-reduce.2.cloned.1.call-update) | async-done | bytes 262160 | tf_op jit(solution)/shard_map/psum | solution.py:37
  721.3 1.0 multiply_add_fusion
  722.4 0.6 dynamic-slice_select_fusion
  723.0 1.7 fusion.20
  (9 shorter events, 0.0 us)
Async XLA Ops:
  7.2 1.0 copy-start
  7.2 279.9 %all-gather.3.cloned.1.call-start = ((), (), s32[]{:S(2)}) async-start(), calls=%async_computation.3 | async-start | bytes 8519680 | tf_op jit(solution)/shard_map/all_gather | solution.py:18
  7.9 622.3 %reduce-scatter.2.cloned.1.call-start = ((), (), s32[]{:S(2)}) async-start(), calls=%async_computation.1 | async-start | bytes 17039360 | tf_op jit(solution)/shard_map/reduce_scatter | solution.py:23
  18.4 0.7 copy-start.5
  18.4 0.9 copy-start.4
  18.4 11.2 %copy-start.3 = (f32[128,128]{1,0:T(8,128)S(1)}, f32[128,128]{1,0:T(8,128)}, u32[]{:S(2)}) copy-start(f32[128,128]{1,0:T(8,128)} %param.10) | copy-start | bytes 196612
  18.5 702.9 %all-reduce.2.cloned.1.call-start = ((), (), s32[]{:S(2)}) async-start(), calls=%async_computation.2 | async-start | bytes 524288 | tf_op jit(solution)/shard_map/psum | solution.py:37
  38.2 592.0 %copy-start.2 = (bf16[1,128,512]{2,1,0:T(8,128)(2,1)S(1)}, bf16[1,128,512]{2,1,0:T(8,128)(2,1)}, u32[]{:S(2)}) copy-start(bf16[1,128,512]{2,1,0:T(8,128)(2,1)} %param.8) | copy-start | bytes 393220
  631.9 91.1 %copy-start.1 = (f32[128,512]{1,0:T(8,128)S(1)}, f32[128,512]{1,0:T(8,128)}, u32[]{:S(2)}) copy-start(f32[128,512]{1,0:T(8,128)} %convert_subtract_fusion) | copy-start | bytes 786436
Sparse Core Ops, SparseCore 0:
  9.8 277.2 all-gather.2
  289.7 340.5 reduce-scatter.1
  632.9 88.4 all-reduce.1
where the time goes:
time: 732 us; the launch traced here: 731 us
  waiting for transfers between devices  667 us (91%)
  matrix products  25.8 us (4%)
  blocking collectives  18.9 us (3%)
  between operations  13.8 us (2%)
    reduce_scatter x1, waiting for transfers between devices, local(): lax.psum_scatter(lax.dot_general(tokens, grads_out, (((0,), (0,)), ((), (...  335 us
    all_gather x1, waiting for transfers between devices, local(): full_weight = lax.all_gather(local_weight, 'fsdp', axis=0, tiled=True)  249 us
    psum x1, waiting for transfers between devices, local(): group_total = lax.psum(inner_weight, 'rep')  81.6 us
  transfers between devices with their start and end apart: 3, of which 3 were waited for; matrix products, arithmetic and copies ran while one was open for 4% of the time, Pallas kernels for 0%

commit v1 on v0

v1 whole, which is shorter than its diff:
```python
import functools
import math

import jax
import jax.numpy as jnp
from jax import lax
from jax.experimental import pallas as pl
from jax.experimental.pallas import tpu as pltpu
from jax.sharding import Mesh, PartitionSpec as P

outer_rate = 0.7
momentum_coef = 0.9
NY, NX, NZ = 4, 2, 8
SUB = NY * NX
REP = ("xh", "core")
FSDP = ("y", "xl", "z")
ANY = pl.BlockSpec(memory_space=pl.ANY)
F32 = jnp.float32
BF16 = jnp.bfloat16


def shift_z(x, dz):
    return lax.ppermute(x, "z", [(i, (i + dz) % NZ) for i in range(NZ)])


def shift_yx(x, dy, dx):
    pairs = [
        (y * NX + c, (y + dy) % NY * NX + (c ^ dx)) for y in range(NY) for c in range(NX)
    ]
    return lax.ppermute(x, ("y", "xl"), pairs)


def grad_kernel(place_ref, own_ref, *refs):
    blocks, grads_ref, out_ref = (own_ref,) + refs[: SUB - 1], refs[SUB - 1], refs[SUB]
    total = None
    for k, block in enumerate(blocks):
        term = lax.dot_general(
            block[...],
            grads_ref[place_ref[NZ * 2 + k]],
            (((0,), (0,)), ((), ())),
            preferred_element_type=F32,
        )
        total = term if total is None else total + term
    out_ref[0] = total


def partial_grad(tokens, received, grads, place):
    width = received[0].shape[1] // NZ
    rows = tokens.shape[0]
    heads = grads.shape[2]
    grid_spec = pltpu.PrefetchScalarGridSpec(
        num_scalar_prefetch=1,
        grid=(NZ,),
        in_specs=[pl.BlockSpec((rows, width), lambda d, p: (0, p[d]))]
        + [pl.BlockSpec((rows, width), lambda d, p: (0, p[NZ + d]))] * (SUB - 1)
        + [pl.BlockSpec(grads.shape, lambda d, p: (0, 0, 0))],
        out_specs=pl.BlockSpec((1, width, heads), lambda d, p: (d, 0, 0)),
    )
    return pl.pallas_call(
        grad_kernel,
        grid_spec=grid_spec,
        out_shape=jax.ShapeDtypeStruct((NZ, width, heads), F32),
        compiler_params=pltpu.CompilerParams(vmem_limit_bytes=32 << 20),
        cost_estimate=pl.CostEstimate(
            flops=2 * SUB * rows * NZ * width * heads,
            bytes_accessed=SUB * rows * NZ * width * 2 + NZ * width * heads * 4,
            transcendentals=0,
        ),
        name="partial_grad",
    )(place, tokens, *received, grads)


def project_kernel(sizes, first, last, place_ref, tokens_ref, grads_ref, *refs):
    n = len(sizes)
    weight_refs, refs = refs[:n], refs[n:]
    if not first:
        sum_ref, _, refs = refs[0], refs[1], refs[2:]
    sum_out, grad_out, token_buf, grad_buf, in_sem, out_sem = refs
    width = token_buf.shape[2] // NX
    rows = token_buf.shape[1]
    pieces = [(i, j) for i, size in enumerate(sizes) for j in range(size)]

    def columns(k, c):
        return pl.ds(pl.multiple_of((place_ref[k] + c * NZ) * width, width), width)

    def fetch(k, c):
        return pltpu.make_async_copy(
            tokens_ref.at[:, columns(k, c)],
            token_buf.at[k, :, pl.ds(c * width, width)],
            in_sem.at[k, c],
        )

    def put(k, c):
        return pltpu.make_async_copy(
            grad_buf.at[k, :, pl.ds(c * width, width)],
            grad_out.at[:, columns(k, c)],
            out_sem.at[k, c],
        )

    for k in range(len(pieces)):
        for c in range(NX):
            fetch(k, c).start()
    grads = grads_ref[...]
    total = None if first else sum_ref[...]
    for k, (i, j) in enumerate(pieces):
        weight = weight_refs[i][pl.ds(j * NX * width, NX * width), :]
        grad_buf[k] = lax.dot_general(
            grads, weight, (((1,), (1,)), ((), ())), preferred_element_type=F32
        ).astype(BF16)
        for c in range(NX):
            put(k, c).start()
        for c in range(NX):
            fetch(k, c).wait()
        term = jnp.dot(token_buf[k], weight, preferred_element_type=F32)
        total = term if total is None else total + term
    sum_out[...] = total.astype(sum_out.dtype)
    for k in range(len(pieces)):
        for c in range(NX):
            put(k, c).wait()


def project(tokens, grads, weights, place, state, last):
    rows, heads = grads.shape
    width = tokens.shape[1] // (NY * NX * NZ)
    pair = NX * width
    sizes = tuple(w.shape[0] // pair for w in weights)
    count = sum(sizes)
    first = state is None
    whole = pl.BlockSpec(memory_space=pltpu.VMEM)
    n_in = 3 + len(weights)
    return pl.pallas_call(
        functools.partial(project_kernel, sizes, first, last),
        in_specs=[pl.BlockSpec(memory_space=pltpu.SMEM), ANY, whole]
        + [whole] * len(weights)
        + ([] if first else [whole, ANY]),
        out_specs=(whole, ANY),
        out_shape=(
            jax.ShapeDtypeStruct((rows, heads), BF16 if last else F32),
            jax.ShapeDtypeStruct(tokens.shape, BF16),
        ),
        scratch_shapes=[
            pltpu.VMEM((count, rows, pair), BF16),
            pltpu.VMEM((count, rows, pair), BF16),
            pltpu.SemaphoreType.DMA((count, NX)),
            pltpu.SemaphoreType.DMA((count, NX)),
        ],
        input_output_aliases={} if first else {n_in + 1: 1},
        compiler_params=pltpu.CompilerParams(vmem_limit_bytes=24 << 20),
        cost_estimate=pl.CostEstimate(
            flops=4 * rows * heads * count * pair,
            bytes_accessed=count * pair * (rows * 4 + heads * 2),
            transcendentals=0,
        ),
        name="project",
    )(place, tokens, grads, *weights, *(() if first else state))


def outer_kernel(plan_ref, rank_ref, near_ref, far_ref, inner_ref, state_ref, new_ref, mom_ref):
    width = mom_ref.shape[1]
    groups = state_ref.shape[0]

    def step(at, columns):
        anchor, momentum = state_ref[at, 0], state_ref[at, 1]
        mean = (near_ref[:, columns] + far_ref[:, columns]) / groups
        pseudo = anchor - mean
        return anchor, momentum, pseudo, momentum_coef * momentum + pseudo

    per_head = plan_ref.shape[0]
    for b in range(per_head):
        columns = pl.ds(b * width, width)
        anchor, _, pseudo, following = step(b, columns)
        outer = anchor - outer_rate * (pseudo + momentum_coef * following)
        synced = jnp.full(outer.shape, plan_ref[b], jnp.int32) > 0
        new_ref[:, columns] = jnp.where(synced, outer, inner_ref[:, columns]).astype(BF16)
    rank = rank_ref[0]
    columns = pl.ds(pl.multiple_of(rank * width, width), width)
    _, momentum, _, following = step(rank, columns)
    synced = jnp.full(momentum.shape, plan_ref[rank], jnp.int32) > 0
    mom_ref[...] = jnp.where(synced, following, momentum)


def outer_step(plan, rank, near, far, inner, state):
    smem = pl.BlockSpec(memory_space=pltpu.SMEM)
    whole = pl.BlockSpec(memory_space=pltpu.VMEM)
    return pl.pallas_call(
        outer_kernel,
        in_specs=[smem, smem, whole, whole, whole, whole],
        out_specs=(whole, whole),
        out_shape=(
            jax.ShapeDtypeStruct(inner.shape, BF16),
            jax.ShapeDtypeStruct(state.shape[2:], F32),
        ),
        name="outer_step",
    )(plan, rank, near, far, inner, state)


def local(acts, out_grad, weights, anchor, momentum, plan):
    tokens, grads_out, local_weight = acts[0], out_grad[0], weights[0]
    rows, depth = tokens.shape
    total_tokens = rows * NY * NX * NZ
    inner_rate = 1.0 / math.sqrt(total_tokens * depth)
    y, c, z = lax.axis_index("y"), lax.axis_index("xl"), lax.axis_index("z")
    rank = lax.axis_index(REP)
    part = depth // SUB

    block = lax.all_gather(local_weight, ("y", "xl"), axis=0, tiled=True)
    grads = lax.all_gather(grads_out, ("y", "xl"), axis=0, tiled=False)
    state = lax.all_gather(jnp.stack([anchor, momentum]), REP, axis=0, tiled=False)

    received, owners = [], [y * NX + c]
    for dy, dx in [(2, 1), (1, 1), (3, 1), (2, 0), (1, 0), (3, 0), (0, 1)]:
        to = (y + dy) % NY * NX + (c ^ dx)
        piece = lax.dynamic_slice(tokens, (0, to * part), (rows, part))
        received.append(shift_yx(piece, dy, dx))
        owners.append((y - dy) % NY * NX + (c ^ dx))
    relative = [(z + d) % NZ for d in range(NZ)]
    place = jnp.stack([(y * NX + c) * NZ + r for r in relative] + relative + owners)
    terms = partial_grad(tokens, received, grads, place.astype(jnp.int32))

    half = terms.shape[1] // 2
    right = shift_z(terms[4, :half], 1)
    left = shift_z(terms[4, half:], -1)
    right = jnp.concatenate([terms[3, :half] + right, terms[3, half:]])
    left = jnp.concatenate([terms[5, :half], terms[5, half:] + left])
    for d in (2, 1):
        right, left = shift_z(right, 1), shift_z(left, -1)
        right, left = terms[d] + right, terms[NZ - d] + left
    right, left = shift_z(right, 1), shift_z(left, -1)
    inner = local_weight.astype(F32) - inner_rate * (terms[0] + right + left)

    def places(dz, ys=range(NY)):
        return [v * (NX * NZ) + (z + dz) % NZ for v in ys]

    def at(*lists):
        return jnp.stack(sum(lists, [])).astype(jnp.int32)

    carry = project(tokens, grads_out, [block], at(places(0)), None, False)
    right = left = block
    for k in (1, 2, 3):
        right, left = shift_z(right, 1), shift_z(left, -1)
        carry = project(
            tokens, grads_out, [right, left], at(places(-k), places(k)), carry, False
        )
    half = block.shape[0] // 2
    right, left = shift_z(right[:half], 1), shift_z(left[half:], -1)
    values, act_grad = project(
        tokens, grads_out, [right, left], at(places(4)), carry, True
    )

    near = inner + lax.ppermute(inner, "core", [(0, 1), (1, 0)])
    far = lax.ppermute(near, "xh", [(0, 1), (1, 0)])
    new_weight, new_momentum = outer_step(
        plan, jnp.reshape(rank, (1,)).astype(jnp.int32), near, far, inner, state
    )
    return values[None], act_grad[None], new_weight[None], new_momentum


def solution(mesh):
    fine = Mesh(mesh.devices.reshape(2, 2, NY, NX, NZ), ("xh", "core", "y", "xl", "z"))
    placed = (
        P(REP, FSDP, None),
        P(REP, FSDP, None),
        P(REP, FSDP, None),
        P(FSDP, REP),
        P(FSDP, REP),
        P(),
    )
    return jax.shard_map(
        local,
        mesh=fine,
        in_specs=placed,
        out_specs=(
            P(REP, FSDP, None),
            P(REP, FSDP, None),
            P(REP, FSDP, None),
            P(FSDP, REP),
        ),
        check_vma=False,
    )
```

time: 732 us -> 283 us (0.39)
  waiting for transfers between devices: 667 us -> 144 us
  starting transfers between devices: 0.12 us -> 47.4 us
  Pallas kernels: 0 us -> 30.6 us
  local copies, waits for them, and re-layouts: 0.94 us -> 29.7 us
  matrix products: 25.8 us -> 0 us
  blocking collectives: 18.9 us -> 9.81 us
    reduce_scatter x1 -> x0, waiting for transfers between devices: 335 us -> none  [local(): lax.psum_scatter(lax.dot_general(tokens, grads_out, (((0,), (0,)), ((), (...]
    all_gather x1 -> x2, waiting for transfers between devices: 249 us -> 59.5 us  [the longest x1 40.2 us: local(): grads = lax.all_gather(grads_out, ('y', 'xl'), axis=0, tiled=False)]
    ppermute x0 -> x25, waiting for transfers between devices: none -> 83.5 us  [the longest x16 60.3 us: shift_z(): return lax.ppermute(x, 'z', [(i, (i + dz) % NZ) for i in range(NZ)])]
    psum x1 -> x0, waiting for transfers between devices: 81.6 us -> none  [local(): group_total = lax.psum(inner_weight, 'rep')]
    ppermute x0 -> x25, starting transfers between devices: none -> 47.3 us  [the longest x7 21.9 us: shift_yx(): return lax.ppermute(x, ('y', 'xl'), pairs)]
    pallas_call x0 -> x7, Pallas kernels: none -> 30.6 us  [the longest x5 22.5 us: project(): pl.pallas_call(functools.partial(project_kernel, sizes, first, last), in_...]
    dot_general x3 -> x0, matrix products: 25.8 us -> none  [the longest x1 10.3 us: local(): lax.dot_general(tokens, grads_out, (((0,), (0,)), ((), ())), preferred_el...]
    unnamed x12 -> x56, local copies, waits for them, and re-layouts: 0.79 us -> 23 us
  transfers between devices with their start and end apart: 3 -> 27, of which waited for: 3 -> 12; matrix products, arithmetic and copies ran while one was open for 4% -> 4% of each run, Pallas kernels for 0% -> 10%
where the time goes in v1:
time: 283 us; the launch traced here: 282 us
  waiting for transfers between devices  144 us (51%)
  starting transfers between devices  47.4 us (17%)
  Pallas kernels  30.6 us (11%)
  local copies, waits for them, and re-layouts  29.7 us (10%)
  between operations  14.4 us (5%)
  blocking collectives  9.81 us (3%)
  other arithmetic  5.36 us (2%)
    ppermute x16, waiting for transfers between devices, shift_z(): return lax.ppermute(x, 'z', [(i, (i + dz) % NZ) for i in range(NZ)])  60.3 us
    all_gather x1, waiting for transfers between devices, local(): grads = lax.all_gather(grads_out, ('y', 'xl'), axis=0, tiled=False)  40.2 us
    ppermute x7, waiting for transfers between devices, shift_yx(): return lax.ppermute(x, ('y', 'xl'), pairs)  23.2 us
    unnamed x56, local copies, waits for them, and re-layouts  23 us
    pallas_call x5, Pallas kernels, project(): pl.pallas_call(functools.partial(project_kernel, sizes, first, last), in_...  22.5 us
    ppermute x7, starting transfers between devices, shift_yx(): return lax.ppermute(x, ('y', 'xl'), pairs)  21.9 us
    all_gather x1, waiting for transfers between devices, local(): block = lax.all_gather(local_weight, ('y', 'xl'), axis=0, tiled=True)  19.2 us
    ppermute x16, starting transfers between devices, shift_z(): return lax.ppermute(x, 'z', [(i, (i + dz) % NZ) for i in range(NZ)])  19.1 us
  transfers between devices with their start and end apart: 27, of which 12 were waited for; matrix products, arithmetic and copies ran while one was open for 4% of the time, Pallas kernels for 10%

profile of v1, /device:TPU:1, one launch (start us, length us, event | category | flops | bytes accessed | tf_op | source)
XLA Modules:
  0.0 281.6 jit_solution(9014619926321713563)
XLA Ops:
  8.7 3.6 %dynamic-slice_bitcast_fusion = (bf16[256,1024]{1,0:T(8,128)(2,1)}, bf16[256,1024]{1,0:T(8,128)(2,1)S(1)}, bf16[256,1024]{1,0:T(8,128)(2,1)S(1)}, bf16[256,1024]...) fusion(bf16[1,256,8192]{2,1,0:T(8,128)(2,1)} %param.6, ...), kind=kLoop, calls=%fused_computation | loop fusion | bytes 7340060 | tf_op jit(solution)/shard_map/dynamic_slice | solution.py:213
  12.3 4.5 %collective-permute-start.10 = (bf16[256,1024]{1,0:T(8,128)(2,1)S(1)}, bf16[256,1024]{1,0:T(8,128)(2,1)S(1)}, u32[]{:S(2)}, u32[]{:S(2)}) collective-permute-start(bf16[256,1024]{1,0:T(8,128)(2,1)S(1)} %get-tuple-element.31), channel_id=1, source_target_pairs={{0,56},{8,48},{16,8},{24,0},{32,24},{40,16},{48,40},{56,32},{1,57}... | collective-permute-start | bytes 1572872 | tf_op jit(solution)/shard_map/ppermute | solution.py:30
  20.1 10.3 %collective-permute-done.10.refs_2_ = bf16[256,1024]{1,0:T(8,128)(2,1)S(1)} collective-permute-done((bf16[256,1024]{1,0:T(8,128)(2,1)S(1)}, bf16[256,1024]{1,0:T(8,128)(2,1)S(1)}, u32[]{:S(2)}, u32[]{:S(2)}) %collective-permute-start.10) | collective-permute-done | bytes 524320 | tf_op jit(solution)/shard_map/ppermute | solution.py:30
  32.8 13.4 %collective-permute-start.9 = (bf16[256,1024]{1,0:T(8,128)(2,1)}, bf16[256,1024]{1,0:T(8,128)(2,1)S(1)}, u32[]{:S(2)}, u32[]{:S(2)}) collective-permute-start(bf16[256,1024]{1,0:T(8,128)(2,1)} %get-tuple-element.32), channel_id=1, source_target_pairs={{0,24},{8,16},{16,40},{24,32},{32,56},{40,48},{48,8},{56,0},{1,25}... | collective-permute-start | bytes 1572872 | tf_op jit(solution)/shard_map/ppermute | solution.py:30
  49.2 19.2 %all-gather.7.cloned.1.call-done = bf16[1,1024,512]{2,1,0:T(8,128)(2,1)} async-done(((bf16[1,128,512]{2,1,0:T(8,128)(2,1)}), bf16[1,1024,512]{2,1,0:T(8,128)(2,1)}) %all-gather.7.cloned.1.call-update) | async-done | bytes 1048592 | tf_op jit(solution)/shard_map/all_gather | solution.py:206
  74.0 10.7 %collective-permute-done.9.refs_1_ = bf16[256,1024]{1,0:T(8,128)(2,1)S(1)} collective-permute-done((bf16[256,1024]{1,0:T(8,128)(2,1)}, bf16[256,1024]{1,0:T(8,128)(2,1)S(1)}, u32[]{:S(2)}, u32[]{:S(2)}) %collective-permute-start.9) | collective-permute-done | bytes 524320 | tf_op jit(solution)/shard_map/ppermute | solution.py:30
  85.4 40.2 %all-gather.5.cloned.1.call-done.refs_7_ = bf16[8,256,512]{2,1,0:T(8,128)(2,1)} async-done(((bf16[1,256,512]{2,1,0:T(8,128)(2,1)}), bf16[8,256,512]{2,1,0:T(8,128)(2,1)}) %all-gather.5.cloned.1.call-update) | async-done | bytes 2097168 | tf_op jit(solution)/shard_map/all_gather | solution.py:207
  136.8 6.0 %partial_grad.1 = f32[8,128,512]{2,1,0:T(8,128)S(1)} custom-call(s32[24]{0:T(128)S(1)} %stack.241.place_ref, bf16[256,8192]{1,0:T(8,128)(2,1)S(1)} %bitcast.120, bf16[256,1024]{1,0:T(8,128)(2,1)S(1)} %copy-done.19, bf16[256,1024]{1,0:T(8,128)(2,1)S(1)} %copy-done.21, bf16[256,1024]{1,0:T(8,128)(2,1)S(1)} %copy-done.9, bf16[256,1024]{1,0:T(8,128)(2,1)S(1)} %copy-done.11, ...), custom_call_target="tpu_custom_call" | custom-call | flops 2147483648 | bytes 6291456 | tf_op jit(solution)/shard_map/partial_grad/pallas_call | solution.py:59
  142.9 3.6 %collective-permute-start.19 = (f32[64,512]{1,0:T(8,128)S(1)}, f32[64,512]{1,0:T(8,128)S(1)}, u32[]{:S(2)}, u32[]{:S(2)}) collective-permute-start(f32[64,512]{1,0:T(8,128)S(1)} %get-tuple-element.40), channel_id=1, source_target_pairs={{0,7},{1,0},{2,1},{3,2},{4,3},{5,4},{6,5},{7,6},{8,15},{9,8},{10,9... | collective-permute-start | bytes 393224 | tf_op jit(solution)/shard_map/ppermute | solution.py:23
  146.6 2.7 collective-permute-done.15
  153.9 2.9 %collective-permute-done.16 = f32[128,512]{1,0:T(8,128)S(1)} collective-permute-done((f32[128,512]{1,0:T(8,128)S(1)}, f32[128,512]{1,0:T(8,128)S(1)}, u32[]{:S(2)}, u32[]{:S(2)}) %collective-permute-start.16) | collective-permute-done | bytes 262176 | tf_op jit(solution)/shard_map/ppermute | solution.py:23
  156.9 23.4 %collective-permute-done.20 = f32[128,512]{1,0:T(8,128)S(1)} collective-permute-done((f32[128,512]{1,0:T(8,128)S(1)}, f32[128,512]{1,0:T(8,128)S(1)}, u32[]{:S(2)}, u32[]{:S(2)}) %collective-permute-start.20) | collective-permute-done | bytes 262176 | tf_op jit(solution)/shard_map/ppermute | solution.py:23
  180.2 4.6 %collective-permute-done.17 = f32[128,512]{1,0:T(8,128)S(1)} collective-permute-done((f32[128,512]{1,0:T(8,128)S(1)}, f32[128,512]{1,0:T(8,128)S(1)}, u32[]{:S(2)}, u32[]{:S(2)}) %collective-permute-start.17) | collective-permute-done | bytes 262176 | tf_op jit(solution)/shard_map/ppermute | solution.py:23
  194.2 20.3 %collective-permute-done.18 = f32[128,512]{1,0:T(8,128)} collective-permute-done((f32[128,512]{1,0:T(8,128)}, f32[128,512]{1,0:T(8,128)}, u32[]{:S(2)}, u32[]{:S(2)}) %collective-permute-start.18) | collective-permute-done | bytes 262176 | tf_op jit(solution)/shard_map/ppermute | solution.py:23
  214.5 4.5 %collective-permute-done.22 = f32[128,512]{1,0:T(8,128)} collective-permute-done((f32[128,512]{1,0:T(8,128)}, f32[128,512]{1,0:T(8,128)}, u32[]{:S(2)}, u32[]{:S(2)}) %collective-permute-start.22) | collective-permute-done | bytes 262176 | tf_op jit(solution)/shard_map/ppermute | solution.py:23
  220.8 3.5 %collective-permute-start.23 = (f32[128,512]{1,0:T(8,128)}, f32[128,512]{1,0:T(8,128)}, u32[]{:S(2)}, u32[]{:S(2)}) collective-permute-start(f32[128,512]{1,0:T(8,128)} %fusion.7.inner_ref), channel_id=1, source_target_pairs={{0,64},{64,0},{1,65},{65,1},{2,66},{66,2},{3,67},{67,3},{4,68},{68... | collective-permute-start | bytes 786440 | tf_op jit(solution)/shard_map/ppermute | solution.py:250
  227.4 2.7 collective-permute-start.7
  230.1 9.8 %all-gather.1 = f32[8,128,128]{2,1,0:T(8,128)} all-gather(f32[2,128,128]{2,1,0:T(8,128)S(1)} %copy-done.24), channel_id=3, replica_groups=mesh['xh'=2,'core'=2,'y'=4,'xl'=2,'z'=8] {'xh','core'}, dimensions={0}, use_global_device_ids=true | all-gather | bytes 655360 | tf_op jit(solution)/shard_map/all_gather | solution.py:208
  243.3 3.0 %project.5 = (f32[256,512]{1,0:T(8,128)S(1)}, bf16[256,8192]{1,0:T(8,128)(2,1)}) custom-call(s32[4]{0:T(128)S(1)} %pad_add_fusion.1.place_ref, bf16[256,8192]{1,0:T(8,128)(2,1)S(1)} %bitcast.121, bf16[256,512]{1,0:T(8,128)(2,1)S(1)} %bitcast.126, bf16[1024,512]{1,0:T(8,128)(2,1)S(1)} %bitcast.133), custom_call_target="tpu_custom_call" | custom-call | flops 536870912 | bytes 2097152 | tf_op jit(solution)/shard_map/project/pallas_call | solution.py:131
  247.4 2.7 collective-permute-start.24
  250.2 5.2 %project.6 = (f32[256,512]{1,0:T(8,128)S(1)}, bf16[256,8192]{1,0:T(8,128)(2,1)}) custom-call(s32[8]{0:T(128)S(1)} %stack.216.place_ref, bf16[256,8192]{1,0:T(8,128)(2,1)S(1)} %bitcast.122, bf16[256,512]{1,0:T(8,128)(2,1)S(1)} %bitcast.127, bf16[1024,512]{1,0:T(8,128)(2,1)S(1)} %copy-done.7, ...), custom_call_target="tpu_custom_call", output_to_operand_aliasing={{1}: (6, {})} | custom-call | flops 1073741824 | bytes 4194304 | tf_op jit(solution)/shard_map/project/pallas_call | solution.py:131
  255.4 5.5 %project.7 = (f32[256,512]{1,0:T(8,128)S(1)}, bf16[256,8192]{1,0:T(8,128)(2,1)}) custom-call(s32[8]{0:T(128)S(1)} %stack.207.place_ref, bf16[256,8192]{1,0:T(8,128)(2,1)S(1)} %bitcast.123, bf16[256,512]{1,0:T(8,128)(2,1)S(1)} %bitcast.128, bf16[1024,512]{1,0:T(8,128)(2,1)} %collective-permute-done.1.refs_0_, ...), custom_call_target="tpu_custom_call", output_to_operand_aliasing={{1}: (6, {})} | custom-call | flops 1073741824 | bytes 4194304 | tf_op jit(solution)/shard_map/project/pallas_call | solution.py:131
  260.9 5.2 %project.8 = (f32[256,512]{1,0:T(8,128)S(1)}, bf16[256,8192]{1,0:T(8,128)(2,1)}) custom-call(s32[8]{0:T(128)S(1)} %stack.198.place_ref, bf16[256,8192]{1,0:T(8,128)(2,1)S(1)} %bitcast.124, bf16[256,512]{1,0:T(8,128)(2,1)S(1)} %bitcast.129, bf16[1024,512]{1,0:T(8,128)(2,1)S(1)} %collective-permute-done.2.refs_0_, ...), custom_call_target="tpu_custom_call", output_to_operand_aliasing={{1}: (6, {})} | custom-call | flops 1073741824 | bytes 4194304 | tf_op jit(solution)/shard_map/project/pallas_call | solution.py:131
  271.1 3.6 %project.9 = (bf16[256,512]{1,0:T(8,128)(2,1)}, bf16[256,8192]{1,0:T(8,128)(2,1)}) custom-call(s32[4]{0:T(128)S(1)} %pad_add_fusion.place_ref, bf16[256,8192]{1,0:T(8,128)(2,1)S(1)} %bitcast.125, bf16[256,512]{1,0:T(8,128)(2,1)S(1)} %bitcast.130, bf16[512,512]{1,0:T(8,128)(2,1)S(1)} %collective-permute-done.3.refs_0_, ...), custom_call_target="tpu_custom_call", output_to_operand_aliasing={{1}: (6, {})} | custom-call | flops 536870912 | bytes 2097152 | tf_op jit(solution)/shard_map/project/pallas_call | solution.py:131
  (115 shorter events, 55.9 us)
Async XLA Ops:
  7.2 61.2 %all-gather.7.cloned.1.call-start = ((), (), s32[]{:S(2)}) async-start(), calls=%async_computation.1 | async-start | bytes 1179648 | tf_op jit(solution)/shard_map/all_gather | solution.py:206
  7.9 117.8 %all-gather.5.cloned.1.call-start = ((), (), s32[]{:S(2)}) async-start(), calls=%async_computation | async-start | bytes 2359296 | tf_op jit(solution)/shard_map/all_gather | solution.py:207
  12.3 18.1 %collective-permute-start.10 = (bf16[256,1024]{1,0:T(8,128)(2,1)S(1)}, bf16[256,1024]{1,0:T(8,128)(2,1)S(1)}, u32[]{:S(2)}, u32[]{:S(2)}) collective-permute-start(bf16[256,1024]{1,0:T(8,128)(2,1)S(1)} %get-tuple-element.31), channel_id=1, source_target_pairs={{0,56},{8,48},{16,8},{24,0},{32,24},{40,16},{48,40},{56,32},{1,57}... | collective-permute-start | bytes 1572872 | tf_op jit(solution)/shard_map/ppermute | solution.py:30
  16.8 15.2 %collective-permute-start.11 = (bf16[256,1024]{1,0:T(8,128)(2,1)S(1)}, bf16[256,1024]{1,0:T(8,128)(2,1)S(1)}, u32[]{:S(2)}, u32[]{:S(2)}) collective-permute-start(bf16[256,1024]{1,0:T(8,128)(2,1)S(1)} %get-tuple-element.30), channel_id=1, source_target_pairs={{0,32},{8,40},{16,48},{24,56},{32,0},{40,8},{48,16},{56,24},{1,33}... | collective-permute-start | bytes 1572872 | tf_op jit(solution)/shard_map/ppermute | solution.py:30
  17.2 31.2 %collective-permute-start.12 = (bf16[256,1024]{1,0:T(8,128)(2,1)S(1)}, bf16[256,1024]{1,0:T(8,128)(2,1)S(1)}, u32[]{:S(2)}, u32[]{:S(2)}) collective-permute-start(bf16[256,1024]{1,0:T(8,128)(2,1)S(1)} %get-tuple-element.29), channel_id=1, source_target_pairs={{0,16},{8,24},{16,32},{24,40},{32,48},{40,56},{48,0},{56,8},{1,17}... | collective-permute-start | bytes 1572872 | tf_op jit(solution)/shard_map/ppermute | solution.py:30
  17.9 51.8 %collective-permute-start.13 = (bf16[256,1024]{1,0:T(8,128)(2,1)}, bf16[256,1024]{1,0:T(8,128)(2,1)S(1)}, u32[]{:S(2)}, u32[]{:S(2)}) collective-permute-start(bf16[256,1024]{1,0:T(8,128)(2,1)} %get-tuple-element.34), channel_id=1, source_target_pairs={{0,48},{8,56},{16,0},{24,8},{32,16},{40,24},{48,32},{56,40},{1,49}... | collective-permute-start | bytes 1572872 | tf_op jit(solution)/shard_map/ppermute | solution.py:30
  19.8 52.5 %collective-permute-start.14 = (bf16[256,1024]{1,0:T(8,128)(2,1)}, bf16[256,1024]{1,0:T(8,128)(2,1)S(1)}, u32[]{:S(2)}, u32[]{:S(2)}) collective-permute-start(bf16[256,1024]{1,0:T(8,128)(2,1)} %get-tuple-element.28), channel_id=1, source_target_pairs={{0,8},{8,0},{16,24},{24,16},{32,40},{40,32},{48,56},{56,48},{1,9},... | collective-permute-start | bytes 1572872 | tf_op jit(solution)/shard_map/ppermute | solution.py:30
  31.3 42.0 %collective-permute-start.8 = (bf16[256,1024]{1,0:T(8,128)(2,1)}, bf16[256,1024]{1,0:T(8,128)(2,1)S(1)}, u32[]{:S(2)}, u32[]{:S(2)}) collective-permute-start(bf16[256,1024]{1,0:T(8,128)(2,1)} %get-tuple-element.33), channel_id=1, source_target_pairs={{0,40},{8,32},{16,56},{24,48},{32,8},{40,0},{48,24},{56,16},{1,41}... | collective-permute-start | bytes 1572872 | tf_op jit(solution)/shard_map/ppermute | solution.py:30
  32.8 51.9 %collective-permute-start.9 = (bf16[256,1024]{1,0:T(8,128)(2,1)}, bf16[256,1024]{1,0:T(8,128)(2,1)S(1)}, u32[]{:S(2)}, u32[]{:S(2)}) collective-permute-start(bf16[256,1024]{1,0:T(8,128)(2,1)} %get-tuple-element.32), channel_id=1, source_target_pairs={{0,24},{8,16},{16,40},{24,32},{32,56},{40,48},{48,8},{56,0},{1,25}... | collective-permute-start | bytes 1572872 | tf_op jit(solution)/shard_map/ppermute | solution.py:30
  68.4 81.0 %collective-permute-start = (bf16[1024,512]{1,0:T(8,128)(2,1)}, bf16[1024,512]{1,0:T(8,128)(2,1)S(1)}, u32[]{:S(2)}, u32[]{:S(2)}) collective-permute-start(bf16[1024,512]{1,0:T(8,128)(2,1)} %bitcast.131), channel_id=1, source_target_pairs={{0,1},{1,2},{2,3},{3,4},{4,5},{5,6},{6,7},{7,0},{8,9},{9,10},{10,1... | collective-permute-start | bytes 3145736 | tf_op jit(solution)/shard_map/ppermute | solution.py:23
  70.5 80.7 %collective-permute-start.4 = (bf16[1024,512]{1,0:T(8,128)(2,1)}, bf16[1024,512]{1,0:T(8,128)(2,1)}, u32[]{:S(2)}, u32[]{:S(2)}) collective-permute-start(bf16[1024,512]{1,0:T(8,128)(2,1)} %bitcast.132), channel_id=1, source_target_pairs={{0,7},{1,0},{2,1},{3,2},{4,3},{5,4},{6,5},{7,6},{8,15},{9,8},{10,9... | collective-permute-start | bytes 3145736 | tf_op jit(solution)/shard_map/ppermute | solution.py:23
  149.3 7.4 %collective-permute-start.16 = (f32[128,512]{1,0:T(8,128)S(1)}, f32[128,512]{1,0:T(8,128)S(1)}, u32[]{:S(2)}, u32[]{:S(2)}) collective-permute-start(f32[128,512]{1,0:T(8,128)S(1)} %pad_maximum_fusion), channel_id=1, source_target_pairs={{0,1},{1,2},{2,3},{3,4},{4,5},{5,6},{6,7},{7,0},{8,9},{9,10},{10,1... | collective-permute-start | bytes 786440 | tf_op jit(solution)/shard_map/ppermute | solution.py:23
  149.5 36.8 %collective-permute-start.1 = (bf16[1024,512]{1,0:T(8,128)(2,1)S(1)}, bf16[1024,512]{1,0:T(8,128)(2,1)}, u32[]{:S(2)}, u32[]{:S(2)}) collective-permute-start(bf16[1024,512]{1,0:T(8,128)(2,1)S(1)} %collective-permute-done.refs_0_), channel_id=1, source_target_pairs={{0,1},{1,2},{2,3},{3,4},{4,5},{5,6},{6,7},{7,0},{8,9},{9,10},{10,1... | collective-permute-start | bytes 3145736 | tf_op jit(solution)/shard_map/ppermute | solution.py:23
  151.2 35.9 %collective-permute-start.5 = (bf16[1024,512]{1,0:T(8,128)(2,1)}, bf16[1024,512]{1,0:T(8,128)(2,1)}, u32[]{:S(2)}, u32[]{:S(2)}) collective-permute-start(bf16[1024,512]{1,0:T(8,128)(2,1)} %collective-permute-done.4.refs_1_), channel_id=1, source_target_pairs={{0,7},{1,0},{2,1},{3,2},{4,3},{5,4},{6,5},{7,6},{8,15},{9,8},{10,9... | collective-permute-start | bytes 3145736 | tf_op jit(solution)/shard_map/ppermute | solution.py:23
  152.2 28.0 %collective-permute-start.20 = (f32[128,512]{1,0:T(8,128)S(1)}, f32[128,512]{1,0:T(8,128)S(1)}, u32[]{:S(2)}, u32[]{:S(2)}) collective-permute-start(f32[128,512]{1,0:T(8,128)S(1)} %pad_maximum_fusion.1), channel_id=1, source_target_pairs={{0,7},{1,0},{2,1},{3,2},{4,3},{5,4},{6,5},{7,6},{8,15},{9,8},{10,9... | collective-permute-start | bytes 786440 | tf_op jit(solution)/shard_map/ppermute | solution.py:23
  156.8 28.0 %collective-permute-start.17 = (f32[128,512]{1,0:T(8,128)S(1)}, f32[128,512]{1,0:T(8,128)S(1)}, u32[]{:S(2)}, u32[]{:S(2)}) collective-permute-start(f32[128,512]{1,0:T(8,128)S(1)} %fusion.2), channel_id=1, source_target_pairs={{0,1},{1,2},{2,3},{3,4},{4,5},{5,6},{6,7},{7,0},{8,9},{9,10},{10,1... | collective-permute-start | bytes 786440 | tf_op jit(solution)/shard_map/ppermute | solution.py:23
  186.2 38.5 %collective-permute-start.2 = (bf16[1024,512]{1,0:T(8,128)(2,1)}, bf16[1024,512]{1,0:T(8,128)(2,1)S(1)}, u32[]{:S(2)}, u32[]{:S(2)}) collective-permute-start(bf16[1024,512]{1,0:T(8,128)(2,1)} %collective-permute-done.1.refs_0_), channel_id=1, source_target_pairs={{0,1},{1,2},{2,3},{3,4},{4,5},{5,6},{6,7},{7,0},{8,9},{9,10},{10,1... | collective-permute-start | bytes 3145736 | tf_op jit(solution)/shard_map/ppermute | solution.py:23
  187.1 38.4 %collective-permute-start.6 = (bf16[1024,512]{1,0:T(8,128)(2,1)}, bf16[1024,512]{1,0:T(8,128)(2,1)}, u32[]{:S(2)}, u32[]{:S(2)}) collective-permute-start(bf16[1024,512]{1,0:T(8,128)(2,1)} %collective-permute-done.5.refs_1_), channel_id=1, source_target_pairs={{0,7},{1,0},{2,1},{3,2},{4,3},{5,4},{6,5},{7,6},{8,15},{9,8},{10,9... | collective-permute-start | bytes 3145736 | tf_op jit(solution)/shard_map/ppermute | solution.py:23
  188.9 25.6 %collective-permute-start.18 = (f32[128,512]{1,0:T(8,128)}, f32[128,512]{1,0:T(8,128)}, u32[]{:S(2)}, u32[]{:S(2)}) collective-permute-start(f32[128,512]{1,0:T(8,128)} %get-tuple-element.35), channel_id=1, source_target_pairs={{0,1},{1,2},{2,3},{3,4},{4,5},{5,6},{6,7},{7,0},{8,9},{9,10},{10,1... | collective-permute-start | bytes 786440 | tf_op jit(solution)/shard_map/ppermute | solution.py:23
  191.6 27.4 %collective-permute-start.22 = (f32[128,512]{1,0:T(8,128)}, f32[128,512]{1,0:T(8,128)}, u32[]{:S(2)}, u32[]{:S(2)}) collective-permute-start(f32[128,512]{1,0:T(8,128)} %fusion.1), channel_id=1, source_target_pairs={{0,7},{1,0},{2,1},{3,2},{4,3},{5,4},{6,5},{7,6},{8,15},{9,8},{10,9... | collective-permute-start | bytes 786440 | tf_op jit(solution)/shard_map/ppermute | solution.py:23
  220.8 25.5 %collective-permute-start.23 = (f32[128,512]{1,0:T(8,128)}, f32[128,512]{1,0:T(8,128)}, u32[]{:S(2)}, u32[]{:S(2)}) collective-permute-start(f32[128,512]{1,0:T(8,128)} %fusion.7.inner_ref), channel_id=1, source_target_pairs={{0,64},{64,0},{1,65},{65,1},{2,66},{66,2},{3,67},{67,3},{4,68},{68... | collective-permute-start | bytes 786440 | tf_op jit(solution)/shard_map/ppermute | solution.py:250
  225.5 43.4 %collective-permute-start.3 = (bf16[512,512]{1,0:T(8,128)(2,1)}, bf16[512,512]{1,0:T(8,128)(2,1)S(1)}, u32[]{:S(2)}, u32[]{:S(2)}) collective-permute-start(bf16[512,512]{1,0:T(8,128)(2,1)} %slice.52), channel_id=1, source_target_pairs={{0,1},{1,2},{2,3},{3,4},{4,5},{5,6},{6,7},{7,0},{8,9},{9,10},{10,1... | collective-permute-start | bytes 1572872 | tf_op jit(solution)/shard_map/ppermute | solution.py:23
  227.4 41.5 %collective-permute-start.7 = (bf16[512,512]{1,0:T(8,128)(2,1)}, bf16[512,512]{1,0:T(8,128)(2,1)S(1)}, u32[]{:S(2)}, u32[]{:S(2)}) collective-permute-start(bf16[512,512]{1,0:T(8,128)(2,1)} %slice.53), channel_id=1, source_target_pairs={{0,7},{1,0},{2,1},{3,2},{4,3},{5,4},{6,5},{7,6},{8,15},{9,8},{10,9... | collective-permute-start | bytes 1572872 | tf_op jit(solution)/shard_map/ppermute | solution.py:23
  247.4 18.7 %collective-permute-start.24 = (f32[128,512]{1,0:T(8,128)S(1)}, f32[128,512]{1,0:T(8,128)S(1)}, u32[]{:S(2)}, u32[]{:S(2)}) collective-permute-start(f32[128,512]{1,0:T(8,128)S(1)} %add.452.near_ref), channel_id=1, source_target_pairs={{0,128},{128,0},{1,129},{129,1},{2,130},{130,2},{3,131},{131,3},{4... | collective-permute-start | bytes 786440 | tf_op jit(solution)/shard_map/ppermute | solution.py:251
  (31 other events, 305.7 us)
Sparse Core Ops, SparseCore 0:
  9.8 58.5 all-gather.6
  70.2 55.4 all-gather.4

commit v2 on v1

v2 whole, which is shorter than its diff:
```python
import functools
import math

import jax
import jax.numpy as jnp
from jax import lax
from jax.experimental import pallas as pl
from jax.experimental.pallas import tpu as pltpu
from jax.sharding import Mesh, PartitionSpec as P

outer_rate = 0.7
momentum_coef = 0.9
NY, NX, NZ = 4, 2, 8
SUB = NY * NX
REP = ("xh", "core")
FSDP = ("y", "xl", "z")
HBM = pl.BlockSpec(memory_space=pltpu.HBM)
F32 = jnp.float32
BF16 = jnp.bfloat16
STAGES = ((4, 3, 5), (2, 6, 1, 7, 0))


def shift_z(x, dz):
    return lax.ppermute(x, "z", [(i, (i + dz) % NZ) for i in range(NZ)])


def shift_y(x, dy):
    return lax.ppermute(x, "y", [(i, (i + dy) % NY) for i in range(NY)])


def shift_x(x):
    return lax.ppermute(x, "xl", [(0, 1), (1, 0)])


def shift_core(x):
    return lax.ppermute(x, "core", [(0, 1), (1, 0)])


def shift_far(x):
    return lax.ppermute(x, "xh", [(0, 1), (1, 0)])


def sort_kernel(place_ref, tokens_ref, grads_ref, *refs):
    n = len(STAGES)
    outs, (tokens_buf, grads_buf), bufs, (in_sem, out_sem) = (
        refs[:n], refs[n : n + 2], refs[n + 2 : 2 * n + 2], refs[2 * n + 2 :]
    )
    heads = grads_ref.shape[1]
    part = tokens_buf.shape[2]
    width = part // NZ
    fetches = [pltpu.make_async_copy(grads_ref, grads_buf, in_sem.at[SUB])]
    for j in range(SUB):
        fetches.append(
            pltpu.make_async_copy(
                tokens_ref.at[:, pl.ds(j * part, part)], tokens_buf.at[j], in_sem.at[j]
            )
        )
    for fetch in fetches:
        fetch.start()
    fetches[0].wait()
    puts = []
    for j in range(SUB):
        fetches[1 + j].wait()
        bufs[0][j, :, :heads] = grads_buf[...]
        for s, stage in enumerate(STAGES):
            start = heads if s == 0 else 0
            for i, d in enumerate(stage):
                source = pl.multiple_of(place_ref[d] * width, width)
                bufs[s][j, :, pl.ds(start + i * width, width)] = tokens_buf[
                    j, :, pl.ds(source, width)
                ]
            put = pltpu.make_async_copy(bufs[s].at[j], outs[s].at[j], out_sem.at[s, j])
            put.start()
            puts.append(put)
    for put in puts:
        put.wait()


def sort_tokens(tokens, grads, place):
    tokens = pltpu.with_memory_space_constraint(tokens, pltpu.HBM)
    grads = pltpu.with_memory_space_constraint(grads, pltpu.HBM)
    rows, depth = tokens.shape
    heads = grads.shape[1]
    part = depth // SUB
    width = part // NZ
    sizes = [len(stage) * width + (heads if s == 0 else 0) for s, stage in enumerate(STAGES)]
    return pl.pallas_call(
        sort_kernel,
        in_specs=[pl.BlockSpec(memory_space=pltpu.SMEM), HBM, HBM],
        out_specs=(HBM,) * len(sizes),
        out_shape=tuple(pltpu.HBM((SUB, rows, n), tokens.dtype) for n in sizes),
        scratch_shapes=[
            pltpu.VMEM((SUB, rows, part), tokens.dtype),
            pltpu.VMEM((rows, heads), tokens.dtype),
            *[pltpu.VMEM((SUB, rows, n), tokens.dtype) for n in sizes],
            pltpu.SemaphoreType.DMA((SUB + 1,)),
            pltpu.SemaphoreType.DMA((len(sizes), SUB)),
        ],
        compiler_params=pltpu.CompilerParams(vmem_limit_bytes=24 << 20),
        cost_estimate=pl.CostEstimate(
            flops=0, bytes_accessed=4 * rows * (depth + heads), transcendentals=0
        ),
        name="sort_tokens",
    )(place, tokens, grads)


def grad_kernel(tokens_ref, grads_ref, out_ref):
    members, rows, width = tokens_ref.shape
    heads = grads_ref.shape[2]
    out_ref[0] = lax.dot_general(
        tokens_ref[...].reshape(members * rows, width),
        grads_ref[...].reshape(members * rows, heads),
        (((0,), (0,)), ((), ())),
        preferred_element_type=F32,
    )


def partial_grad(tokens, first, heads, width, own):
    members, rows, columns = tokens.shape
    skip = heads // width if own else 0
    count = columns // width - skip
    return pl.pallas_call(
        grad_kernel,
        grid=(count,),
        in_specs=[
            pl.BlockSpec((members, rows, width), lambda d: (0, 0, d + skip)),
            pl.BlockSpec((members, rows, heads), lambda d: (0, 0, 0)),
        ],
        out_specs=pl.BlockSpec((1, width, heads), lambda d: (d, 0, 0)),
        out_shape=jax.ShapeDtypeStruct((count, width, heads), F32),
        compiler_params=pltpu.CompilerParams(vmem_limit_bytes=16 << 20),
        cost_estimate=pl.CostEstimate(flops=0, bytes_accessed=0, transcendentals=0),
        name="partial_grad",
    )(tokens, first)


def project_kernel(sizes, first, last, place_ref, tokens_ref, grads_ref, *refs):
    n = len(sizes)
    weight_refs, refs = refs[:n], refs[n:]
    if not first:
        sum_ref, _, refs = refs[0], refs[1], refs[2:]
    sum_out, grad_out, token_buf, grad_buf, in_sem, out_sem = refs
    width = token_buf.shape[2] // NX
    rows = token_buf.shape[1]
    pieces = [(i, j) for i, size in enumerate(sizes) for j in range(size)]

    def columns(k, c):
        return pl.ds(pl.multiple_of(place_ref[k * NX + c] * width, width), width)

    def fetch(k, c):
        return pltpu.make_async_copy(
            tokens_ref.at[:, columns(k, c)],
            token_buf.at[k, :, pl.ds(c * width, width)],
            in_sem.at[k, c],
        )

    def put(k, c):
        return pltpu.make_async_copy(
            grad_buf.at[k, :, pl.ds(c * width, width)],
            grad_out.at[:, columns(k, c)],
            out_sem.at[k, c],
        )

    for k in range(len(pieces)):
        for c in range(NX):
            fetch(k, c).start()
    grads = grads_ref[...]
    total = None if first else sum_ref[...]
    for k, (i, j) in enumerate(pieces):
        weight = weight_refs[i][pl.ds(j * NX * width, NX * width), :]
        grad_buf[k] = lax.dot_general(
            grads, weight, (((1,), (1,)), ((), ())), preferred_element_type=F32
        ).astype(BF16)
        for c in range(NX):
            put(k, c).start()
        for c in range(NX):
            fetch(k, c).wait()
        term = jnp.dot(token_buf[k], weight, preferred_element_type=F32)
        total = term if total is None else total + term
    sum_out[...] = total.astype(sum_out.dtype)
    for k in range(len(pieces)):
        for c in range(NX):
            put(k, c).wait()


def project(tokens, grads, weights, place, state, last, span=1):
    rows, heads = grads.shape
    tokens = pltpu.with_memory_space_constraint(tokens, pltpu.HBM)
    width = tokens.shape[1] // (NY * NX * NZ)
    pair = NX * width
    sizes = tuple(w.shape[0] // pair for w in weights)
    count = sum(sizes)
    first = state is None
    whole = pl.BlockSpec(memory_space=pltpu.VMEM)
    n_in = 3 + len(weights)
    return pl.pallas_call(
        functools.partial(project_kernel, sizes, first, last),
        in_specs=[pl.BlockSpec(memory_space=pltpu.SMEM), HBM, whole]
        + [whole] * len(weights)
        + ([] if first else [whole, HBM]),
        out_specs=(whole, HBM),
        out_shape=(
            jax.ShapeDtypeStruct((rows, heads), BF16 if last else F32),
            pltpu.HBM(tokens.shape, BF16),
        ),
        scratch_shapes=[
            pltpu.VMEM((count, rows, pair), BF16),
            pltpu.VMEM((count, rows, pair), BF16),
            pltpu.SemaphoreType.DMA((count, NX)),
            pltpu.SemaphoreType.DMA((count, NX)),
        ],
        input_output_aliases={} if first else {n_in + 1: 1},
        compiler_params=pltpu.CompilerParams(vmem_limit_bytes=24 << 20),
        cost_estimate=pl.CostEstimate(
            flops=span * 4 * rows * heads * count * pair,
            bytes_accessed=count * pair * (rows * 4 + heads * 2),
            transcendentals=0,
        ),
        name="project",
    )(place, tokens, grads, *weights, *(() if first else state))


def outer_kernel(plan_ref, rank_ref, near_ref, far_ref, inner_ref, *refs):
    states, (new_ref, mom_ref) = refs[:-2], refs[-2:]
    groups, width = len(states), mom_ref.shape[1]
    rank = rank_ref[0]
    for b in range(groups):
        head = b ^ rank
        columns = pl.ds(pl.multiple_of(head * width, width), width)
        anchor, momentum = states[b][0], states[b][1]
        mean = (near_ref[:, columns] + far_ref[:, columns]) / groups
        pseudo = anchor - mean
        following = momentum_coef * momentum + pseudo
        outer = anchor - outer_rate * (pseudo + momentum_coef * following)
        synced = jnp.full(outer.shape, plan_ref[head], jnp.int32) > 0
        new_ref[:, columns] = jnp.where(synced, outer, inner_ref[:, columns]).astype(BF16)
        if b == 0:
            mom_ref[...] = jnp.where(synced, following, momentum)


def outer_step(plan, rank, near, far, inner, state):
    smem = pl.BlockSpec(memory_space=pltpu.SMEM)
    whole = pl.BlockSpec(memory_space=pltpu.VMEM)
    return pl.pallas_call(
        outer_kernel,
        in_specs=[smem, smem] + [whole] * (3 + len(state)),
        out_specs=(whole, whole),
        out_shape=(
            jax.ShapeDtypeStruct(inner.shape, BF16),
            jax.ShapeDtypeStruct(state[0].shape[1:], F32),
        ),
        name="outer_step",
    )(plan, rank, near, far, inner, *state)


def local(acts, out_grad, weights, anchor, momentum, plan):
    tokens, grads_out, local_weight = acts[0], out_grad[0], weights[0]
    rows, depth = tokens.shape
    heads = grads_out.shape[1]
    total_tokens = rows * NY * NX * NZ
    inner_rate = 1.0 / math.sqrt(total_tokens * depth)
    z = lax.axis_index("z")
    rank = lax.axis_index(REP)
    part = depth // SUB
    sub = ("y", "xl")

    width = part // NZ
    after = lambda x, *others: lax.optimization_barrier((x, *others))[0]

    width = part // NZ
    after = lambda x, *others: lax.optimization_barrier((x, *others))[0]

    pair = jnp.stack([local_weight, shift_x(local_weight)])
    block = jnp.stack([pair] + [shift_y(pair, dy) for dy in range(1, NY)])
    block = block.reshape(part, heads)

    place = jnp.stack([(z + d) % NZ for d in range(NZ)]).astype(jnp.int32)
    first, second = sort_tokens(tokens, grads_out, place)
    block, first = lax.optimization_barrier((block, first))
    first = lax.all_to_all(first, sub, 0, 0)

    y, x = lax.axis_index("y"), lax.axis_index("xl")

    def places(*shifts, rows=range(NY)):
        members = [(y - v) % NY * NX + (x ^ c) for v in rows for c in range(NX)]
        at = [member * NZ + (z + dz) % NZ for dz in shifts for member in members]
        return jnp.stack(at).astype(jnp.int32)

    carries = [project(tokens, grads_out, [block], places(0), None, False)]
    ring = [(block, block)]

    def ring_step(k, span, *earlier):
        right, left = ring[-1]
        if earlier:
            right, left = after(right, *earlier), after(left, *earlier)
        ring.append((shift_z(right, 1), shift_z(left, -1)))
        carries.append(
            project(tokens, grads_out, list(ring[-1]), places(-k, k), carries[-1], False, span)
        )

    ring_step(1, 5)
    ring_step(2, 1)

    first, _ = lax.optimization_barrier((first, carries[1][0]))
    second = lax.all_to_all(after(second, first), sub, 0, 0)
    state = after(jnp.stack([anchor, momentum]), first)
    first, ring[2] = lax.optimization_barrier((first, ring[2]))
    terms = {}
    for s, stage in enumerate(STAGES):
        if s == 1:
            second = after(second, carries[2][0])
        sums = partial_grad((first, second)[s], first, heads, width, s == 0)
        terms.update({d: sums[i] for i, d in enumerate(stage)})

    half = width // 2
    right = shift_z(terms[4][:half], 1)
    left = shift_z(terms[4][half:], -1)
    right = jnp.concatenate([terms[3][:half] + right, terms[3][half:]])
    left = jnp.concatenate([terms[5][:half], terms[5][half:] + left])
    right, left = shift_z(right, 1), shift_z(left, -1)
    ring_step(3, 1, right, left)
    states = [state, shift_core(state)]
    right, left = terms[2] + right, terms[6] + left
    right, left, states = lax.optimization_barrier((right, left, states))
    right, left = shift_z(right, 1), shift_z(left, -1)
    states += [shift_far(x) for x in states]
    right, left = terms[1] + right, terms[7] + left
    right, left, states, ring[3] = lax.optimization_barrier((right, left, states, ring[3]))
    right, left = shift_z(right, 1), shift_z(left, -1)
    right = after(right, carries[3][0])
    inner = local_weight.astype(F32) - inner_rate * (terms[0] + right + left)

    near = inner + shift_core(inner)
    half = part // 2
    right, left = shift_z(ring[3][0][:half], 1), shift_z(ring[3][1][half:], -1)
    near, right, left = lax.optimization_barrier((near, right, left))
    far = shift_far(near)
    values, act_grad = project(tokens, grads_out, [right, left], places(4), carries[3], True)
    new_weight, new_momentum = outer_step(
        plan, jnp.reshape(rank, (1,)).astype(jnp.int32), near, far, inner, states
    )
    return values[None], act_grad[None], new_weight[None], new_momentum


def solution(mesh):
    fine = Mesh(mesh.devices.reshape(2, 2, NY, NX, NZ), ("xh", "core", "y", "xl", "z"))
    placed = (
        P(REP, FSDP, None),
        P(REP, FSDP, None),
        P(REP, FSDP, None),
        P(FSDP, REP),
        P(FSDP, REP),
        P(),
    )
    return jax.shard_map(
        local,
        mesh=fine,
        in_specs=placed,
        out_specs=(
            P(REP, FSDP, None),
            P(REP, FSDP, None),
            P(REP, FSDP, None),
            P(FSDP, REP),
        ),
        check_vma=False,
    )
```

time: 283 us -> 173 us (0.61)
  waiting for transfers between devices: 144 us -> 64.5 us
  local copies, waits for them, and re-layouts: 29.7 us -> 6.05 us
  between operations: 14.4 us -> 1.04 us
  starting transfers between devices: 47.4 us -> 57.5 us
  blocking collectives: 9.81 us -> 0 us
  Pallas kernels: 30.6 us -> 40.2 us
  other arithmetic: 5.36 us -> 2.49 us
    all_gather x2 -> x0, waiting for transfers between devices: 59.5 us -> none  [the longest x1 40.2 us: local(): grads = lax.all_gather(grads_out, ('y', 'xl'), axis=0, tiled=False)]
    unnamed x56 -> x34, local copies, waits for them, and re-layouts: 23 us -> 3.33 us
    ppermute x16, waiting for transfers between devices: 60.3 us -> 41.2 us  [shift_z(): return lax.ppermute(x, 'z', [(i, (i + dz) % NZ) for i in range(NZ)])]
    all_gather x1 -> x0, blocking collectives: 9.81 us -> none  [local(): lax.all_gather(jnp.stack([anchor, momentum]), REP, axis=0, tiled=False)]
    all_to_all x0 -> x2, starting transfers between devices: none -> 8.26 us  [the longest x1 4.63 us: local(): first = lax.all_to_all(first, sub, 0, 0)]
    pallas_call x2 -> x4, Pallas kernels: 8.09 us -> 14.9 us  [the longest x2 8.15 us: partial_grad(): pl.pallas_call(grad_kernel, grid=(count,), in_specs=[pl.BlockSpec((member...]
    all_to_all x0 -> x2, waiting for transfers between devices: none -> 5.26 us  [the longest x1 5.25 us: local(): first = lax.all_to_all(first, sub, 0, 0)]
    ppermute x9, waiting for transfers between devices: 23.2 us -> 18 us  [the longest x3 9.58 us: shift_y(): return lax.ppermute(x, 'y', [(i, (i + dy) % NY) for i in range(NY)])]
  transfers between devices with their start and end apart: 27 -> 27, of which waited for: 12 -> 14; matrix products, arithmetic and copies ran while one was open for 4% -> 2% of each run, Pallas kernels for 10% -> 22%
where the time goes in v2:
time: 173 us; the launch traced here: 172 us
  waiting for transfers between devices  64.5 us (37%)
  starting transfers between devices  57.5 us (33%)
  Pallas kernels  40.2 us (23%)
  local copies, waits for them, and re-layouts  6.05 us (3%)
  other arithmetic  2.49 us (1%)
    ppermute x16, waiting for transfers between devices, shift_z(): return lax.ppermute(x, 'z', [(i, (i + dz) % NZ) for i in range(NZ)])  41.2 us
    pallas_call x5, Pallas kernels, project(): pl.pallas_call(functools.partial(project_kernel, sizes, first, last), in_...  25.3 us
    ppermute x16, starting transfers between devices, shift_z(): return lax.ppermute(x, 'z', [(i, (i + dz) % NZ) for i in range(NZ)])  21.9 us
    ppermute x2, starting transfers between devices, shift_core(): return lax.ppermute(x, 'core', [(0, 1), (1, 0)])  12.2 us
    ppermute x3, waiting for transfers between devices, shift_y(): return lax.ppermute(x, 'y', [(i, (i + dy) % NY) for i in range(NY)])  9.58 us
    ppermute x3, starting transfers between devices, shift_far(): return lax.ppermute(x, 'xh', [(0, 1), (1, 0)])  8.31 us
    pallas_call x2, Pallas kernels, partial_grad(): pl.pallas_call(grad_kernel, grid=(count,), in_specs=[pl.BlockSpec((member...  8.15 us
    all_to_all x1, waiting for transfers between devices, local(): first = lax.all_to_all(first, sub, 0, 0)  5.25 us
  transfers between devices with their start and end apart: 27, of which 14 were waited for; matrix products, arithmetic and copies ran while one was open for 2% of the time, Pallas kernels for 22%

profile of v2, /device:TPU:1, one launch (start us, length us, event | category | flops | bytes accessed | tf_op | source)
XLA Modules:
  0.0 171.8 jit_solution(17157716563253263177)
XLA Ops:
  6.3 3.6 %collective-permute-start.3 = (bf16[2,128,512]{2,1,0:T(8,128)(2,1)S(1)}, bf16[2,128,512]{2,1,0:T(8,128)(2,1)S(1)}, u32[]{:S(2)}, u32[]{:S(2)}) collective-permute-start(bf16[2,128,512]{2,1,0:T(8,128)(2,1)S(1)} %get-tuple-element.97), channel_id=1, source_target_pairs={{0,48},{16,0},{32,16},{48,32},{1,49},{17,1},{33,17},{49,33},{2,50}... | collective-permute-start | bytes 786440 | tf_op jit(solution)/shard_map/ppermute | solution.py:28
  11.0 4.6 %sort_tokens.1 = (bf16[8,256,896]{2,1,0:T(8,128)(2,1)}, bf16[8,256,640]{2,1,0:T(8,128)(2,1)}) custom-call(s32[8]{0:T(128)S(1)} %stack.281.place_ref, bf16[256,8192]{1,0:T(8,128)(2,1)} %bitcast.140, bf16[256,512]{1,0:T(8,128)(2,1)} %bitcast.131), custom_call_target="tpu_custom_call" | custom-call | bytes 8912896 | tf_op jit(solution)/shard_map/sort_tokens/pallas_call | solution.py:87
  15.6 4.6 %collective-permute-done.3 = bf16[2,128,512]{2,1,0:T(8,128)(2,1)S(1)} collective-permute-done((bf16[2,128,512]{2,1,0:T(8,128)(2,1)S(1)}, bf16[2,128,512]{2,1,0:T(8,128)(2,1)S(1)}, u32[]{:S(2)}, u32[]{:S(2)}) %collective-permute-start.3) | collective-permute-done | bytes 262176 | tf_op jit(solution)/shard_map/ppermute | solution.py:28
  20.2 5.0 %collective-permute-done.1 = bf16[2,128,512]{2,1,0:T(8,128)(2,1)S(1)} collective-permute-done((bf16[2,128,512]{2,1,0:T(8,128)(2,1)S(1)}, bf16[2,128,512]{2,1,0:T(8,128)(2,1)S(1)}, u32[]{:S(2)}, u32[]{:S(2)}) %collective-permute-start.1) | collective-permute-done | bytes 262176 | tf_op jit(solution)/shard_map/ppermute | solution.py:28
  25.4 4.6 %all-to-all-start = ((bf16[8,256,896]{2,1,0:T(8,128)(2,1)}), bf16[8,256,896]{2,1,0:T(8,128)(2,1)}, u32[]{:S(2)}, u32[]{:S(2)}) async-start(bf16[8,256,896]{2,1,0:T(8,128)(2,1)} %get-tuple-element.47), calls=%async_computation | async-start | bytes 7340032 | tf_op jit(solution)/shard_map/all_to_all | solution.py:280
  31.7 4.0 %collective-permute-start.5 = (bf16[1024,512]{1,0:T(8,128)(2,1)S(1)}, bf16[1024,512]{1,0:T(8,128)(2,1)}, u32[]{:S(2)}, u32[]{:S(2)}) collective-permute-start(bf16[1024,512]{1,0:T(8,128)(2,1)S(1)} %bitcast.138), channel_id=1, source_target_pairs={{0,7},{1,0},{2,1},{3,2},{4,3},{5,4},{6,5},{7,6},{8,15},{9,8},{10,9... | collective-permute-start | bytes 3145736 | tf_op jit(solution)/shard_map/ppermute | solution.py:24
  36.0 3.5 %project.5 = (f32[256,512]{1,0:T(8,128)S(1)}, bf16[256,8192]{1,0:T(8,128)(2,1)}) custom-call(s32[8]{0:T(128)S(1)} %stack.314.place_ref, bf16[256,8192]{1,0:T(8,128)(2,1)} %bitcast.141, bf16[256,512]{1,0:T(8,128)(2,1)S(1)} %bitcast.132, bf16[1024,512]{1,0:T(8,128)(2,1)S(1)} %bitcast.139), custom_call_target="tpu_custom_call" | custom-call | flops 536870912 | bytes 2097152 | tf_op jit(solution)/shard_map/project/pallas_call | solution.py:196
  39.4 19.4 %collective-permute-done.4.refs_0_ = bf16[1024,512]{1,0:T(8,128)(2,1)} collective-permute-done((bf16[1024,512]{1,0:T(8,128)(2,1)S(1)}, bf16[1024,512]{1,0:T(8,128)(2,1)}, u32[]{:S(2)}, u32[]{:S(2)}) %collective-permute-start.4) | collective-permute-done | bytes 1048608 | tf_op jit(solution)/shard_map/ppermute | solution.py:24
  61.5 5.9 %project.6 = (f32[256,512]{1,0:T(8,128)S(1)}, bf16[256,8192]{1,0:T(8,128)(2,1)}) custom-call(s32[16]{0:T(128)S(1)} %stack.305.place_ref, bf16[256,8192]{1,0:T(8,128)(2,1)} %bitcast.142, bf16[256,512]{1,0:T(8,128)(2,1)S(1)} %bitcast.133, bf16[1024,512]{1,0:T(8,128)(2,1)} %collective-permute-done.4.refs_0_, ...), custom_call_target="tpu_custom_call", output_to_operand_aliasing={{1}: (6, {})} | custom-call | flops 5368709120 | bytes 4194304 | tf_op jit(solution)/shard_map/project/pallas_call | solution.py:196
  68.2 5.3 %all-to-all-done.grads_ref.tokens_ref = bf16[8,256,896]{2,1,0:T(8,128)(2,1)} async-done(((bf16[8,256,896]{2,1,0:T(8,128)(2,1)}), bf16[8,256,896]{2,1,0:T(8,128)(2,1)}, u32[]{:S(2)}, u32[]{:S(2)}) %all-to-all-start) | async-done | bytes 3670048 | tf_op jit(solution)/shard_map/all_to_all | solution.py:280
  73.5 3.6 %all-to-all-start.1 = ((bf16[8,256,640]{2,1,0:T(8,128)(2,1)}), bf16[8,256,640]{2,1,0:T(8,128)(2,1)S(1)}, u32[]{:S(2)}, u32[]{:S(2)}) async-start(bf16[8,256,640]{2,1,0:T(8,128)(2,1)} %get-tuple-element.53), calls=%async_computation.1 | async-start | bytes 5242880 | tf_op jit(solution)/shard_map/all_to_all | solution.py:305
  77.1 6.9 %collective-permute-done.6.refs_0_ = bf16[1024,512]{1,0:T(8,128)(2,1)} collective-permute-done((bf16[1024,512]{1,0:T(8,128)(2,1)}, bf16[1024,512]{1,0:T(8,128)(2,1)}, u32[]{:S(2)}, u32[]{:S(2)}) %collective-permute-start.6) | collective-permute-done | bytes 1048608 | tf_op jit(solution)/shard_map/ppermute | solution.py:24
  84.0 3.8 %partial_grad.3 = f32[3,128,512]{2,1,0:T(8,128)S(1)} custom-call(bf16[8,256,896]{2,1,0:T(8,128)(2,1)} %all-to-all-done.grads_ref.tokens_ref, bf16[8,256,896]{2,1,0:T(8,128)(2,1)} %all-to-all-done.grads_ref.tokens_ref), custom_call_target="tpu_custom_call" | custom-call | tf_op jit(solution)/shard_map/partial_grad/pallas_call | solution.py:122
  92.3 3.4 %collective-permute-done.8 = f32[64,512]{1,0:T(8,128)S(1)} collective-permute-done((f32[64,512]{1,0:T(8,128)S(1)}, f32[64,512]{1,0:T(8,128)S(1)}, u32[]{:S(2)}, u32[]{:S(2)}) %collective-permute-start.8) | collective-permute-done | bytes 131104 | tf_op jit(solution)/shard_map/ppermute | solution.py:24
  97.4 4.0 %collective-permute-done.11 = f32[128,512]{1,0:T(8,128)S(1)} collective-permute-done((f32[128,512]{1,0:T(8,128)S(1)}, f32[128,512]{1,0:T(8,128)S(1)}, u32[]{:S(2)}, u32[]{:S(2)}) %collective-permute-start.11) | collective-permute-done | bytes 262176 | tf_op jit(solution)/shard_map/ppermute | solution.py:24
  106.6 5.9 %project.7 = (f32[256,512]{1,0:T(8,128)S(1)}, bf16[256,8192]{1,0:T(8,128)(2,1)}) custom-call(s32[16]{0:T(128)S(1)} %stack.331.place_ref, bf16[256,8192]{1,0:T(8,128)(2,1)} %bitcast.143, bf16[256,512]{1,0:T(8,128)(2,1)S(1)} %bitcast.134, bf16[1024,512]{1,0:T(8,128)(2,1)} %collective-permute-done.6.refs_0_, ...), custom_call_target="tpu_custom_call", output_to_operand_aliasing={{1}: (6, {})} | custom-call | flops 1073741824 | bytes 4194304 | tf_op jit(solution)/shard_map/project/pallas_call | solution.py:196
  112.5 4.9 %collective-permute-start.12 = (f32[2,128,128]{2,1,0:T(8,128)S(1)}, f32[2,128,128]{2,1,0:T(8,128)}, u32[]{:S(2)}, u32[]{:S(2)}) collective-permute-start(f32[2,128,128]{2,1,0:T(8,128)S(1)} %pad_maximum_fusion.4.refs_0_), channel_id=1, source_target_pairs={{0,64},{64,0},{1,65},{65,1},{2,66},{66,2},{3,67},{67,3},{4,68},{68... | collective-permute-start | bytes 393224 | tf_op jit(solution)/shard_map/ppermute | solution.py:36
  117.3 4.4 %partial_grad.2 = f32[5,128,512]{2,1,0:T(8,128)S(1)} custom-call(bf16[8,256,640]{2,1,0:T(8,128)(2,1)S(1)} %all-to-all-done.1.tokens_ref, bf16[8,256,896]{2,1,0:T(8,128)(2,1)} %all-to-all-done.grads_ref.tokens_ref), custom_call_target="tpu_custom_call" | custom-call | tf_op jit(solution)/shard_map/partial_grad/pallas_call | solution.py:122
  126.1 4.3 %collective-permute-done.14 = f32[128,512]{1,0:T(8,128)S(1)} collective-permute-done((f32[128,512]{1,0:T(8,128)S(1)}, f32[128,512]{1,0:T(8,128)S(1)}, u32[]{:S(2)}, u32[]{:S(2)}) %collective-permute-start.14) | collective-permute-done | bytes 262176 | tf_op jit(solution)/shard_map/ppermute | solution.py:24
  141.2 3.0 %collective-permute-start.23 = (bf16[512,512]{1,0:T(8,128)(2,1)S(1)}, bf16[512,512]{1,0:T(8,128)(2,1)S(1)}, u32[]{:S(2)}, u32[]{:S(2)}) collective-permute-start(bf16[512,512]{1,0:T(8,128)(2,1)S(1)} %slice.84), channel_id=1, source_target_pairs={{0,7},{1,0},{2,1},{3,2},{4,3},{5,4},{6,5},{7,6},{8,15},{9,8},{10,9... | collective-permute-start | bytes 1572872 | tf_op jit(solution)/shard_map/ppermute | solution.py:24
  144.1 5.9 %project.8 = (f32[256,512]{1,0:T(8,128)S(1)}, bf16[256,8192]{1,0:T(8,128)(2,1)}) custom-call(s32[16]{0:T(128)S(1)} %stack.351.place_ref, bf16[256,8192]{1,0:T(8,128)(2,1)} %bitcast.144, bf16[256,512]{1,0:T(8,128)(2,1)S(1)} %bitcast.135, bf16[1024,512]{1,0:T(8,128)(2,1)} %collective-permute-done.17.refs_0_, ...), custom_call_target="tpu_custom_call", output_to_operand_aliasing={{1}: (6, {})} | custom-call | flops 1073741824 | bytes 4194304 | tf_op jit(solution)/shard_map/project/pallas_call | solution.py:196
  151.2 7.4 %collective-permute-start.21 = (f32[128,512]{1,0:T(8,128)S(1)}, f32[128,512]{1,0:T(8,128)S(1)}, u32[]{:S(2)}, u32[]{:S(2)}) collective-permute-start(f32[128,512]{1,0:T(8,128)S(1)} %fusion.7.inner_ref), channel_id=1, source_target_pairs={{0,64},{64,0},{1,65},{65,1},{2,66},{66,2},{3,67},{67,3},{4,68},{68... | collective-permute-start | bytes 786440 | tf_op jit(solution)/shard_map/ppermute | solution.py:36
  159.8 2.8 %collective-permute-start.24 = (f32[128,512]{1,0:T(8,128)S(1)}, f32[128,512]{1,0:T(8,128)S(1)}, u32[]{:S(2)}, u32[]{:S(2)}) collective-permute-start(f32[128,512]{1,0:T(8,128)S(1)} %add.612.near_ref), channel_id=1, source_target_pairs={{0,128},{128,0},{1,129},{129,1},{2,130},{130,2},{3,131},{131,3},{4... | collective-permute-start | bytes 786440 | tf_op jit(solution)/shard_map/ppermute | solution.py:40
  162.8 4.2 %project.9 = (bf16[256,512]{1,0:T(8,128)(2,1)}, bf16[256,8192]{1,0:T(8,128)(2,1)}) custom-call(s32[8]{0:T(128)S(1)} %stack.272.place_ref, bf16[256,8192]{1,0:T(8,128)(2,1)} %bitcast.145, bf16[256,512]{1,0:T(8,128)(2,1)S(1)} %bitcast.136, bf16[512,512]{1,0:T(8,128)(2,1)S(1)} %collective-permute-done.22.refs_0_, ...), custom_call_target="tpu_custom_call", output_to_operand_aliasing={{1}: (6, {})} | custom-call | flops 536870912 | bytes 2097152 | tf_op jit(solution)/shard_map/project/pallas_call | solution.py:196
  (92 shorter events, 46.0 us)
Async XLA Ops:
  6.3 13.9 %collective-permute-start.3 = (bf16[2,128,512]{2,1,0:T(8,128)(2,1)S(1)}, bf16[2,128,512]{2,1,0:T(8,128)(2,1)S(1)}, u32[]{:S(2)}, u32[]{:S(2)}) collective-permute-start(bf16[2,128,512]{2,1,0:T(8,128)(2,1)S(1)} %get-tuple-element.97), channel_id=1, source_target_pairs={{0,48},{16,0},{32,16},{48,32},{1,49},{17,1},{33,17},{49,33},{2,50}... | collective-permute-start | bytes 786440 | tf_op jit(solution)/shard_map/ppermute | solution.py:28
  9.9 10.3 %collective-permute-start.2 = (bf16[2,128,512]{2,1,0:T(8,128)(2,1)S(1)}, bf16[2,128,512]{2,1,0:T(8,128)(2,1)S(1)}, u32[]{:S(2)}, u32[]{:S(2)}) collective-permute-start(bf16[2,128,512]{2,1,0:T(8,128)(2,1)S(1)} %get-tuple-element.97), channel_id=1, source_target_pairs={{0,32},{16,48},{32,0},{48,16},{1,33},{17,49},{33,1},{49,17},{2,34}... | collective-permute-start | bytes 786440 | tf_op jit(solution)/shard_map/ppermute | solution.py:28
  10.2 15.0 %collective-permute-start.1 = (bf16[2,128,512]{2,1,0:T(8,128)(2,1)S(1)}, bf16[2,128,512]{2,1,0:T(8,128)(2,1)S(1)}, u32[]{:S(2)}, u32[]{:S(2)}) collective-permute-start(bf16[2,128,512]{2,1,0:T(8,128)(2,1)S(1)} %get-tuple-element.97), channel_id=1, source_target_pairs={{0,16},{16,32},{32,48},{48,0},{1,17},{17,33},{33,49},{49,1},{2,18}... | collective-permute-start | bytes 786440 | tf_op jit(solution)/shard_map/ppermute | solution.py:28
  25.4 48.1 %all-to-all-start = ((bf16[8,256,896]{2,1,0:T(8,128)(2,1)}), bf16[8,256,896]{2,1,0:T(8,128)(2,1)}, u32[]{:S(2)}, u32[]{:S(2)}) async-start(bf16[8,256,896]{2,1,0:T(8,128)(2,1)} %get-tuple-element.47), calls=%async_computation | async-start | bytes 7340032 | tf_op jit(solution)/shard_map/all_to_all | solution.py:280
  30.0 28.9 %collective-permute-start.4 = (bf16[1024,512]{1,0:T(8,128)(2,1)S(1)}, bf16[1024,512]{1,0:T(8,128)(2,1)}, u32[]{:S(2)}, u32[]{:S(2)}) collective-permute-start(bf16[1024,512]{1,0:T(8,128)(2,1)S(1)} %bitcast.137), channel_id=1, source_target_pairs={{0,1},{1,2},{2,3},{3,4},{4,5},{5,6},{6,7},{7,0},{8,9},{9,10},{10,1... | collective-permute-start | bytes 3145736 | tf_op jit(solution)/shard_map/ppermute | solution.py:24
  31.7 27.1 %collective-permute-start.5 = (bf16[1024,512]{1,0:T(8,128)(2,1)S(1)}, bf16[1024,512]{1,0:T(8,128)(2,1)}, u32[]{:S(2)}, u32[]{:S(2)}) collective-permute-start(bf16[1024,512]{1,0:T(8,128)(2,1)S(1)} %bitcast.138), channel_id=1, source_target_pairs={{0,7},{1,0},{2,1},{3,2},{4,3},{5,4},{6,5},{7,6},{8,15},{9,8},{10,9... | collective-permute-start | bytes 3145736 | tf_op jit(solution)/shard_map/ppermute | solution.py:24
  58.9 25.2 %collective-permute-start.6 = (bf16[1024,512]{1,0:T(8,128)(2,1)}, bf16[1024,512]{1,0:T(8,128)(2,1)}, u32[]{:S(2)}, u32[]{:S(2)}) collective-permute-start(bf16[1024,512]{1,0:T(8,128)(2,1)} %collective-permute-done.4.refs_0_), channel_id=1, source_target_pairs={{0,1},{1,2},{2,3},{3,4},{4,5},{5,6},{6,7},{7,0},{8,9},{9,10},{10,1... | collective-permute-start | bytes 3145736 | tf_op jit(solution)/shard_map/ppermute | solution.py:24
  58.9 25.2 %collective-permute-start.7 = (bf16[1024,512]{1,0:T(8,128)(2,1)}, bf16[1024,512]{1,0:T(8,128)(2,1)}, u32[]{:S(2)}, u32[]{:S(2)}) collective-permute-start(bf16[1024,512]{1,0:T(8,128)(2,1)} %collective-permute-done.5.refs_1_), channel_id=1, source_target_pairs={{0,7},{1,0},{2,1},{3,2},{4,3},{5,4},{6,5},{7,6},{8,15},{9,8},{10,9... | collective-permute-start | bytes 3145736 | tf_op jit(solution)/shard_map/ppermute | solution.py:24
  73.5 43.8 %all-to-all-start.1 = ((bf16[8,256,640]{2,1,0:T(8,128)(2,1)}), bf16[8,256,640]{2,1,0:T(8,128)(2,1)S(1)}, u32[]{:S(2)}, u32[]{:S(2)}) async-start(bf16[8,256,640]{2,1,0:T(8,128)(2,1)} %get-tuple-element.53), calls=%async_computation.1 | async-start | bytes 5242880 | tf_op jit(solution)/shard_map/all_to_all | solution.py:305
  95.7 5.6 %collective-permute-start.11 = (f32[128,512]{1,0:T(8,128)S(1)}, f32[128,512]{1,0:T(8,128)S(1)}, u32[]{:S(2)}, u32[]{:S(2)}) collective-permute-start(f32[128,512]{1,0:T(8,128)S(1)} %pad_maximum_fusion.3), channel_id=1, source_target_pairs={{0,7},{1,0},{2,1},{3,2},{4,3},{5,4},{6,5},{7,6},{8,15},{9,8},{10,9... | collective-permute-start | bytes 786440 | tf_op jit(solution)/shard_map/ppermute | solution.py:24
  95.8 6.8 %collective-permute-start.9 = (f32[128,512]{1,0:T(8,128)S(1)}, f32[128,512]{1,0:T(8,128)S(1)}, u32[]{:S(2)}, u32[]{:S(2)}) collective-permute-start(f32[128,512]{1,0:T(8,128)S(1)} %pad_maximum_fusion.2), channel_id=1, source_target_pairs={{0,1},{1,2},{2,3},{3,4},{4,5},{5,6},{6,7},{7,0},{8,9},{9,10},{10,1... | collective-permute-start | bytes 786440 | tf_op jit(solution)/shard_map/ppermute | solution.py:24
  102.7 30.6 %collective-permute-start.17 = (bf16[1024,512]{1,0:T(8,128)(2,1)}, bf16[1024,512]{1,0:T(8,128)(2,1)}, u32[]{:S(2)}, u32[]{:S(2)}) collective-permute-start(bf16[1024,512]{1,0:T(8,128)(2,1)} %collective-permute-done.6.refs_0_), channel_id=1, source_target_pairs={{0,1},{1,2},{2,3},{3,4},{4,5},{5,6},{6,7},{7,0},{8,9},{9,10},{10,1... | collective-permute-start | bytes 3145736 | tf_op jit(solution)/shard_map/ppermute | solution.py:24
  103.4 29.9 %collective-permute-start.18 = (bf16[1024,512]{1,0:T(8,128)(2,1)}, bf16[1024,512]{1,0:T(8,128)(2,1)}, u32[]{:S(2)}, u32[]{:S(2)}) collective-permute-start(bf16[1024,512]{1,0:T(8,128)(2,1)} %collective-permute-done.7.refs_1_), channel_id=1, source_target_pairs={{0,7},{1,0},{2,1},{3,2},{4,3},{5,4},{6,5},{7,6},{8,15},{9,8},{10,9... | collective-permute-start | bytes 3145736 | tf_op jit(solution)/shard_map/ppermute | solution.py:24
  112.5 9.4 %collective-permute-start.12 = (f32[2,128,128]{2,1,0:T(8,128)S(1)}, f32[2,128,128]{2,1,0:T(8,128)}, u32[]{:S(2)}, u32[]{:S(2)}) collective-permute-start(f32[2,128,128]{2,1,0:T(8,128)S(1)} %pad_maximum_fusion.4.refs_0_), channel_id=1, source_target_pairs={{0,64},{64,0},{1,65},{65,1},{2,66},{66,2},{3,67},{67,3},{4,68},{68... | collective-permute-start | bytes 393224 | tf_op jit(solution)/shard_map/ppermute | solution.py:36
  121.8 8.6 %collective-permute-start.14 = (f32[128,512]{1,0:T(8,128)S(1)}, f32[128,512]{1,0:T(8,128)S(1)}, u32[]{:S(2)}, u32[]{:S(2)}) collective-permute-start(f32[128,512]{1,0:T(8,128)S(1)} %get-tuple-element.60), channel_id=1, source_target_pairs={{0,7},{1,0},{2,1},{3,2},{4,3},{5,4},{6,5},{7,6},{8,15},{9,8},{10,9... | collective-permute-start | bytes 786440 | tf_op jit(solution)/shard_map/ppermute | solution.py:24
  122.7 10.5 %collective-permute-start.13 = (f32[128,512]{1,0:T(8,128)S(1)}, f32[128,512]{1,0:T(8,128)S(1)}, u32[]{:S(2)}, u32[]{:S(2)}) collective-permute-start(f32[128,512]{1,0:T(8,128)S(1)} %get-tuple-element.59), channel_id=1, source_target_pairs={{0,1},{1,2},{2,3},{3,4},{4,5},{5,6},{6,7},{7,0},{8,9},{9,10},{10,1... | collective-permute-start | bytes 786440 | tf_op jit(solution)/shard_map/ppermute | solution.py:24
  123.4 9.9 %collective-permute-start.15 = (f32[2,128,128]{2,1,0:T(8,128)S(1)}, f32[2,128,128]{2,1,0:T(8,128)S(1)}, u32[]{:S(2)}, u32[]{:S(2)}) collective-permute-start(f32[2,128,128]{2,1,0:T(8,128)S(1)} %pad_maximum_fusion.4.refs_0_), channel_id=1, source_target_pairs={{0,128},{128,0},{1,129},{129,1},{2,130},{130,2},{3,131},{131,3},{4... | collective-permute-start | bytes 393224 | tf_op jit(solution)/shard_map/ppermute | solution.py:40
  130.4 5.5 %collective-permute-start.16 = (f32[2,128,128]{2,1,0:T(8,128)}, f32[2,128,128]{2,1,0:T(8,128)S(1)}, u32[]{:S(2)}, u32[]{:S(2)}) collective-permute-start(f32[2,128,128]{2,1,0:T(8,128)} %collective-permute-done.12.refs_1_), channel_id=1, source_target_pairs={{0,128},{128,0},{1,129},{129,1},{2,130},{130,2},{3,131},{131,3},{4... | collective-permute-start | bytes 393224 | tf_op jit(solution)/shard_map/ppermute | solution.py:40
  136.0 14.1 %collective-permute-start.19 = (f32[128,512]{1,0:T(8,128)S(1)}, f32[128,512]{1,0:T(8,128)S(1)}, u32[]{:S(2)}, u32[]{:S(2)}) collective-permute-start(f32[128,512]{1,0:T(8,128)S(1)} %get-tuple-element.67), channel_id=1, source_target_pairs={{0,1},{1,2},{2,3},{3,4},{4,5},{5,6},{6,7},{7,0},{8,9},{9,10},{10,1... | collective-permute-start | bytes 786440 | tf_op jit(solution)/shard_map/ppermute | solution.py:24
  136.6 13.5 %collective-permute-start.20 = (f32[128,512]{1,0:T(8,128)S(1)}, f32[128,512]{1,0:T(8,128)}, u32[]{:S(2)}, u32[]{:S(2)}) collective-permute-start(f32[128,512]{1,0:T(8,128)S(1)} %get-tuple-element.71), channel_id=1, source_target_pairs={{0,7},{1,0},{2,1},{3,2},{4,3},{5,4},{6,5},{7,6},{8,15},{9,8},{10,9... | collective-permute-start | bytes 786440 | tf_op jit(solution)/shard_map/ppermute | solution.py:24
  140.0 19.8 %collective-permute-start.22 = (bf16[512,512]{1,0:T(8,128)(2,1)S(1)}, bf16[512,512]{1,0:T(8,128)(2,1)S(1)}, u32[]{:S(2)}, u32[]{:S(2)}) collective-permute-start(bf16[512,512]{1,0:T(8,128)(2,1)S(1)} %slice.83), channel_id=1, source_target_pairs={{0,1},{1,2},{2,3},{3,4},{4,5},{5,6},{6,7},{7,0},{8,9},{9,10},{10,1... | collective-permute-start | bytes 1572872 | tf_op jit(solution)/shard_map/ppermute | solution.py:24
  141.2 18.7 %collective-permute-start.23 = (bf16[512,512]{1,0:T(8,128)(2,1)S(1)}, bf16[512,512]{1,0:T(8,128)(2,1)S(1)}, u32[]{:S(2)}, u32[]{:S(2)}) collective-permute-start(bf16[512,512]{1,0:T(8,128)(2,1)S(1)} %slice.84), channel_id=1, source_target_pairs={{0,7},{1,0},{2,1},{3,2},{4,3},{5,4},{6,5},{7,6},{8,15},{9,8},{10,9... | collective-permute-start | bytes 1572872 | tf_op jit(solution)/shard_map/ppermute | solution.py:24
  151.2 8.5 %collective-permute-start.21 = (f32[128,512]{1,0:T(8,128)S(1)}, f32[128,512]{1,0:T(8,128)S(1)}, u32[]{:S(2)}, u32[]{:S(2)}) collective-permute-start(f32[128,512]{1,0:T(8,128)S(1)} %fusion.7.inner_ref), channel_id=1, source_target_pairs={{0,64},{64,0},{1,65},{65,1},{2,66},{66,2},{3,67},{67,3},{4,68},{68... | collective-permute-start | bytes 786440 | tf_op jit(solution)/shard_map/ppermute | solution.py:36
  159.8 9.1 %collective-permute-start.24 = (f32[128,512]{1,0:T(8,128)S(1)}, f32[128,512]{1,0:T(8,128)S(1)}, u32[]{:S(2)}, u32[]{:S(2)}) collective-permute-start(f32[128,512]{1,0:T(8,128)S(1)} %add.612.near_ref), channel_id=1, source_target_pairs={{0,128},{128,0},{1,129},{129,1},{2,130},{130,2},{3,131},{131,3},{4... | collective-permute-start | bytes 786440 | tf_op jit(solution)/shard_map/ppermute | solution.py:40
  (20 other events, 164.7 us)

commit v3 on v2

--- a/solution.py
+++ b/solution.py
@@ -96,7 +96,7 @@
             pltpu.SemaphoreType.DMA((SUB + 1,)),
             pltpu.SemaphoreType.DMA((len(sizes), SUB)),
         ],
-        compiler_params=pltpu.CompilerParams(vmem_limit_bytes=24 << 20),
+        compiler_params=pltpu.CompilerParams(vmem_limit_bytes=14 << 20),
         cost_estimate=pl.CostEstimate(
             flops=0, bytes_accessed=4 * rows * (depth + heads), transcendentals=0
         ),
@@ -115,86 +115,91 @@
     )
 
 
-def partial_grad(tokens, first, heads, width, own):
-    members, rows, columns = tokens.shape
-    skip = heads // width if own else 0
-    count = columns // width - skip
+def partial_grad(tokens, first, heads, width, at, count, span):
+    members, rows, _ = tokens.shape
     return pl.pallas_call(
         grad_kernel,
         grid=(count,),
         in_specs=[
-            pl.BlockSpec((members, rows, width), lambda d: (0, 0, d + skip)),
+            pl.BlockSpec((members, rows, width), lambda d: (0, 0, d + at)),
             pl.BlockSpec((members, rows, heads), lambda d: (0, 0, 0)),
         ],
         out_specs=pl.BlockSpec((1, width, heads), lambda d: (d, 0, 0)),
         out_shape=jax.ShapeDtypeStruct((count, width, heads), F32),
-        compiler_params=pltpu.CompilerParams(vmem_limit_bytes=16 << 20),
-        cost_estimate=pl.CostEstimate(flops=0, bytes_accessed=0, transcendentals=0),
+        compiler_params=pltpu.CompilerParams(vmem_limit_bytes=10 << 20),
+        cost_estimate=pl.CostEstimate(
+            flops=span * 2 * members * rows * count * width * heads,
+            bytes_accessed=0,
+            transcendentals=0,
+        ),
         name="partial_grad",
     )(tokens, first)
 
 
-def project_kernel(sizes, first, last, place_ref, tokens_ref, grads_ref, *refs):
+def project_kernel(sizes, first, place_ref, tokens_ref, grads_ref, *refs):
     n = len(sizes)
     weight_refs, refs = refs[:n], refs[n:]
     if not first:
         sum_ref, _, refs = refs[0], refs[1], refs[2:]
     sum_out, grad_out, token_buf, grad_buf, in_sem, out_sem = refs
-    width = token_buf.shape[2] // NX
-    rows = token_buf.shape[1]
-    pieces = [(i, j) for i, size in enumerate(sizes) for j in range(size)]
-
-    def columns(k, c):
-        return pl.ds(pl.multiple_of(place_ref[k * NX + c] * width, width), width)
-
-    def fetch(k, c):
+    count = sum(sizes)
+    width = token_buf.shape[1] // count
+
+    def columns(k):
+        return pl.ds(pl.multiple_of(place_ref[k] * width, width), width)
+
+    def fetch(k):
         return pltpu.make_async_copy(
-            tokens_ref.at[:, columns(k, c)],
-            token_buf.at[k, :, pl.ds(c * width, width)],
-            in_sem.at[k, c],
-        )
-
-    def put(k, c):
+            tokens_ref.at[:, columns(k)], token_buf.at[:, pl.ds(k * width, width)], in_sem.at[k]
+        )
+
+    def put(k):
         return pltpu.make_async_copy(
-            grad_buf.at[k, :, pl.ds(c * width, width)],
-            grad_out.at[:, columns(k, c)],
-            out_sem.at[k, c],
-        )
-
-    for k in range(len(pieces)):
-        for c in range(NX):
-            fetch(k, c).start()
+            grad_buf.at[:, pl.ds(k * width, width)], grad_out.at[:, columns(k)], out_sem.at[k]
+        )
+
+    for k in range(count):
+        fetch(k).start()
     grads = grads_ref[...]
-    total = None if first else sum_ref[...]
-    for k, (i, j) in enumerate(pieces):
-        weight = weight_refs[i][pl.ds(j * NX * width, NX * width), :]
-        grad_buf[k] = lax.dot_general(
-            grads, weight, (((1,), (1,)), ((), ())), preferred_element_type=F32
-        ).astype(BF16)
-        for c in range(NX):
-            put(k, c).start()
-        for c in range(NX):
-            fetch(k, c).wait()
-        term = jnp.dot(token_buf[k], weight, preferred_element_type=F32)
+    at = 0
+    for weight_ref, size in zip(weight_refs, sizes):
+        for j in range(0, size, 4):
+            grad_buf[:, pl.ds((at + j) * width, 4 * width)] = lax.dot_general(
+                grads,
+                weight_ref[pl.ds(j * width, 4 * width), :],
+                (((1,), (1,)), ((), ())),
+                preferred_element_type=F32,
+            ).astype(BF16)
+            for k in range(at + j, at + j + 4):
+                put(k).start()
+        at += size
+    for k in range(count):
+        fetch(k).wait()
+    total, at = None if first else sum_ref[...], 0
+    for weight_ref, size in zip(weight_refs, sizes):
+        term = jnp.dot(
+            token_buf[:, pl.ds(at * width, size * width)],
+            weight_ref[...],
+            preferred_element_type=F32,
+        )
         total = term if total is None else total + term
+        at += size
     sum_out[...] = total.astype(sum_out.dtype)
-    for k in range(len(pieces)):
-        for c in range(NX):
-            put(k, c).wait()
+    for k in range(count):
+        put(k).wait()
 
 
 def project(tokens, grads, weights, place, state, last, span=1):
     rows, heads = grads.shape
     tokens = pltpu.with_memory_space_constraint(tokens, pltpu.HBM)
     width = tokens.shape[1] // (NY * NX * NZ)
-    pair = NX * width
-    sizes = tuple(w.shape[0] // pair for w in weights)
+    sizes = tuple(w.shape[0] // width for w in weights)
     count = sum(sizes)
     first = state is None
     whole = pl.BlockSpec(memory_space=pltpu.VMEM)
     n_in = 3 + len(weights)
     return pl.pallas_call(
-        functools.partial(project_kernel, sizes, first, last),
+        functools.partial(project_kernel, sizes, first),
         in_specs=[pl.BlockSpec(memory_space=pltpu.SMEM), HBM, whole]
         + [whole] * len(weights)
         + ([] if first else [whole, HBM]),
@@ -204,16 +209,16 @@
             pltpu.HBM(tokens.shape, BF16),
         ),
         scratch_shapes=[
-            pltpu.VMEM((count, rows, pair), BF16),
-            pltpu.VMEM((count, rows, pair), BF16),
-            pltpu.SemaphoreType.DMA((count, NX)),
-            pltpu.SemaphoreType.DMA((count, NX)),
+            pltpu.VMEM((rows, count * width), BF16),
+            pltpu.VMEM((rows, count * width), BF16),
+            pltpu.SemaphoreType.DMA((count,)),
+            pltpu.SemaphoreType.DMA((count,)),
         ],
         input_output_aliases={} if first else {n_in + 1: 1},
-        compiler_params=pltpu.CompilerParams(vmem_limit_bytes=24 << 20),
+        compiler_params=pltpu.CompilerParams(vmem_limit_bytes=14 << 20),
         cost_estimate=pl.CostEstimate(
-            flops=span * 4 * rows * heads * count * pair,
-            bytes_accessed=count * pair * (rows * 4 + heads * 2),
+            flops=span * 4 * rows * heads * count * width,
+            bytes_accessed=count * width * (rows * 4 + heads * 2),
             transcendentals=0,
         ),
         name="project",
@@ -249,6 +254,7 @@
             jax.ShapeDtypeStruct(inner.shape, BF16),
             jax.ShapeDtypeStruct(state[0].shape[1:], F32),
         ),
+        compiler_params=pltpu.CompilerParams(vmem_limit_bytes=4 << 20),
         name="outer_step",
     )(plan, rank, near, far, inner, *state)
 
@@ -281,8 +287,8 @@
 
     y, x = lax.axis_index("y"), lax.axis_index("xl")
 
-    def places(*shifts, rows=range(NY)):
-        members = [(y - v) % NY * NX + (x ^ c) for v in rows for c in range(NX)]
+    def places(*shifts):
+        members = [(y - v) % NY * NX + (x ^ c) for v in range(NY) for c in range(NX)]
         at = [member * NZ + (z + dz) % NZ for dz in shifts for member in members]
         return jnp.stack(at).astype(jnp.int32)
 
@@ -294,47 +300,48 @@
         if earlier:
             right, left = after(right, *earlier), after(left, *earlier)
         ring.append((shift_z(right, 1), shift_z(left, -1)))
+        at = places(-k, k)
         carries.append(
-            project(tokens, grads_out, list(ring[-1]), places(-k, k), carries[-1], False, span)
+            project(tokens, grads_out, list(ring[-1]), at, carries[-1], False, span)
         )
 
     ring_step(1, 5)
-    ring_step(2, 1)
+    ring_step(2, 5)
 
     first, _ = lax.optimization_barrier((first, carries[1][0]))
     second = lax.all_to_all(after(second, first), sub, 0, 0)
     state = after(jnp.stack([anchor, momentum]), first)
     first, ring[2] = lax.optimization_barrier((first, ring[2]))
-    terms = {}
-    for s, stage in enumerate(STAGES):
-        if s == 1:
-            second = after(second, carries[2][0])
-        sums = partial_grad((first, second)[s], first, heads, width, s == 0)
-        terms.update({d: sums[i] for i, d in enumerate(stage)})
+    def terms(*distances):
+        s = 0 if distances[0] in STAGES[0] else 1
+        at = STAGES[s].index(distances[0]) + (heads // width if s == 0 else 0)
+        span = 8 if s == 0 else 1
+        return partial_grad((first, second)[s], first, heads, width, at, len(distances), span)
 
     half = width // 2
-    right = shift_z(terms[4][:half], 1)
-    left = shift_z(terms[4][half:], -1)
-    right = jnp.concatenate([terms[3][:half] + right, terms[3][half:]])
-    left = jnp.concatenate([terms[5][:half], terms[5][half:] + left])
+    middle, ahead, back = terms(4, 3, 5)
+    right, left = shift_z(middle[:half], 1), shift_z(middle[half:], -1)
+    states = [state, shift_core(state)]
+    right = jnp.concatenate([ahead[:half] + right, ahead[half:]])
+    left = jnp.concatenate([back[:half], back[half:] + left])
+    right, left, states = lax.optimization_barrier((right, left, states))
     right, left = shift_z(right, 1), shift_z(left, -1)
     ring_step(3, 1, right, left)
-    states = [state, shift_core(state)]
-    right, left = terms[2] + right, terms[6] + left
-    right, left, states = lax.optimization_barrier((right, left, states))
+    ahead, back = terms(2, 6)
+    right, left = ahead + right, back + left
+    states += [shift_far(x) for x in states]
     right, left = shift_z(right, 1), shift_z(left, -1)
-    states += [shift_far(x) for x in states]
-    right, left = terms[1] + right, terms[7] + left
-    right, left, states, ring[3] = lax.optimization_barrier((right, left, states, ring[3]))
+    second, states, _ = lax.optimization_barrier((second, states, carries[2][0]))
+    ahead, back, rest = terms(1, 7, 0)
+    right, left = ahead + right, back + left
+    right, left, ring[3] = lax.optimization_barrier((right, left, ring[3]))
     right, left = shift_z(right, 1), shift_z(left, -1)
-    right = after(right, carries[3][0])
-    inner = local_weight.astype(F32) - inner_rate * (terms[0] + right + left)
+    inner = local_weight.astype(F32) - inner_rate * (rest + right + left)
 
     near = inner + shift_core(inner)
+    far = shift_far(near)
     half = part // 2
     right, left = shift_z(ring[3][0][:half], 1), shift_z(ring[3][1][half:], -1)
-    near, right, left = lax.optimization_barrier((near, right, left))
-    far = shift_far(near)
     values, act_grad = project(tokens, grads_out, [right, left], places(4), carries[3], True)
     new_weight, new_momentum = outer_step(
         plan, jnp.reshape(rank, (1,)).astype(jnp.int32), near, far, inner, states

time: 173 us -> 165 us (0.954)
  waiting for transfers between devices: 64.5 us -> 60.3 us
  Pallas kernels: 40.2 us -> 36.1 us
    pallas_call x5, Pallas kernels: 25.3 us -> 20 us  [project(): pl.pallas_call(functools.partial(project_kernel, sizes, first), in_specs=...]
    ppermute x3, waiting for transfers between devices: 4.67 us -> 0.01 us  [shift_far(): return lax.ppermute(x, 'xh', [(0, 1), (1, 0)])]
    ppermute x16, starting transfers between devices: 21.9 us -> 25.9 us  [shift_z(): return lax.ppermute(x, 'z', [(i, (i + dz) % NZ) for i in range(NZ)])]
    ppermute x16, waiting for transfers between devices: 41.2 us -> 38.7 us  [shift_z(): return lax.ppermute(x, 'z', [(i, (i + dz) % NZ) for i in range(NZ)])]
    ppermute x3, starting transfers between devices: 8.31 us -> 5.89 us  [shift_far(): return lax.ppermute(x, 'xh', [(0, 1), (1, 0)])]
    unnamed x34 -> x18, local copies, waits for them, and re-layouts: 3.33 us -> 1.49 us
    pallas_call x2 -> x3, Pallas kernels: 8.15 us -> 9.69 us  [partial_grad(): pl.pallas_call(grad_kernel, grid=(count,), in_specs=[pl.BlockSpec((member...]
  transfers between devices with their start and end apart: 27 -> 27, of which waited for: 14 -> 14; matrix products, arithmetic and copies ran while one was open for 2% -> 3% of each run, Pallas kernels for 22% -> 21%
where the time goes in v3:
time: 165 us; the launch traced here: 164 us
  waiting for transfers between devices  60.3 us (37%)
  starting transfers between devices  58.8 us (36%)
  Pallas kernels  36.1 us (22%)
  local copies, waits for them, and re-layouts  5 us (3%)
  other arithmetic  3.2 us (2%)
    ppermute x16, waiting for transfers between devices, shift_z(): return lax.ppermute(x, 'z', [(i, (i + dz) % NZ) for i in range(NZ)])  38.7 us
    ppermute x16, starting transfers between devices, shift_z(): return lax.ppermute(x, 'z', [(i, (i + dz) % NZ) for i in range(NZ)])  25.9 us
    pallas_call x5, Pallas kernels, project(): pl.pallas_call(functools.partial(project_kernel, sizes, first), in_specs=...  20 us
    ppermute x2, starting transfers between devices, shift_core(): return lax.ppermute(x, 'core', [(0, 1), (1, 0)])  12 us
    pallas_call x3, Pallas kernels, partial_grad(): pl.pallas_call(grad_kernel, grid=(count,), in_specs=[pl.BlockSpec((member...  9.69 us
    ppermute x3, waiting for transfers between devices, shift_y(): return lax.ppermute(x, 'y', [(i, (i + dy) % NY) for i in range(NY)])  9.61 us
    all_to_all x1, waiting for transfers between devices, local(): first = lax.all_to_all(first, sub, 0, 0)  6.5 us
    ppermute x3, starting transfers between devices, shift_far(): return lax.ppermute(x, 'xh', [(0, 1), (1, 0)])  5.89 us
  transfers between devices with their start and end apart: 27, of which 14 were waited for; matrix products, arithmetic and copies ran while one was open for 3% of the time, Pallas kernels for 21%

profile of v3, /device:TPU:1, one launch (start us, length us, event | category | flops | bytes accessed | tf_op | source)
XLA Modules:
  0.0 164.4 jit_solution(3252413904245851505)
XLA Ops:
  6.3 3.6 %collective-permute-start.3 = (bf16[2,128,512]{2,1,0:T(8,128)(2,1)S(1)}, bf16[2,128,512]{2,1,0:T(8,128)(2,1)S(1)}, u32[]{:S(2)}, u32[]{:S(2)}) collective-permute-start(bf16[2,128,512]{2,1,0:T(8,128)(2,1)S(1)} %get-tuple-element.89), channel_id=1, source_target_pairs={{0,48},{16,0},{32,16},{48,32},{1,49},{17,1},{33,17},{49,33},{2,50}... | collective-permute-start | bytes 786440 | tf_op jit(solution)/shard_map/ppermute | solution.py:28
  11.0 4.6 %sort_tokens.1 = (bf16[8,256,896]{2,1,0:T(8,128)(2,1)}, bf16[8,256,640]{2,1,0:T(8,128)(2,1)}) custom-call(s32[8]{0:T(128)S(1)} %stack.281.place_ref, bf16[256,8192]{1,0:T(8,128)(2,1)} %bitcast.140, bf16[256,512]{1,0:T(8,128)(2,1)} %bitcast.131), custom_call_target="tpu_custom_call" | custom-call | bytes 8912896 | tf_op jit(solution)/shard_map/sort_tokens/pallas_call | solution.py:87
  15.6 4.6 %collective-permute-done.3 = bf16[2,128,512]{2,1,0:T(8,128)(2,1)S(1)} collective-permute-done((bf16[2,128,512]{2,1,0:T(8,128)(2,1)S(1)}, bf16[2,128,512]{2,1,0:T(8,128)(2,1)S(1)}, u32[]{:S(2)}, u32[]{:S(2)}) %collective-permute-start.3) | collective-permute-done | bytes 262176 | tf_op jit(solution)/shard_map/ppermute | solution.py:28
  20.2 5.0 %collective-permute-done.1 = bf16[2,128,512]{2,1,0:T(8,128)(2,1)S(1)} collective-permute-done((bf16[2,128,512]{2,1,0:T(8,128)(2,1)S(1)}, bf16[2,128,512]{2,1,0:T(8,128)(2,1)S(1)}, u32[]{:S(2)}, u32[]{:S(2)}) %collective-permute-start.1) | collective-permute-done | bytes 262176 | tf_op jit(solution)/shard_map/ppermute | solution.py:28
  25.4 4.7 %all-to-all-start = ((bf16[8,256,896]{2,1,0:T(8,128)(2,1)}), bf16[8,256,896]{2,1,0:T(8,128)(2,1)}, u32[]{:S(2)}, u32[]{:S(2)}) async-start(bf16[8,256,896]{2,1,0:T(8,128)(2,1)} %get-tuple-element.43), calls=%async_computation | async-start | bytes 7340032 | tf_op jit(solution)/shard_map/all_to_all | solution.py:286
  31.7 4.0 %collective-permute-start.5 = (bf16[1024,512]{1,0:T(8,128)(2,1)S(1)}, bf16[1024,512]{1,0:T(8,128)(2,1)}, u32[]{:S(2)}, u32[]{:S(2)}) collective-permute-start(bf16[1024,512]{1,0:T(8,128)(2,1)S(1)} %bitcast.138), channel_id=1, source_target_pairs={{0,7},{1,0},{2,1},{3,2},{4,3},{5,4},{6,5},{7,6},{8,15},{9,8},{10,9... | collective-permute-start | bytes 3145736 | tf_op jit(solution)/shard_map/ppermute | solution.py:24
  36.0 2.7 %project.5 = (f32[256,512]{1,0:T(8,128)S(1)}, bf16[256,8192]{1,0:T(8,128)(2,1)}) custom-call(s32[8]{0:T(128)S(1)} %stack.314.place_ref, bf16[256,8192]{1,0:T(8,128)(2,1)} %bitcast.141, bf16[256,512]{1,0:T(8,128)(2,1)S(1)} %bitcast.132, bf16[1024,512]{1,0:T(8,128)(2,1)S(1)} %bitcast.139), custom_call_target="tpu_custom_call" | custom-call | flops 536870912 | bytes 2097152 | tf_op jit(solution)/shard_map/project/pallas_call | solution.py:201
  38.7 20.2 %collective-permute-done.4.refs_0_ = bf16[1024,512]{1,0:T(8,128)(2,1)} collective-permute-done((bf16[1024,512]{1,0:T(8,128)(2,1)S(1)}, bf16[1024,512]{1,0:T(8,128)(2,1)}, u32[]{:S(2)}, u32[]{:S(2)}) %collective-permute-start.4) | collective-permute-done | bytes 1048608 | tf_op jit(solution)/shard_map/ppermute | solution.py:24
  61.6 4.6 %project.6 = (f32[256,512]{1,0:T(8,128)S(1)}, bf16[256,8192]{1,0:T(8,128)(2,1)}) custom-call(s32[16]{0:T(128)S(1)} %stack.305.place_ref, bf16[256,8192]{1,0:T(8,128)(2,1)} %bitcast.142, bf16[256,512]{1,0:T(8,128)(2,1)S(1)} %bitcast.133, bf16[1024,512]{1,0:T(8,128)(2,1)} %collective-permute-done.4.refs_0_, ...), custom_call_target="tpu_custom_call", output_to_operand_aliasing={{1}: (6, {})} | custom-call | flops 5368709120 | bytes 4194304 | tf_op jit(solution)/shard_map/project/pallas_call | solution.py:201
  67.0 6.5 %all-to-all-done.tokens_ref.grads_ref = bf16[8,256,896]{2,1,0:T(8,128)(2,1)} async-done(((bf16[8,256,896]{2,1,0:T(8,128)(2,1)}), bf16[8,256,896]{2,1,0:T(8,128)(2,1)}, u32[]{:S(2)}, u32[]{:S(2)}) %all-to-all-start) | async-done | bytes 3670048 | tf_op jit(solution)/shard_map/all_to_all | solution.py:286
  73.5 3.6 %all-to-all-start.1 = ((bf16[8,256,640]{2,1,0:T(8,128)(2,1)}), bf16[8,256,640]{2,1,0:T(8,128)(2,1)S(1)}, u32[]{:S(2)}, u32[]{:S(2)}) async-start(bf16[8,256,640]{2,1,0:T(8,128)(2,1)} %get-tuple-element.49), calls=%async_computation.1 | async-start | bytes 5242880 | tf_op jit(solution)/shard_map/all_to_all | solution.py:312
  77.2 6.9 %collective-permute-done.6.refs_0_ = bf16[1024,512]{1,0:T(8,128)(2,1)} collective-permute-done((bf16[1024,512]{1,0:T(8,128)(2,1)}, bf16[1024,512]{1,0:T(8,128)(2,1)}, u32[]{:S(2)}, u32[]{:S(2)}) %collective-permute-start.6) | collective-permute-done | bytes 1048608 | tf_op jit(solution)/shard_map/ppermute | solution.py:24
  84.0 3.8 %partial_grad.3 = f32[3,128,512]{2,1,0:T(8,128)S(1)} custom-call(bf16[8,256,896]{2,1,0:T(8,128)(2,1)} %all-to-all-done.tokens_ref.grads_ref, bf16[8,256,896]{2,1,0:T(8,128)(2,1)} %all-to-all-done.tokens_ref.grads_ref), custom_call_target="tpu_custom_call" | custom-call | flops 6442450944 | tf_op jit(solution)/shard_map/partial_grad/pallas_call | solution.py:120
  90.4 2.8 %collective-permute-start.10 = (f32[2,128,128]{2,1,0:T(8,128)S(1)}, f32[2,128,128]{2,1,0:T(8,128)}, u32[]{:S(2)}, u32[]{:S(2)}) collective-permute-start(f32[2,128,128]{2,1,0:T(8,128)S(1)} %pad_maximum_fusion.4.refs_0_), channel_id=1, source_target_pairs={{0,64},{64,0},{1,65},{65,1},{2,66},{66,2},{3,67},{67,3},{4,68},{68... | collective-permute-start | bytes 393224 | tf_op jit(solution)/shard_map/ppermute | solution.py:36
  98.1 2.8 %collective-permute-start.11 = (f32[2,128,128]{2,1,0:T(8,128)S(1)}, f32[2,128,128]{2,1,0:T(8,128)S(1)}, u32[]{:S(2)}, u32[]{:S(2)}) collective-permute-start(f32[2,128,128]{2,1,0:T(8,128)S(1)} %pad_maximum_fusion.4.refs_0_), channel_id=1, source_target_pairs={{0,128},{128,0},{1,129},{129,1},{2,130},{130,2},{3,131},{131,3},{4... | collective-permute-start | bytes 393224 | tf_op jit(solution)/shard_map/ppermute | solution.py:40
  108.4 2.7 %partial_grad.5 = f32[2,128,512]{2,1,0:T(8,128)S(1)} custom-call(bf16[8,256,640]{2,1,0:T(8,128)(2,1)S(1)} %all-to-all-done.1.tokens_ref, bf16[8,256,896]{2,1,0:T(8,128)(2,1)} %all-to-all-done.tokens_ref.grads_ref), custom_call_target="tpu_custom_call" | custom-call | flops 536870912 | tf_op jit(solution)/shard_map/partial_grad/pallas_call | solution.py:120
  112.1 5.7 %collective-permute-start.16 = (f32[128,512]{1,0:T(8,128)S(1)}, f32[128,512]{1,0:T(8,128)S(1)}, u32[]{:S(2)}, u32[]{:S(2)}) collective-permute-start(f32[128,512]{1,0:T(8,128)S(1)} %get-tuple-element.86), channel_id=1, source_target_pairs={{0,7},{1,0},{2,1},{3,2},{4,3},{5,4},{6,5},{7,6},{8,15},{9,8},{10,9... | collective-permute-start | bytes 786440 | tf_op jit(solution)/shard_map/ppermute | solution.py:24
  118.4 4.6 %project.7 = (f32[256,512]{1,0:T(8,128)S(1)}, bf16[256,8192]{1,0:T(8,128)(2,1)}) custom-call(s32[16]{0:T(128)S(1)} %stack.334.place_ref, bf16[256,8192]{1,0:T(8,128)(2,1)} %bitcast.143, bf16[256,512]{1,0:T(8,128)(2,1)S(1)} %bitcast.134, bf16[1024,512]{1,0:T(8,128)(2,1)} %collective-permute-done.6.refs_0_, ...), custom_call_target="tpu_custom_call", output_to_operand_aliasing={{1}: (6, {})} | custom-call | flops 5368709120 | bytes 4194304 | tf_op jit(solution)/shard_map/project/pallas_call | solution.py:201
  123.1 3.2 %partial_grad.4 = f32[3,128,512]{2,1,0:T(8,128)S(1)} custom-call(bf16[8,256,640]{2,1,0:T(8,128)(2,1)S(1)} %all-to-all-done.1.tokens_ref, bf16[8,256,896]{2,1,0:T(8,128)(2,1)} %all-to-all-done.tokens_ref.grads_ref), custom_call_target="tpu_custom_call" | custom-call | flops 805306368 | tf_op jit(solution)/shard_map/partial_grad/pallas_call | solution.py:120
  126.3 4.5 %collective-permute-done.16 = f32[128,512]{1,0:T(8,128)S(1)} collective-permute-done((f32[128,512]{1,0:T(8,128)S(1)}, f32[128,512]{1,0:T(8,128)S(1)}, u32[]{:S(2)}, u32[]{:S(2)}) %collective-permute-start.16) | collective-permute-done | bytes 262176 | tf_op jit(solution)/shard_map/ppermute | solution.py:24
  141.0 9.2 %collective-permute-start.23 = (f32[128,512]{1,0:T(8,128)S(1)}, f32[128,512]{1,0:T(8,128)S(1)}, u32[]{:S(2)}, u32[]{:S(2)}) collective-permute-start(f32[128,512]{1,0:T(8,128)S(1)} %fusion.3.inner_ref), channel_id=1, source_target_pairs={{0,64},{64,0},{1,65},{65,1},{2,66},{66,2},{3,67},{67,3},{4,68},{68... | collective-permute-start | bytes 786440 | tf_op jit(solution)/shard_map/ppermute | solution.py:36
  151.4 2.8 %collective-permute-start.24 = (f32[128,512]{1,0:T(8,128)S(1)}, f32[128,512]{1,0:T(8,128)S(1)}, u32[]{:S(2)}, u32[]{:S(2)}) collective-permute-start(f32[128,512]{1,0:T(8,128)S(1)} %add.613.near_ref), channel_id=1, source_target_pairs={{0,128},{128,0},{1,129},{129,1},{2,130},{130,2},{3,131},{131,3},{4... | collective-permute-start | bytes 786440 | tf_op jit(solution)/shard_map/ppermute | solution.py:40
  154.4 4.6 %project.8 = (f32[256,512]{1,0:T(8,128)S(1)}, bf16[256,8192]{1,0:T(8,128)(2,1)}) custom-call(s32[16]{0:T(128)S(1)} %stack.351.place_ref, bf16[256,8192]{1,0:T(8,128)(2,1)} %bitcast.144, bf16[256,512]{1,0:T(8,128)(2,1)S(1)} %bitcast.135, bf16[1024,512]{1,0:T(8,128)(2,1)} %collective-permute-done.17.refs_0_, ...), custom_call_target="tpu_custom_call", output_to_operand_aliasing={{1}: (6, {})} | custom-call | flops 1073741824 | bytes 4194304 | tf_op jit(solution)/shard_map/project/pallas_call | solution.py:201
  159.1 3.4 %project.9 = (bf16[256,512]{1,0:T(8,128)(2,1)}, bf16[256,8192]{1,0:T(8,128)(2,1)}) custom-call(s32[8]{0:T(128)S(1)} %stack.272.place_ref, bf16[256,8192]{1,0:T(8,128)(2,1)} %bitcast.145, bf16[256,512]{1,0:T(8,128)(2,1)S(1)} %bitcast.136, bf16[512,512]{1,0:T(8,128)(2,1)S(1)} %collective-permute-done.19.refs_0_, ...), custom_call_target="tpu_custom_call", output_to_operand_aliasing={{1}: (6, {})} | custom-call | flops 536870912 | bytes 2097152 | tf_op jit(solution)/shard_map/project/pallas_call | solution.py:201
  (76 shorter events, 42.2 us)
Async XLA Ops:
  6.3 13.9 %collective-permute-start.3 = (bf16[2,128,512]{2,1,0:T(8,128)(2,1)S(1)}, bf16[2,128,512]{2,1,0:T(8,128)(2,1)S(1)}, u32[]{:S(2)}, u32[]{:S(2)}) collective-permute-start(bf16[2,128,512]{2,1,0:T(8,128)(2,1)S(1)} %get-tuple-element.89), channel_id=1, source_target_pairs={{0,48},{16,0},{32,16},{48,32},{1,49},{17,1},{33,17},{49,33},{2,50}... | collective-permute-start | bytes 786440 | tf_op jit(solution)/shard_map/ppermute | solution.py:28
  9.9 10.3 %collective-permute-start.2 = (bf16[2,128,512]{2,1,0:T(8,128)(2,1)S(1)}, bf16[2,128,512]{2,1,0:T(8,128)(2,1)S(1)}, u32[]{:S(2)}, u32[]{:S(2)}) collective-permute-start(bf16[2,128,512]{2,1,0:T(8,128)(2,1)S(1)} %get-tuple-element.89), channel_id=1, source_target_pairs={{0,32},{16,48},{32,0},{48,16},{1,33},{17,49},{33,1},{49,17},{2,34}... | collective-permute-start | bytes 786440 | tf_op jit(solution)/shard_map/ppermute | solution.py:28
  10.2 15.0 %collective-permute-start.1 = (bf16[2,128,512]{2,1,0:T(8,128)(2,1)S(1)}, bf16[2,128,512]{2,1,0:T(8,128)(2,1)S(1)}, u32[]{:S(2)}, u32[]{:S(2)}) collective-permute-start(bf16[2,128,512]{2,1,0:T(8,128)(2,1)S(1)} %get-tuple-element.89), channel_id=1, source_target_pairs={{0,16},{16,32},{32,48},{48,0},{1,17},{17,33},{33,49},{49,1},{2,18}... | collective-permute-start | bytes 786440 | tf_op jit(solution)/shard_map/ppermute | solution.py:28
  25.4 48.1 %all-to-all-start = ((bf16[8,256,896]{2,1,0:T(8,128)(2,1)}), bf16[8,256,896]{2,1,0:T(8,128)(2,1)}, u32[]{:S(2)}, u32[]{:S(2)}) async-start(bf16[8,256,896]{2,1,0:T(8,128)(2,1)} %get-tuple-element.43), calls=%async_computation | async-start | bytes 7340032 | tf_op jit(solution)/shard_map/all_to_all | solution.py:286
  30.0 28.9 %collective-permute-start.4 = (bf16[1024,512]{1,0:T(8,128)(2,1)S(1)}, bf16[1024,512]{1,0:T(8,128)(2,1)}, u32[]{:S(2)}, u32[]{:S(2)}) collective-permute-start(bf16[1024,512]{1,0:T(8,128)(2,1)S(1)} %bitcast.137), channel_id=1, source_target_pairs={{0,1},{1,2},{2,3},{3,4},{4,5},{5,6},{6,7},{7,0},{8,9},{9,10},{10,1... | collective-permute-start | bytes 3145736 | tf_op jit(solution)/shard_map/ppermute | solution.py:24
  31.7 27.1 %collective-permute-start.5 = (bf16[1024,512]{1,0:T(8,128)(2,1)S(1)}, bf16[1024,512]{1,0:T(8,128)(2,1)}, u32[]{:S(2)}, u32[]{:S(2)}) collective-permute-start(bf16[1024,512]{1,0:T(8,128)(2,1)S(1)} %bitcast.138), channel_id=1, source_target_pairs={{0,7},{1,0},{2,1},{3,2},{4,3},{5,4},{6,5},{7,6},{8,15},{9,8},{10,9... | collective-permute-start | bytes 3145736 | tf_op jit(solution)/shard_map/ppermute | solution.py:24
  58.9 25.2 %collective-permute-start.6 = (bf16[1024,512]{1,0:T(8,128)(2,1)}, bf16[1024,512]{1,0:T(8,128)(2,1)}, u32[]{:S(2)}, u32[]{:S(2)}) collective-permute-start(bf16[1024,512]{1,0:T(8,128)(2,1)} %collective-permute-done.4.refs_0_), channel_id=1, source_target_pairs={{0,1},{1,2},{2,3},{3,4},{4,5},{5,6},{6,7},{7,0},{8,9},{9,10},{10,1... | collective-permute-start | bytes 3145736 | tf_op jit(solution)/shard_map/ppermute | solution.py:24
  58.9 25.2 %collective-permute-start.7 = (bf16[1024,512]{1,0:T(8,128)(2,1)}, bf16[1024,512]{1,0:T(8,128)(2,1)}, u32[]{:S(2)}, u32[]{:S(2)}) collective-permute-start(bf16[1024,512]{1,0:T(8,128)(2,1)} %collective-permute-done.5.refs_1_), channel_id=1, source_target_pairs={{0,7},{1,0},{2,1},{3,2},{4,3},{5,4},{6,5},{7,6},{8,15},{9,8},{10,9... | collective-permute-start | bytes 3145736 | tf_op jit(solution)/shard_map/ppermute | solution.py:24
  73.5 34.9 %all-to-all-start.1 = ((bf16[8,256,640]{2,1,0:T(8,128)(2,1)}), bf16[8,256,640]{2,1,0:T(8,128)(2,1)S(1)}, u32[]{:S(2)}, u32[]{:S(2)}) async-start(bf16[8,256,640]{2,1,0:T(8,128)(2,1)} %get-tuple-element.49), calls=%async_computation.1 | async-start | bytes 5242880 | tf_op jit(solution)/shard_map/all_to_all | solution.py:312
  90.4 6.2 %collective-permute-start.10 = (f32[2,128,128]{2,1,0:T(8,128)S(1)}, f32[2,128,128]{2,1,0:T(8,128)}, u32[]{:S(2)}, u32[]{:S(2)}) collective-permute-start(f32[2,128,128]{2,1,0:T(8,128)S(1)} %pad_maximum_fusion.4.refs_0_), channel_id=1, source_target_pairs={{0,64},{64,0},{1,65},{65,1},{2,66},{66,2},{3,67},{67,3},{4,68},{68... | collective-permute-start | bytes 393224 | tf_op jit(solution)/shard_map/ppermute | solution.py:36
  96.6 5.7 %collective-permute-start.15 = (f32[128,512]{1,0:T(8,128)}, f32[128,512]{1,0:T(8,128)S(1)}, u32[]{:S(2)}, u32[]{:S(2)}) collective-permute-start(f32[128,512]{1,0:T(8,128)} %get-tuple-element.58), channel_id=1, source_target_pairs={{0,7},{1,0},{2,1},{3,2},{4,3},{5,4},{6,5},{7,6},{8,15},{9,8},{10,9... | collective-permute-start | bytes 786440 | tf_op jit(solution)/shard_map/ppermute | solution.py:24
  97.2 6.7 %collective-permute-start.13 = (f32[128,512]{1,0:T(8,128)}, f32[128,512]{1,0:T(8,128)}, u32[]{:S(2)}, u32[]{:S(2)}) collective-permute-start(f32[128,512]{1,0:T(8,128)} %get-tuple-element.57), channel_id=1, source_target_pairs={{0,1},{1,2},{2,3},{3,4},{4,5},{5,6},{6,7},{7,0},{8,9},{9,10},{10,1... | collective-permute-start | bytes 786440 | tf_op jit(solution)/shard_map/ppermute | solution.py:24
  98.1 19.6 %collective-permute-start.11 = (f32[2,128,128]{2,1,0:T(8,128)S(1)}, f32[2,128,128]{2,1,0:T(8,128)S(1)}, u32[]{:S(2)}, u32[]{:S(2)}) collective-permute-start(f32[2,128,128]{2,1,0:T(8,128)S(1)} %pad_maximum_fusion.4.refs_0_), channel_id=1, source_target_pairs={{0,128},{128,0},{1,129},{129,1},{2,130},{130,2},{3,131},{131,3},{4... | collective-permute-start | bytes 393224 | tf_op jit(solution)/shard_map/ppermute | solution.py:40
  100.9 22.1 %collective-permute-start.12 = (f32[2,128,128]{2,1,0:T(8,128)}, f32[2,128,128]{2,1,0:T(8,128)}, u32[]{:S(2)}, u32[]{:S(2)}) collective-permute-start(f32[2,128,128]{2,1,0:T(8,128)} %collective-permute-done.10.refs_1_), channel_id=1, source_target_pairs={{0,128},{128,0},{1,129},{129,1},{2,130},{130,2},{3,131},{131,3},{4... | collective-permute-start | bytes 393224 | tf_op jit(solution)/shard_map/ppermute | solution.py:40
  104.0 28.0 %collective-permute-start.17 = (bf16[1024,512]{1,0:T(8,128)(2,1)}, bf16[1024,512]{1,0:T(8,128)(2,1)}, u32[]{:S(2)}, u32[]{:S(2)}) collective-permute-start(bf16[1024,512]{1,0:T(8,128)(2,1)} %collective-permute-done.6.refs_0_), channel_id=1, source_target_pairs={{0,1},{1,2},{2,3},{3,4},{4,5},{5,6},{6,7},{7,0},{8,9},{9,10},{10,1... | collective-permute-start | bytes 3145736 | tf_op jit(solution)/shard_map/ppermute | solution.py:24
  104.0 28.0 %collective-permute-start.18 = (bf16[1024,512]{1,0:T(8,128)(2,1)}, bf16[1024,512]{1,0:T(8,128)(2,1)}, u32[]{:S(2)}, u32[]{:S(2)}) collective-permute-start(bf16[1024,512]{1,0:T(8,128)(2,1)} %collective-permute-done.7.refs_1_), channel_id=1, source_target_pairs={{0,7},{1,0},{2,1},{3,2},{4,3},{5,4},{6,5},{7,6},{8,15},{9,8},{10,9... | collective-permute-start | bytes 3145736 | tf_op jit(solution)/shard_map/ppermute | solution.py:24
  112.1 18.7 %collective-permute-start.16 = (f32[128,512]{1,0:T(8,128)S(1)}, f32[128,512]{1,0:T(8,128)S(1)}, u32[]{:S(2)}, u32[]{:S(2)}) collective-permute-start(f32[128,512]{1,0:T(8,128)S(1)} %get-tuple-element.86), channel_id=1, source_target_pairs={{0,7},{1,0},{2,1},{3,2},{4,3},{5,4},{6,5},{7,6},{8,15},{9,8},{10,9... | collective-permute-start | bytes 786440 | tf_op jit(solution)/shard_map/ppermute | solution.py:24
  118.4 13.5 %collective-permute-start.14 = (f32[128,512]{1,0:T(8,128)S(1)}, f32[128,512]{1,0:T(8,128)S(1)}, u32[]{:S(2)}, u32[]{:S(2)}) collective-permute-start(f32[128,512]{1,0:T(8,128)S(1)} %get-tuple-element.87), channel_id=1, source_target_pairs={{0,1},{1,2},{2,3},{3,4},{4,5},{5,6},{6,7},{7,0},{8,9},{9,10},{10,1... | collective-permute-start | bytes 786440 | tf_op jit(solution)/shard_map/ppermute | solution.py:24
  132.0 8.2 %collective-permute-start.22 = (f32[128,512]{1,0:T(8,128)S(1)}, f32[128,512]{1,0:T(8,128)S(1)}, u32[]{:S(2)}, u32[]{:S(2)}) collective-permute-start(f32[128,512]{1,0:T(8,128)S(1)} %get-tuple-element.71), channel_id=1, source_target_pairs={{0,7},{1,0},{2,1},{3,2},{4,3},{5,4},{6,5},{7,6},{8,15},{9,8},{10,9... | collective-permute-start | bytes 786440 | tf_op jit(solution)/shard_map/ppermute | solution.py:24
  134.5 6.4 %collective-permute-start.21 = (f32[128,512]{1,0:T(8,128)S(1)}, f32[128,512]{1,0:T(8,128)S(1)}, u32[]{:S(2)}, u32[]{:S(2)}) collective-permute-start(f32[128,512]{1,0:T(8,128)S(1)} %get-tuple-element.70), channel_id=1, source_target_pairs={{0,1},{1,2},{2,3},{3,4},{4,5},{5,6},{6,7},{7,0},{8,9},{9,10},{10,1... | collective-permute-start | bytes 786440 | tf_op jit(solution)/shard_map/ppermute | solution.py:24
  135.6 23.5 %collective-permute-start.19 = (bf16[512,512]{1,0:T(8,128)(2,1)S(1)}, bf16[512,512]{1,0:T(8,128)(2,1)S(1)}, u32[]{:S(2)}, u32[]{:S(2)}) collective-permute-start(bf16[512,512]{1,0:T(8,128)(2,1)S(1)} %slice.60), channel_id=1, source_target_pairs={{0,1},{1,2},{2,3},{3,4},{4,5},{5,6},{6,7},{7,0},{8,9},{9,10},{10,1... | collective-permute-start | bytes 1572872 | tf_op jit(solution)/shard_map/ppermute | solution.py:24
  137.5 21.5 %collective-permute-start.20 = (bf16[512,512]{1,0:T(8,128)(2,1)}, bf16[512,512]{1,0:T(8,128)(2,1)S(1)}, u32[]{:S(2)}, u32[]{:S(2)}) collective-permute-start(bf16[512,512]{1,0:T(8,128)(2,1)} %slice.61), channel_id=1, source_target_pairs={{0,7},{1,0},{2,1},{3,2},{4,3},{5,4},{6,5},{7,6},{8,15},{9,8},{10,9... | collective-permute-start | bytes 1572872 | tf_op jit(solution)/shard_map/ppermute | solution.py:24
  141.0 10.4 %collective-permute-start.23 = (f32[128,512]{1,0:T(8,128)S(1)}, f32[128,512]{1,0:T(8,128)S(1)}, u32[]{:S(2)}, u32[]{:S(2)}) collective-permute-start(f32[128,512]{1,0:T(8,128)S(1)} %fusion.3.inner_ref), channel_id=1, source_target_pairs={{0,64},{64,0},{1,65},{65,1},{2,66},{66,2},{3,67},{67,3},{4,68},{68... | collective-permute-start | bytes 786440 | tf_op jit(solution)/shard_map/ppermute | solution.py:36
  151.4 11.1 %collective-permute-start.24 = (f32[128,512]{1,0:T(8,128)S(1)}, f32[128,512]{1,0:T(8,128)S(1)}, u32[]{:S(2)}, u32[]{:S(2)}) collective-permute-start(f32[128,512]{1,0:T(8,128)S(1)} %add.613.near_ref), channel_id=1, source_target_pairs={{0,128},{128,0},{1,129},{129,1},{2,130},{130,2},{3,131},{131,3},{4... | collective-permute-start | bytes 786440 | tf_op jit(solution)/shard_map/ppermute | solution.py:40
  (12 other events, 88.7 us)

commit v4 on v3

--- a/solution.py
+++ b/solution.py
@@ -98,7 +98,7 @@
         ],
         compiler_params=pltpu.CompilerParams(vmem_limit_bytes=14 << 20),
         cost_estimate=pl.CostEstimate(
-            flops=0, bytes_accessed=4 * rows * (depth + heads), transcendentals=0
+            flops=0, bytes_accessed=8 * rows * (depth + heads), transcendentals=0
         ),
         name="sort_tokens",
     )(place, tokens, grads)
@@ -276,9 +276,11 @@
     width = part // NZ
     after = lambda x, *others: lax.optimization_barrier((x, *others))[0]
 
-    pair = jnp.stack([local_weight, shift_x(local_weight)])
-    block = jnp.stack([pair] + [shift_y(pair, dy) for dy in range(1, NY)])
-    block = block.reshape(part, heads)
+    beside = shift_x(local_weight)
+    moved = [local_weight, beside]
+    for dy in range(1, NY):
+        moved += [shift_y(local_weight, dy), shift_y(beside, dy)]
+    block = [jnp.concatenate(moved[:NY]), jnp.concatenate(moved[NY:])]
 
     place = jnp.stack([(z + d) % NZ for d in range(NZ)]).astype(jnp.int32)
     first, second = sort_tokens(tokens, grads_out, place)
@@ -292,57 +294,64 @@
         at = [member * NZ + (z + dz) % NZ for dz in shifts for member in members]
         return jnp.stack(at).astype(jnp.int32)
 
-    carries = [project(tokens, grads_out, [block], places(0), None, False)]
-    ring = [(block, block)]
-
-    def ring_step(k, span, *earlier):
-        right, left = ring[-1]
-        if earlier:
-            right, left = after(right, *earlier), after(left, *earlier)
-        ring.append((shift_z(right, 1), shift_z(left, -1)))
-        at = places(-k, k)
-        carries.append(
-            project(tokens, grads_out, list(ring[-1]), at, carries[-1], False, span)
-        )
-
-    ring_step(1, 5)
-    ring_step(2, 5)
-
-    first, _ = lax.optimization_barrier((first, carries[1][0]))
+    def add(carry, k, pieces, span=1, last=False):
+        at = places(k) if k in (0, 4) else places(-k, k)
+        return project(tokens, grads_out, pieces, at, carry, last, span)
+
+    right, left = (
+        [[block[h]] for h in range(2)],
+        [[block[h]] for h in range(2)],
+    )
+    carry = add(None, 0, block)
+    for k in (1, 2):
+        for h in range(2):
+            right[h].append(shift_z(right[h][-1], 1))
+            left[h].append(shift_z(left[h][-1], -1))
+    carry = add(carry, 1, [right[0][1], right[1][1], left[0][1], left[1][1]], 10)
+
+    first, _ = lax.optimization_barrier((first, carry[0]))
     second = lax.all_to_all(after(second, first), sub, 0, 0)
     state = after(jnp.stack([anchor, momentum]), first)
-    first, ring[2] = lax.optimization_barrier((first, ring[2]))
+    step2 = [right[0][2], right[1][2], left[0][2], left[1][2]]
+    first, step2 = lax.optimization_barrier((first, step2))
+    carry = add(carry, 2, step2, 3)
+
     def terms(*distances):
         s = 0 if distances[0] in STAGES[0] else 1
         at = STAGES[s].index(distances[0]) + (heads // width if s == 0 else 0)
-        span = 8 if s == 0 else 1
+        span = 13 if s == 0 else 1
         return partial_grad((first, second)[s], first, heads, width, at, len(distances), span)
 
     half = width // 2
     middle, ahead, back = terms(4, 3, 5)
-    right, left = shift_z(middle[:half], 1), shift_z(middle[half:], -1)
+    up, down = shift_z(middle[:half], 1), shift_z(middle[half:], -1)
     states = [state, shift_core(state)]
-    right = jnp.concatenate([ahead[:half] + right, ahead[half:]])
-    left = jnp.concatenate([back[:half], back[half:] + left])
-    right, left, states = lax.optimization_barrier((right, left, states))
-    right, left = shift_z(right, 1), shift_z(left, -1)
-    ring_step(3, 1, right, left)
+    up = jnp.concatenate([ahead[:half] + up, ahead[half:]])
+    down = jnp.concatenate([back[:half], back[half:] + down])
+    up, down, states = lax.optimization_barrier((up, down, states))
+    up, down = shift_z(up, 1), shift_z(down, -1)
+    step3 = [None] * 4
+    step3[0] = shift_z(after(step2[0], up, down), 1)
+    step3[3] = shift_z(after(step2[3], up, down), -1)
     ahead, back = terms(2, 6)
-    right, left = ahead + right, back + left
+    up, down = ahead + up, back + down
     states += [shift_far(x) for x in states]
-    right, left = shift_z(right, 1), shift_z(left, -1)
-    second, states, _ = lax.optimization_barrier((second, states, carries[2][0]))
+    up, down = shift_z(up, 1), shift_z(down, -1)
+    second, states = lax.optimization_barrier((second, states))
     ahead, back, rest = terms(1, 7, 0)
-    right, left = ahead + right, back + left
-    right, left, ring[3] = lax.optimization_barrier((right, left, ring[3]))
-    right, left = shift_z(right, 1), shift_z(left, -1)
-    inner = local_weight.astype(F32) - inner_rate * (rest + right + left)
+    step3[1] = shift_z(after(step2[1], rest), 1)
+    step3[2] = shift_z(after(step2[2], rest), -1)
+    up, down = ahead + up, back + down
+    up, down, step3[0], step3[3] = lax.optimization_barrier((up, down, step3[0], step3[3]))
+    up, down = shift_z(up, 1), shift_z(down, -1)
+    up, down, step3, _ = lax.optimization_barrier((up, down, step3, carry[0]))
+    inner = local_weight.astype(F32) - inner_rate * (rest + up + down)
 
     near = inner + shift_core(inner)
     far = shift_far(near)
-    half = part // 2
-    right, left = shift_z(ring[3][0][:half], 1), shift_z(ring[3][1][half:], -1)
-    values, act_grad = project(tokens, grads_out, [right, left], places(4), carries[3], True)
+    step4 = [shift_z(step3[0], 1), shift_z(step3[3], -1)]
+    carry = add(carry, 3, step3)
+    values, act_grad = add(carry, 4, step4, last=True)
     new_weight, new_momentum = outer_step(
         plan, jnp.reshape(rank, (1,)).astype(jnp.int32), near, far, inner, states
     )

time: 165 us -> 159 us (0.964)
  waiting for transfers between devices: 60.3 us -> 44.7 us
  starting transfers between devices: 58.8 us -> 71.8 us
  local copies, waits for them, and re-layouts: 5 us -> 2.11 us
    ppermute x3 -> x6, waiting for transfers between devices: 9.61 us -> 0.26 us  [shift_y(): return lax.ppermute(x, 'y', [(i, (i + dy) % NY) for i in range(NY)])]
    ppermute x16 -> x22, waiting for transfers between devices: 38.7 us -> 31.6 us  [shift_z(): return lax.ppermute(x, 'z', [(i, (i + dz) % NZ) for i in range(NZ)])]
    ppermute x16 -> x22, starting transfers between devices: 25.9 us -> 32.4 us  [shift_z(): return lax.ppermute(x, 'z', [(i, (i + dz) % NZ) for i in range(NZ)])]
    ppermute x3 -> x6, starting transfers between devices: 4.65 us -> 8.66 us  [shift_y(): return lax.ppermute(x, 'y', [(i, (i + dy) % NY) for i in range(NY)])]
    slice x3 -> x1, local copies, waits for them, and re-layouts: 2.99 us -> 0.04 us  [local(): down = jnp.concatenate([back[:half], back[half:] + down])]
    all_to_all x1, starting transfers between devices: 4.65 us -> 7.07 us  [local(): first = lax.all_to_all(first, sub, 0, 0)]
    all_to_all x1, starting transfers between devices: 3.63 us -> 5.58 us  [local(): second = lax.all_to_all(after(second, first), sub, 0, 0)]
    all_to_all x1, waiting for transfers between devices: 1.71 us -> 3.62 us  [local(): second = lax.all_to_all(after(second, first), sub, 0, 0)]
  transfers between devices with their start and end apart: 27 -> 36, of which waited for: 14 -> 15; matrix products, arithmetic and copies ran while one was open for 3% -> 2% of each run, Pallas kernels for 21% -> 22%
where the time goes in v4:
time: 159 us; the launch traced here: 158 us
  starting transfers between devices  71.8 us (45%)
  waiting for transfers between devices  44.7 us (28%)
  Pallas kernels  36.1 us (23%)
  other arithmetic  2.19 us (1%)
  local copies, waits for them, and re-layouts  2.11 us (1%)
    ppermute x22, starting transfers between devices, shift_z(): return lax.ppermute(x, 'z', [(i, (i + dz) % NZ) for i in range(NZ)])  32.4 us
    ppermute x22, waiting for transfers between devices, shift_z(): return lax.ppermute(x, 'z', [(i, (i + dz) % NZ) for i in range(NZ)])  31.6 us
    pallas_call x5, Pallas kernels, project(): pl.pallas_call(functools.partial(project_kernel, sizes, first), in_specs=...  19.9 us
    ppermute x2, starting transfers between devices, shift_core(): return lax.ppermute(x, 'core', [(0, 1), (1, 0)])  10.4 us
    pallas_call x3, Pallas kernels, partial_grad(): pl.pallas_call(grad_kernel, grid=(count,), in_specs=[pl.BlockSpec((member...  9.65 us
    ppermute x6, starting transfers between devices, shift_y(): return lax.ppermute(x, 'y', [(i, (i + dy) % NY) for i in range(NY)])  8.66 us
    all_to_all x1, starting transfers between devices, local(): first = lax.all_to_all(first, sub, 0, 0)  7.07 us
    all_to_all x1, waiting for transfers between devices, local(): first = lax.all_to_all(first, sub, 0, 0)  6.8 us
  transfers between devices with their start and end apart: 36, of which 15 were waited for; matrix products, arithmetic and copies ran while one was open for 2% of the time, Pallas kernels for 22%

profile of v4, /device:TPU:1, one launch (start us, length us, event | category | flops | bytes accessed | tf_op | source)
XLA Modules:
  0.0 157.9 jit_solution(17996710166404931542)
XLA Ops:
  12.8 4.6 %sort_tokens.1 = (bf16[8,256,896]{2,1,0:T(8,128)(2,1)}, bf16[8,256,640]{2,1,0:T(8,128)(2,1)}) custom-call(s32[8]{0:T(128)S(1)} %stack.260.place_ref, bf16[256,8192]{1,0:T(8,128)(2,1)} %bitcast.124, bf16[256,512]{1,0:T(8,128)(2,1)} %bitcast.118), custom_call_target="tpu_custom_call" | custom-call | bytes 17825792 | tf_op jit(solution)/shard_map/sort_tokens/pallas_call | solution.py:87
  17.8 7.1 %all-to-all-start = ((bf16[8,256,896]{2,1,0:T(8,128)(2,1)}), bf16[8,256,896]{2,1,0:T(8,128)(2,1)}, u32[]{:S(2)}, u32[]{:S(2)}) async-start(bf16[8,256,896]{2,1,0:T(8,128)(2,1)} %get-tuple-element.54), calls=%async_computation | async-start | bytes 7340032 | tf_op jit(solution)/shard_map/all_to_all | solution.py:288
  32.2 2.7 %project.5 = (f32[256,512]{1,0:T(8,128)S(1)}, bf16[256,8192]{1,0:T(8,128)(2,1)}) custom-call(s32[8]{0:T(128)S(1)} %stack.286.place_ref, bf16[256,8192]{1,0:T(8,128)(2,1)} %bitcast.125, bf16[256,512]{1,0:T(8,128)(2,1)S(1)} %bitcast.119, bf16[512,512]{1,0:T(8,128)(2,1)S(1)} %pad_maximum_fusion.refs_0_, bf16[512,512]{1,0:T(8,128)(2,1)S(1)} %pad_maximum_fusion.1.refs_1_), custom_call_target="tpu_custom_call" | custom-call | flops 536870912 | bytes 2097152 | tf_op jit(solution)/shard_map/project/pallas_call | solution.py:201
  34.9 5.1 %collective-permute-done.7.refs_0_ = bf16[512,512]{1,0:T(8,128)(2,1)S(1)} collective-permute-done((bf16[512,512]{1,0:T(8,128)(2,1)S(1)}, bf16[512,512]{1,0:T(8,128)(2,1)S(1)}, u32[]{:S(2)}, u32[]{:S(2)}) %collective-permute-start.7) | collective-permute-done | bytes 524320 | tf_op jit(solution)/shard_map/ppermute | solution.py:24
  40.0 11.2 %collective-permute-done.8.refs_1_ = bf16[512,512]{1,0:T(8,128)(2,1)} collective-permute-done((bf16[512,512]{1,0:T(8,128)(2,1)S(1)}, bf16[512,512]{1,0:T(8,128)(2,1)}, u32[]{:S(2)}, u32[]{:S(2)}) %collective-permute-start.8) | collective-permute-done | bytes 524320 | tf_op jit(solution)/shard_map/ppermute | solution.py:24
  51.3 2.7 %collective-permute-start.13 = (bf16[512,512]{1,0:T(8,128)(2,1)}, bf16[512,512]{1,0:T(8,128)(2,1)}, u32[]{:S(2)}, u32[]{:S(2)}) collective-permute-start(bf16[512,512]{1,0:T(8,128)(2,1)} %collective-permute-done.9.refs_2_), channel_id=1, source_target_pairs={{0,7},{1,0},{2,1},{3,2},{4,3},{5,4},{6,5},{7,6},{8,15},{9,8},{10,9... | collective-permute-start | bytes 1572872 | tf_op jit(solution)/shard_map/ppermute | solution.py:24
  54.0 4.4 %project.6 = (f32[256,512]{1,0:T(8,128)S(1)}, bf16[256,8192]{1,0:T(8,128)(2,1)}) custom-call(s32[16]{0:T(128)S(1)} %stack.277.place_ref, bf16[256,8192]{1,0:T(8,128)(2,1)} %bitcast.126, bf16[256,512]{1,0:T(8,128)(2,1)S(1)} %bitcast.120, bf16[512,512]{1,0:T(8,128)(2,1)S(1)} %collective-permute-done.7.refs_0_, ...), custom_call_target="tpu_custom_call", output_to_operand_aliasing={{1}: (8, {})} | custom-call | flops 10737418240 | bytes 4194304 | tf_op jit(solution)/shard_map/project/pallas_call | solution.py:201
  59.3 6.8 %all-to-all-done.tokens_ref.grads_ref = bf16[8,256,896]{2,1,0:T(8,128)(2,1)} async-done(((bf16[8,256,896]{2,1,0:T(8,128)(2,1)}), bf16[8,256,896]{2,1,0:T(8,128)(2,1)}, u32[]{:S(2)}, u32[]{:S(2)}) %all-to-all-start) | async-done | bytes 3670048 | tf_op jit(solution)/shard_map/all_to_all | solution.py:288
  66.1 5.6 %all-to-all-start.1 = ((bf16[8,256,640]{2,1,0:T(8,128)(2,1)}), bf16[8,256,640]{2,1,0:T(8,128)(2,1)S(1)}, u32[]{:S(2)}, u32[]{:S(2)}) async-start(bf16[8,256,640]{2,1,0:T(8,128)(2,1)} %get-tuple-element.61), calls=%async_computation.1 | async-start | bytes 5242880 | tf_op jit(solution)/shard_map/all_to_all | solution.py:313
  73.8 3.8 %partial_grad.3 = f32[3,128,512]{2,1,0:T(8,128)S(1)} custom-call(bf16[8,256,896]{2,1,0:T(8,128)(2,1)} %all-to-all-done.tokens_ref.grads_ref, bf16[8,256,896]{2,1,0:T(8,128)(2,1)} %all-to-all-done.tokens_ref.grads_ref), custom_call_target="tpu_custom_call" | custom-call | flops 10468982784 | tf_op jit(solution)/shard_map/partial_grad/pallas_call | solution.py:120
  77.6 3.6 %collective-permute-start.16 = (f32[64,512]{1,0:T(8,128)S(1)}, f32[64,512]{1,0:T(8,128)S(1)}, u32[]{:S(2)}, u32[]{:S(2)}) collective-permute-start(f32[64,512]{1,0:T(8,128)S(1)} %get-tuple-element.103), channel_id=1, source_target_pairs={{0,7},{1,0},{2,1},{3,2},{4,3},{5,4},{6,5},{7,6},{8,15},{9,8},{10,9... | collective-permute-start | bytes 393224 | tf_op jit(solution)/shard_map/ppermute | solution.py:24
  81.3 4.1 %collective-permute-start.17 = (f32[2,128,128]{2,1,0:T(8,128)S(1)}, f32[2,128,128]{2,1,0:T(8,128)}, u32[]{:S(2)}, u32[]{:S(2)}) collective-permute-start(f32[2,128,128]{2,1,0:T(8,128)S(1)} %pad_maximum_fusion.4.refs_0_), channel_id=1, source_target_pairs={{0,64},{64,0},{1,65},{65,1},{2,66},{66,2},{3,67},{67,3},{4,68},{68... | collective-permute-start | bytes 393224 | tf_op jit(solution)/shard_map/ppermute | solution.py:36
  96.4 2.7 %collective-permute-start.25 = (bf16[512,512]{1,0:T(8,128)(2,1)}, bf16[512,512]{1,0:T(8,128)(2,1)}, u32[]{:S(2)}, u32[]{:S(2)}) collective-permute-start(bf16[512,512]{1,0:T(8,128)(2,1)} %collective-permute-done.14.refs_3_), channel_id=1, source_target_pairs={{0,7},{1,0},{2,1},{3,2},{4,3},{5,4},{6,5},{7,6},{8,15},{9,8},{10,9... | collective-permute-start | bytes 1572872 | tf_op jit(solution)/shard_map/ppermute | solution.py:24
  99.0 3.6 %all-to-all-done.1.tokens_ref = bf16[8,256,640]{2,1,0:T(8,128)(2,1)S(1)} async-done(((bf16[8,256,640]{2,1,0:T(8,128)(2,1)}), bf16[8,256,640]{2,1,0:T(8,128)(2,1)S(1)}, u32[]{:S(2)}, u32[]{:S(2)}) %all-to-all-start.1) | async-done | bytes 2621472 | tf_op jit(solution)/shard_map/all_to_all | solution.py:313
  106.4 5.7 %collective-permute-start.23 = (f32[128,512]{1,0:T(8,128)S(1)}, f32[128,512]{1,0:T(8,128)S(1)}, u32[]{:S(2)}, u32[]{:S(2)}) collective-permute-start(f32[128,512]{1,0:T(8,128)S(1)} %get-tuple-element.108), channel_id=1, source_target_pairs={{0,7},{1,0},{2,1},{3,2},{4,3},{5,4},{6,5},{7,6},{8,15},{9,8},{10,9... | collective-permute-start | bytes 786440 | tf_op jit(solution)/shard_map/ppermute | solution.py:24
  112.1 3.2 %partial_grad.4 = f32[3,128,512]{2,1,0:T(8,128)S(1)} custom-call(bf16[8,256,640]{2,1,0:T(8,128)(2,1)S(1)} %all-to-all-done.1.tokens_ref, bf16[8,256,896]{2,1,0:T(8,128)(2,1)} %all-to-all-done.tokens_ref.grads_ref), custom_call_target="tpu_custom_call" | custom-call | flops 805306368 | tf_op jit(solution)/shard_map/partial_grad/pallas_call | solution.py:120
  115.7 2.8 %collective-permute-start.29 = (bf16[512,512]{1,0:T(8,128)(2,1)}, bf16[512,512]{1,0:T(8,128)(2,1)S(1)}, u32[]{:S(2)}, u32[]{:S(2)}) collective-permute-start(bf16[512,512]{1,0:T(8,128)(2,1)} %collective-permute-done.13.refs_2_), channel_id=1, source_target_pairs={{0,7},{1,0},{2,1},{3,2},{4,3},{5,4},{6,5},{7,6},{8,15},{9,8},{10,9... | collective-permute-start | bytes 1572872 | tf_op jit(solution)/shard_map/ppermute | solution.py:24
  121.4 4.6 %project.7 = (f32[256,512]{1,0:T(8,128)S(1)}, bf16[256,8192]{1,0:T(8,128)(2,1)}) custom-call(s32[16]{0:T(128)S(1)} %stack.306.place_ref, bf16[256,8192]{1,0:T(8,128)(2,1)} %bitcast.127, bf16[256,512]{1,0:T(8,128)(2,1)S(1)} %bitcast.121, bf16[512,512]{1,0:T(8,128)(2,1)} %collective-permute-done.11.refs_0_, ...), custom_call_target="tpu_custom_call", output_to_operand_aliasing={{1}: (8, {})} | custom-call | flops 3221225472 | bytes 4194304 | tf_op jit(solution)/shard_map/project/pallas_call | solution.py:201
  126.0 3.2 %collective-permute-done.28.refs_1_ = bf16[512,512]{1,0:T(8,128)(2,1)S(1)} collective-permute-done((bf16[512,512]{1,0:T(8,128)(2,1)}, bf16[512,512]{1,0:T(8,128)(2,1)S(1)}, u32[]{:S(2)}, u32[]{:S(2)}) %collective-permute-start.28) | collective-permute-done | bytes 524320 | tf_op jit(solution)/shard_map/ppermute | solution.py:24
  129.2 5.6 %collective-permute-done.26 = f32[128,512]{1,0:T(8,128)S(1)} collective-permute-done((f32[128,512]{1,0:T(8,128)S(1)}, f32[128,512]{1,0:T(8,128)S(1)}, u32[]{:S(2)}, u32[]{:S(2)}) %collective-permute-start.26) | collective-permute-done | bytes 262176 | tf_op jit(solution)/shard_map/ppermute | solution.py:24
  134.8 2.7 %collective-permute-start.31 = (bf16[512,512]{1,0:T(8,128)(2,1)}, bf16[512,512]{1,0:T(8,128)(2,1)}, u32[]{:S(2)}, u32[]{:S(2)}) collective-permute-start(bf16[512,512]{1,0:T(8,128)(2,1)} %collective-permute-done.25.refs_3_), channel_id=1, source_target_pairs={{0,7},{1,0},{2,1},{3,2},{4,3},{5,4},{6,5},{7,6},{8,15},{9,8},{10,9... | collective-permute-start | bytes 1572872 | tf_op jit(solution)/shard_map/ppermute | solution.py:24
  137.6 6.3 %collective-permute-start.32 = (f32[128,512]{1,0:T(8,128)S(1)}, f32[128,512]{1,0:T(8,128)S(1)}, u32[]{:S(2)}, u32[]{:S(2)}) collective-permute-start(f32[128,512]{1,0:T(8,128)S(1)} %multiply_subtract_fusion.inner_ref), channel_id=1, source_target_pairs={{0,64},{64,0},{1,65},{65,1},{2,66},{66,2},{3,67},{67,3},{4,68},{68... | collective-permute-start | bytes 786440 | tf_op jit(solution)/shard_map/ppermute | solution.py:36
  147.8 4.1 %project.8 = (f32[256,512]{1,0:T(8,128)S(1)}, bf16[256,8192]{1,0:T(8,128)(2,1)}) custom-call(s32[16]{0:T(128)S(1)} %stack.323.place_ref, bf16[256,8192]{1,0:T(8,128)(2,1)} %bitcast.128, bf16[256,512]{1,0:T(8,128)(2,1)S(1)} %bitcast.122, bf16[512,512]{1,0:T(8,128)(2,1)S(1)} %collective-permute-done.24.refs_0_, ...), custom_call_target="tpu_custom_call", output_to_operand_aliasing={{1}: (8, {})} | custom-call | flops 1073741824 | bytes 4194304 | tf_op jit(solution)/shard_map/project/pallas_call | solution.py:201
  152.0 3.9 %project.9 = (bf16[256,512]{1,0:T(8,128)(2,1)}, bf16[256,8192]{1,0:T(8,128)(2,1)}) custom-call(s32[8]{0:T(128)S(1)} %stack.251.place_ref, bf16[256,8192]{1,0:T(8,128)(2,1)} %bitcast.129, bf16[256,512]{1,0:T(8,128)(2,1)S(1)} %bitcast.123, bf16[512,512]{1,0:T(8,128)(2,1)S(1)} %collective-permute-done.30.refs_0_, ...), custom_call_target="tpu_custom_call", output_to_operand_aliasing={{1}: (6, {})} | custom-call | flops 536870912 | bytes 2097152 | tf_op jit(solution)/shard_map/project/pallas_call | solution.py:201
  (94 shorter events, 46.7 us)
Async XLA Ops:
  5.3 12.1 %collective-permute-start.2 = (bf16[128,512]{1,0:T(8,128)(2,1)S(1)}, bf16[128,512]{1,0:T(8,128)(2,1)S(1)}, u32[]{:S(2)}, u32[]{:S(2)}) collective-permute-start(bf16[128,512]{1,0:T(8,128)(2,1)S(1)} %collective-permute-done), channel_id=1, source_target_pairs={{0,16},{16,32},{32,48},{48,0},{1,17},{17,33},{33,49},{49,1},{2,18}... | collective-permute-start | bytes 393224 | tf_op jit(solution)/shard_map/ppermute | solution.py:28
  7.4 10.1 %collective-permute-start.5 = (bf16[128,512]{1,0:T(8,128)(2,1)}, bf16[128,512]{1,0:T(8,128)(2,1)S(1)}, u32[]{:S(2)}, u32[]{:S(2)}) collective-permute-start(bf16[128,512]{1,0:T(8,128)(2,1)} %bitcast.133), channel_id=1, source_target_pairs={{0,48},{16,0},{32,16},{48,32},{1,49},{17,1},{33,17},{49,33},{2,50}... | collective-permute-start | bytes 393224 | tf_op jit(solution)/shard_map/ppermute | solution.py:28
  17.8 48.3 %all-to-all-start = ((bf16[8,256,896]{2,1,0:T(8,128)(2,1)}), bf16[8,256,896]{2,1,0:T(8,128)(2,1)}, u32[]{:S(2)}, u32[]{:S(2)}) async-start(bf16[8,256,896]{2,1,0:T(8,128)(2,1)} %get-tuple-element.54), calls=%async_computation | async-start | bytes 7340032 | tf_op jit(solution)/shard_map/all_to_all | solution.py:288
  24.9 15.2 %collective-permute-start.7 = (bf16[512,512]{1,0:T(8,128)(2,1)S(1)}, bf16[512,512]{1,0:T(8,128)(2,1)S(1)}, u32[]{:S(2)}, u32[]{:S(2)}) collective-permute-start(bf16[512,512]{1,0:T(8,128)(2,1)S(1)} %pad_maximum_fusion.refs_0_), channel_id=1, source_target_pairs={{0,1},{1,2},{2,3},{3,4},{4,5},{5,6},{6,7},{7,0},{8,9},{9,10},{10,1... | collective-permute-start | bytes 1572872 | tf_op jit(solution)/shard_map/ppermute | solution.py:24
  26.5 24.8 %collective-permute-start.8 = (bf16[512,512]{1,0:T(8,128)(2,1)S(1)}, bf16[512,512]{1,0:T(8,128)(2,1)}, u32[]{:S(2)}, u32[]{:S(2)}) collective-permute-start(bf16[512,512]{1,0:T(8,128)(2,1)S(1)} %pad_maximum_fusion.1.refs_1_), channel_id=1, source_target_pairs={{0,1},{1,2},{2,3},{3,4},{4,5},{5,6},{6,7},{7,0},{8,9},{9,10},{10,1... | collective-permute-start | bytes 1572872 | tf_op jit(solution)/shard_map/ppermute | solution.py:24
  28.1 23.1 %collective-permute-start.9 = (bf16[512,512]{1,0:T(8,128)(2,1)S(1)}, bf16[512,512]{1,0:T(8,128)(2,1)}, u32[]{:S(2)}, u32[]{:S(2)}) collective-permute-start(bf16[512,512]{1,0:T(8,128)(2,1)S(1)} %pad_maximum_fusion.refs_0_), channel_id=1, source_target_pairs={{0,7},{1,0},{2,1},{3,2},{4,3},{5,4},{6,5},{7,6},{8,15},{9,8},{10,9... | collective-permute-start | bytes 1572872 | tf_op jit(solution)/shard_map/ppermute | solution.py:24
  30.6 23.3 %collective-permute-start.10 = (bf16[512,512]{1,0:T(8,128)(2,1)S(1)}, bf16[512,512]{1,0:T(8,128)(2,1)}, u32[]{:S(2)}, u32[]{:S(2)}) collective-permute-start(bf16[512,512]{1,0:T(8,128)(2,1)S(1)} %pad_maximum_fusion.1.refs_1_), channel_id=1, source_target_pairs={{0,7},{1,0},{2,1},{3,2},{4,3},{5,4},{6,5},{7,6},{8,15},{9,8},{10,9... | collective-permute-start | bytes 1572872 | tf_op jit(solution)/shard_map/ppermute | solution.py:24
  40.0 31.7 %collective-permute-start.11 = (bf16[512,512]{1,0:T(8,128)(2,1)S(1)}, bf16[512,512]{1,0:T(8,128)(2,1)}, u32[]{:S(2)}, u32[]{:S(2)}) collective-permute-start(bf16[512,512]{1,0:T(8,128)(2,1)S(1)} %collective-permute-done.7.refs_0_), channel_id=1, source_target_pairs={{0,1},{1,2},{2,3},{3,4},{4,5},{5,6},{6,7},{7,0},{8,9},{9,10},{10,1... | collective-permute-start | bytes 1572872 | tf_op jit(solution)/shard_map/ppermute | solution.py:24
  51.3 22.5 %collective-permute-start.12 = (bf16[512,512]{1,0:T(8,128)(2,1)}, bf16[512,512]{1,0:T(8,128)(2,1)}, u32[]{:S(2)}, u32[]{:S(2)}) collective-permute-start(bf16[512,512]{1,0:T(8,128)(2,1)} %collective-permute-done.8.refs_1_), channel_id=1, source_target_pairs={{0,1},{1,2},{2,3},{3,4},{4,5},{5,6},{6,7},{7,0},{8,9},{9,10},{10,1... | collective-permute-start | bytes 1572872 | tf_op jit(solution)/shard_map/ppermute | solution.py:24
  51.3 22.5 %collective-permute-start.13 = (bf16[512,512]{1,0:T(8,128)(2,1)}, bf16[512,512]{1,0:T(8,128)(2,1)}, u32[]{:S(2)}, u32[]{:S(2)}) collective-permute-start(bf16[512,512]{1,0:T(8,128)(2,1)} %collective-permute-done.9.refs_2_), channel_id=1, source_target_pairs={{0,7},{1,0},{2,1},{3,2},{4,3},{5,4},{6,5},{7,6},{8,15},{9,8},{10,9... | collective-permute-start | bytes 1572872 | tf_op jit(solution)/shard_map/ppermute | solution.py:24
  54.0 19.8 %collective-permute-start.14 = (bf16[512,512]{1,0:T(8,128)(2,1)}, bf16[512,512]{1,0:T(8,128)(2,1)}, u32[]{:S(2)}, u32[]{:S(2)}) collective-permute-start(bf16[512,512]{1,0:T(8,128)(2,1)} %collective-permute-done.10.refs_3_), channel_id=1, source_target_pairs={{0,7},{1,0},{2,1},{3,2},{4,3},{5,4},{6,5},{7,6},{8,15},{9,8},{10,9... | collective-permute-start | bytes 1572872 | tf_op jit(solution)/shard_map/ppermute | solution.py:24
  66.1 36.6 %all-to-all-start.1 = ((bf16[8,256,640]{2,1,0:T(8,128)(2,1)}), bf16[8,256,640]{2,1,0:T(8,128)(2,1)S(1)}, u32[]{:S(2)}, u32[]{:S(2)}) async-start(bf16[8,256,640]{2,1,0:T(8,128)(2,1)} %get-tuple-element.61), calls=%async_computation.1 | async-start | bytes 5242880 | tf_op jit(solution)/shard_map/all_to_all | solution.py:313
  89.5 22.5 %collective-permute-start.18 = (f32[2,128,128]{2,1,0:T(8,128)S(1)}, f32[2,128,128]{2,1,0:T(8,128)}, u32[]{:S(2)}, u32[]{:S(2)}) collective-permute-start(f32[2,128,128]{2,1,0:T(8,128)S(1)} %pad_maximum_fusion.4.refs_0_), channel_id=1, source_target_pairs={{0,128},{128,0},{1,129},{129,1},{2,130},{130,2},{3,131},{131,3},{4... | collective-permute-start | bytes 393224 | tf_op jit(solution)/shard_map/ppermute | solution.py:40
  92.1 19.9 %collective-permute-start.19 = (f32[2,128,128]{2,1,0:T(8,128)}, f32[2,128,128]{2,1,0:T(8,128)}, u32[]{:S(2)}, u32[]{:S(2)}) collective-permute-start(f32[2,128,128]{2,1,0:T(8,128)} %collective-permute-done.17.refs_1_), channel_id=1, source_target_pairs={{0,128},{128,0},{1,129},{129,1},{2,130},{130,2},{3,131},{131,3},{4... | collective-permute-start | bytes 393224 | tf_op jit(solution)/shard_map/ppermute | solution.py:40
  96.4 22.3 %collective-permute-start.24 = (bf16[512,512]{1,0:T(8,128)(2,1)}, bf16[512,512]{1,0:T(8,128)(2,1)S(1)}, u32[]{:S(2)}, u32[]{:S(2)}) collective-permute-start(bf16[512,512]{1,0:T(8,128)(2,1)} %collective-permute-done.11.refs_0_), channel_id=1, source_target_pairs={{0,1},{1,2},{2,3},{3,4},{4,5},{5,6},{6,7},{7,0},{8,9},{9,10},{10,1... | collective-permute-start | bytes 1572872 | tf_op jit(solution)/shard_map/ppermute | solution.py:24
  96.4 22.3 %collective-permute-start.25 = (bf16[512,512]{1,0:T(8,128)(2,1)}, bf16[512,512]{1,0:T(8,128)(2,1)}, u32[]{:S(2)}, u32[]{:S(2)}) collective-permute-start(bf16[512,512]{1,0:T(8,128)(2,1)} %collective-permute-done.14.refs_3_), channel_id=1, source_target_pairs={{0,7},{1,0},{2,1},{3,2},{4,3},{5,4},{6,5},{7,6},{8,15},{9,8},{10,9... | collective-permute-start | bytes 1572872 | tf_op jit(solution)/shard_map/ppermute | solution.py:24
  106.4 9.3 %collective-permute-start.23 = (f32[128,512]{1,0:T(8,128)S(1)}, f32[128,512]{1,0:T(8,128)S(1)}, u32[]{:S(2)}, u32[]{:S(2)}) collective-permute-start(f32[128,512]{1,0:T(8,128)S(1)} %get-tuple-element.108), channel_id=1, source_target_pairs={{0,7},{1,0},{2,1},{3,2},{4,3},{5,4},{6,5},{7,6},{8,15},{9,8},{10,9... | collective-permute-start | bytes 786440 | tf_op jit(solution)/shard_map/ppermute | solution.py:24
  115.3 13.9 %collective-permute-start.28 = (bf16[512,512]{1,0:T(8,128)(2,1)}, bf16[512,512]{1,0:T(8,128)(2,1)S(1)}, u32[]{:S(2)}, u32[]{:S(2)}) collective-permute-start(bf16[512,512]{1,0:T(8,128)(2,1)} %collective-permute-done.12.refs_1_), channel_id=1, source_target_pairs={{0,1},{1,2},{2,3},{3,4},{4,5},{5,6},{6,7},{7,0},{8,9},{9,10},{10,1... | collective-permute-start | bytes 1572872 | tf_op jit(solution)/shard_map/ppermute | solution.py:24
  115.7 13.5 %collective-permute-start.29 = (bf16[512,512]{1,0:T(8,128)(2,1)}, bf16[512,512]{1,0:T(8,128)(2,1)S(1)}, u32[]{:S(2)}, u32[]{:S(2)}) collective-permute-start(bf16[512,512]{1,0:T(8,128)(2,1)} %collective-permute-done.13.refs_2_), channel_id=1, source_target_pairs={{0,7},{1,0},{2,1},{3,2},{4,3},{5,4},{6,5},{7,6},{8,15},{9,8},{10,9... | collective-permute-start | bytes 1572872 | tf_op jit(solution)/shard_map/ppermute | solution.py:24
  118.6 16.2 %collective-permute-start.26 = (f32[128,512]{1,0:T(8,128)S(1)}, f32[128,512]{1,0:T(8,128)S(1)}, u32[]{:S(2)}, u32[]{:S(2)}) collective-permute-start(f32[128,512]{1,0:T(8,128)S(1)} %get-tuple-element.73), channel_id=1, source_target_pairs={{0,1},{1,2},{2,3},{3,4},{4,5},{5,6},{6,7},{7,0},{8,9},{9,10},{10,1... | collective-permute-start | bytes 786440 | tf_op jit(solution)/shard_map/ppermute | solution.py:24
  118.7 16.1 %collective-permute-start.27 = (f32[128,512]{1,0:T(8,128)S(1)}, f32[128,512]{1,0:T(8,128)S(1)}, u32[]{:S(2)}, u32[]{:S(2)}) collective-permute-start(f32[128,512]{1,0:T(8,128)S(1)} %get-tuple-element.74), channel_id=1, source_target_pairs={{0,7},{1,0},{2,1},{3,2},{4,3},{5,4},{6,5},{7,6},{8,15},{9,8},{10,9... | collective-permute-start | bytes 786440 | tf_op jit(solution)/shard_map/ppermute | solution.py:24
  134.8 17.1 %collective-permute-start.30 = (bf16[512,512]{1,0:T(8,128)(2,1)S(1)}, bf16[512,512]{1,0:T(8,128)(2,1)S(1)}, u32[]{:S(2)}, u32[]{:S(2)}) collective-permute-start(bf16[512,512]{1,0:T(8,128)(2,1)S(1)} %collective-permute-done.24.refs_0_), channel_id=1, source_target_pairs={{0,1},{1,2},{2,3},{3,4},{4,5},{5,6},{6,7},{7,0},{8,9},{9,10},{10,1... | collective-permute-start | bytes 1572872 | tf_op jit(solution)/shard_map/ppermute | solution.py:24
  134.8 17.1 %collective-permute-start.31 = (bf16[512,512]{1,0:T(8,128)(2,1)}, bf16[512,512]{1,0:T(8,128)(2,1)}, u32[]{:S(2)}, u32[]{:S(2)}) collective-permute-start(bf16[512,512]{1,0:T(8,128)(2,1)} %collective-permute-done.25.refs_3_), channel_id=1, source_target_pairs={{0,7},{1,0},{2,1},{3,2},{4,3},{5,4},{6,5},{7,6},{8,15},{9,8},{10,9... | collective-permute-start | bytes 1572872 | tf_op jit(solution)/shard_map/ppermute | solution.py:24
  145.1 10.8 %collective-permute-start.33 = (f32[128,512]{1,0:T(8,128)S(1)}, f32[128,512]{1,0:T(8,128)}, u32[]{:S(2)}, u32[]{:S(2)}) collective-permute-start(f32[128,512]{1,0:T(8,128)S(1)} %add.613.near_ref), channel_id=1, source_target_pairs={{0,128},{128,0},{1,129},{129,1},{2,130},{130,2},{3,131},{131,3},{4... | collective-permute-start | bytes 786440 | tf_op jit(solution)/shard_map/ppermute | solution.py:40
  (22 other events, 165.7 us)

commit v5 on v4

--- a/solution.py
+++ b/solution.py
@@ -17,7 +17,7 @@
 HBM = pl.BlockSpec(memory_space=pltpu.HBM)
 F32 = jnp.float32
 BF16 = jnp.bfloat16
-STAGES = ((4, 3, 5), (2, 6, 1, 7, 0))
+STAGES = ((4, 3, 5, 2, 6), (1, 7, 0))
 
 
 def shift_z(x, dz):
@@ -96,7 +96,7 @@
             pltpu.SemaphoreType.DMA((SUB + 1,)),
             pltpu.SemaphoreType.DMA((len(sizes), SUB)),
         ],
-        compiler_params=pltpu.CompilerParams(vmem_limit_bytes=14 << 20),
+        compiler_params=pltpu.CompilerParams(vmem_limit_bytes=12 << 20),
         cost_estimate=pl.CostEstimate(
             flops=0, bytes_accessed=8 * rows * (depth + heads), transcendentals=0
         ),
@@ -126,7 +126,7 @@
         ],
         out_specs=pl.BlockSpec((1, width, heads), lambda d: (d, 0, 0)),
         out_shape=jax.ShapeDtypeStruct((count, width, heads), F32),
-        compiler_params=pltpu.CompilerParams(vmem_limit_bytes=10 << 20),
+        compiler_params=pltpu.CompilerParams(vmem_limit_bytes=8 << 20),
         cost_estimate=pl.CostEstimate(
             flops=span * 2 * members * rows * count * width * heads,
             bytes_accessed=0,
@@ -215,7 +215,7 @@
             pltpu.SemaphoreType.DMA((count,)),
         ],
         input_output_aliases={} if first else {n_in + 1: 1},
-        compiler_params=pltpu.CompilerParams(vmem_limit_bytes=14 << 20),
+        compiler_params=pltpu.CompilerParams(vmem_limit_bytes=10 << 20),
         cost_estimate=pl.CostEstimate(
             flops=span * 4 * rows * heads * count * width,
             bytes_accessed=count * width * (rows * 4 + heads * 2),
@@ -227,12 +227,12 @@
 
 def outer_kernel(plan_ref, rank_ref, near_ref, far_ref, inner_ref, *refs):
     states, (new_ref, mom_ref) = refs[:-2], refs[-2:]
-    groups, width = len(states), mom_ref.shape[1]
+    groups, width = 2 * len(states), mom_ref.shape[1]
     rank = rank_ref[0]
     for b in range(groups):
         head = b ^ rank
         columns = pl.ds(pl.multiple_of(head * width, width), width)
-        anchor, momentum = states[b][0], states[b][1]
+        anchor, momentum = states[b // 2][b % 2, 0], states[b // 2][b % 2, 1]
         mean = (near_ref[:, columns] + far_ref[:, columns]) / groups
         pseudo = anchor - mean
         following = momentum_coef * momentum + pseudo
@@ -252,7 +252,7 @@
         out_specs=(whole, whole),
         out_shape=(
             jax.ShapeDtypeStruct(inner.shape, BF16),
-            jax.ShapeDtypeStruct(state[0].shape[1:], F32),
+            jax.ShapeDtypeStruct(state[0].shape[2:], F32),
         ),
         compiler_params=pltpu.CompilerParams(vmem_limit_bytes=4 << 20),
         name="outer_step",
@@ -298,62 +298,55 @@
         at = places(k) if k in (0, 4) else places(-k, k)
         return project(tokens, grads_out, pieces, at, carry, last, span)
 
-    right, left = (
-        [[block[h]] for h in range(2)],
-        [[block[h]] for h in range(2)],
-    )
+    right, left = ([[w] for w in block] for _ in range(2))
     carry = add(None, 0, block)
     for k in (1, 2):
         for h in range(2):
             right[h].append(shift_z(right[h][-1], 1))
             left[h].append(shift_z(left[h][-1], -1))
-    carry = add(carry, 1, [right[0][1], right[1][1], left[0][1], left[1][1]], 10)
-
-    first, _ = lax.optimization_barrier((first, carry[0]))
+        pieces = [right[0][k], right[1][k], left[0][k], left[1][k]]
+        if k == 1:
+            carry = add(carry, 1, pieces, 5)
+    step3 = [None] * 4
+    step3[0], step3[3] = shift_z(pieces[0], 1), shift_z(pieces[3], -1)
+    first, _, pieces = lax.optimization_barrier((first, carry[0], pieces))
     second = lax.all_to_all(after(second, first), sub, 0, 0)
-    state = after(jnp.stack([anchor, momentum]), first)
-    step2 = [right[0][2], right[1][2], left[0][2], left[1][2]]
-    first, step2 = lax.optimization_barrier((first, step2))
-    carry = add(carry, 2, step2, 3)
-
-    def terms(*distances):
+
+    def terms(tokens, span, *distances):
         s = 0 if distances[0] in STAGES[0] else 1
         at = STAGES[s].index(distances[0]) + (heads // width if s == 0 else 0)
-        span = 13 if s == 0 else 1
-        return partial_grad((first, second)[s], first, heads, width, at, len(distances), span)
+        return partial_grad(tokens, first, heads, width, at, len(distances), span)
 
     half = width // 2
-    middle, ahead, back = terms(4, 3, 5)
+    middle, ahead, back = terms(first, 5, 4, 3, 5)
     up, down = shift_z(middle[:half], 1), shift_z(middle[half:], -1)
-    states = [state, shift_core(state)]
+    state = after(jnp.stack([anchor, momentum]), middle)
+    states = jnp.stack([state, shift_core(state)])
     up = jnp.concatenate([ahead[:half] + up, ahead[half:]])
     down = jnp.concatenate([back[:half], back[half:] + down])
-    up, down, states = lax.optimization_barrier((up, down, states))
+    up, down, states, step3 = lax.optimization_barrier((up, down, states, step3))
+    step3[1] = shift_z(after(pieces[1], up), 1)
+    step3[2] = shift_z(after(pieces[2], down), -1)
+    ahead, back = terms(after(first, up, down), 5, 2, 6)
     up, down = shift_z(up, 1), shift_z(down, -1)
-    step3 = [None] * 4
-    step3[0] = shift_z(after(step2[0], up, down), 1)
-    step3[3] = shift_z(after(step2[3], up, down), -1)
-    ahead, back = terms(2, 6)
     up, down = ahead + up, back + down
-    states += [shift_far(x) for x in states]
+    distant = shift_far(after(states, up))
+    nearest = terms(second, 5, 1, 7, 0)
     up, down = shift_z(up, 1), shift_z(down, -1)
-    second, states = lax.optimization_barrier((second, states))
-    ahead, back, rest = terms(1, 7, 0)
-    step3[1] = shift_z(after(step2[1], rest), 1)
-    step3[2] = shift_z(after(step2[2], rest), -1)
-    up, down = ahead + up, back + down
-    up, down, step3[0], step3[3] = lax.optimization_barrier((up, down, step3[0], step3[3]))
+    up, down = nearest[0] + up, nearest[1] + down
+    up, down, distant, step3 = lax.optimization_barrier((up, down, distant, step3))
     up, down = shift_z(up, 1), shift_z(down, -1)
-    up, down, step3, _ = lax.optimization_barrier((up, down, step3, carry[0]))
-    inner = local_weight.astype(F32) - inner_rate * (rest + up + down)
+    step4 = [shift_z(step3[0], 1), shift_z(step3[3], -1)]
+    carry = add(carry, 2, pieces, 3)
+    up, down, _ = lax.optimization_barrier((up, down, carry[0]))
+    inner = local_weight.astype(F32) - inner_rate * (nearest[2] + up + down)
+    carry = add(carry, 3, step3)
 
     near = inner + shift_core(inner)
     far = shift_far(near)
-    step4 = [shift_z(step3[0], 1), shift_z(step3[3], -1)]
-    carry = add(carry, 3, step3)
     values, act_grad = add(carry, 4, step4, last=True)
     new_weight, new_momentum = outer_step(
-        plan, jnp.reshape(rank, (1,)).astype(jnp.int32), near, far, inner, states
+        plan, jnp.reshape(rank, (1,)).astype(jnp.int32), near, far, inner, [states, distant]
     )
     return values[None], act_grad[None], new_weight[None], new_momentum
 

time: 159 us -> 154 us (0.969)
  waiting for transfers between devices: 44.7 us -> 39.8 us
  starting transfers between devices: 71.8 us -> 68.8 us
  other arithmetic: 2.19 us -> 4.94 us
    all_to_all x1, waiting for transfers between devices: 6.8 us -> 2.77 us  [local(): first = lax.all_to_all(first, sub, 0, 0)]
    all_to_all x1, waiting for transfers between devices: 3.62 us -> 0.01 us  [local(): second = lax.all_to_all(after(second, first), sub, 0, 0)]
    ppermute x22, waiting for transfers between devices: 31.6 us -> 34.4 us  [shift_z(): return lax.ppermute(x, 'z', [(i, (i + dz) % NZ) for i in range(NZ)])]
    ppermute x3 -> x2, starting transfers between devices: 5.59 us -> 5.01 us  [shift_far(): return lax.ppermute(x, 'xh', [(0, 1), (1, 0)])]
  transfers between devices with their start and end apart: 36 -> 35, of which waited for: 15 -> 14; matrix products, arithmetic and copies ran while one was open for 2% -> 4% of each run, Pallas kernels for 22% -> 22%
where the time goes in v5:
time: 154 us; the launch traced here: 152 us
  starting transfers between devices  68.8 us (45%)
  waiting for transfers between devices  39.8 us (26%)
  Pallas kernels  35.8 us (23%)
  other arithmetic  4.94 us (3%)
  local copies, waits for them, and re-layouts  2.21 us (1%)
    ppermute x22, waiting for transfers between devices, shift_z(): return lax.ppermute(x, 'z', [(i, (i + dz) % NZ) for i in range(NZ)])  34.4 us
    ppermute x22, starting transfers between devices, shift_z(): return lax.ppermute(x, 'z', [(i, (i + dz) % NZ) for i in range(NZ)])  30.9 us
    pallas_call x5, Pallas kernels, project(): pl.pallas_call(functools.partial(project_kernel, sizes, first), in_specs=...  19.6 us
    pallas_call x3, Pallas kernels, partial_grad(): pl.pallas_call(grad_kernel, grid=(count,), in_specs=[pl.BlockSpec((member...  9.8 us
    ppermute x2, starting transfers between devices, shift_core(): return lax.ppermute(x, 'core', [(0, 1), (1, 0)])  9.33 us
    ppermute x6, starting transfers between devices, shift_y(): return lax.ppermute(x, 'y', [(i, (i + dy) % NY) for i in range(NY)])  8.66 us
    all_to_all x1, starting transfers between devices, local(): first = lax.all_to_all(first, sub, 0, 0)  7.2 us
    all_to_all x1, starting transfers between devices, local(): second = lax.all_to_all(after(second, first), sub, 0, 0)  5.58 us
  transfers between devices with their start and end apart: 35, of which 14 were waited for; matrix products, arithmetic and copies ran while one was open for 4% of the time, Pallas kernels for 22%

profile of v5, /device:TPU:1, one launch (start us, length us, event | category | flops | bytes accessed | tf_op | source)
XLA Modules:
  0.0 152.5 jit_solution(7456225749973016873)
XLA Ops:
  12.8 4.7 %sort_tokens.1 = (bf16[8,256,1152]{2,1,0:T(8,128)(2,1)}, bf16[8,256,384]{2,1,0:T(8,128)(2,1)}) custom-call(s32[8]{0:T(128)S(1)} %stack.269.place_ref, bf16[256,8192]{1,0:T(8,128)(2,1)} %bitcast.132, bf16[256,512]{1,0:T(8,128)(2,1)} %bitcast.126), custom_call_target="tpu_custom_call" | custom-call | bytes 17825792 | tf_op jit(solution)/shard_map/sort_tokens/pallas_call | solution.py:87
  17.8 7.2 %all-to-all-start = ((bf16[8,256,1152]{2,1,0:T(8,128)(2,1)}), bf16[8,256,1152]{2,1,0:T(8,128)(2,1)}, u32[]{:S(2)}, u32[]{:S(2)}) async-start(bf16[8,256,1152]{2,1,0:T(8,128)(2,1)} %get-tuple-element.47), calls=%async_computation | async-start | bytes 9437184 | tf_op jit(solution)/shard_map/all_to_all | solution.py:288
  32.2 3.7 %collective-permute-start.17 = (f32[2,128,128]{2,1,0:T(8,128)S(1)}, f32[2,128,128]{2,1,0:T(8,128)}, u32[]{:S(2)}, u32[]{:S(2)}) collective-permute-start(f32[2,128,128]{2,1,0:T(8,128)S(1)} %pad_maximum_fusion.5), channel_id=1, source_target_pairs={{0,64},{64,0},{1,65},{65,1},{2,66},{66,2},{3,67},{67,3},{4,68},{68... | collective-permute-start | bytes 393224 | tf_op jit(solution)/shard_map/ppermute | solution.py:36
  36.0 4.2 %collective-permute-done.7.refs_0_ = bf16[512,512]{1,0:T(8,128)(2,1)S(1)} collective-permute-done((bf16[512,512]{1,0:T(8,128)(2,1)S(1)}, bf16[512,512]{1,0:T(8,128)(2,1)S(1)}, u32[]{:S(2)}, u32[]{:S(2)}) %collective-permute-start.7) | collective-permute-done | bytes 524320 | tf_op jit(solution)/shard_map/ppermute | solution.py:24
  40.2 11.2 %collective-permute-done.8.refs_1_ = bf16[512,512]{1,0:T(8,128)(2,1)S(1)} collective-permute-done((bf16[512,512]{1,0:T(8,128)(2,1)S(1)}, bf16[512,512]{1,0:T(8,128)(2,1)S(1)}, u32[]{:S(2)}, u32[]{:S(2)}) %collective-permute-start.8) | collective-permute-done | bytes 524320 | tf_op jit(solution)/shard_map/ppermute | solution.py:24
  51.5 2.7 %collective-permute-start.13 = (bf16[512,512]{1,0:T(8,128)(2,1)}, bf16[512,512]{1,0:T(8,128)(2,1)}, u32[]{:S(2)}, u32[]{:S(2)}) collective-permute-start(bf16[512,512]{1,0:T(8,128)(2,1)} %collective-permute-done.9.refs_2_), channel_id=1, source_target_pairs={{0,7},{1,0},{2,1},{3,2},{4,3},{5,4},{6,5},{7,6},{8,15},{9,8},{10,9... | collective-permute-start | bytes 1572872 | tf_op jit(solution)/shard_map/ppermute | solution.py:24
  54.2 2.7 %project.5 = (f32[256,512]{1,0:T(8,128)S(1)}, bf16[256,8192]{1,0:T(8,128)(2,1)}) custom-call(s32[8]{0:T(128)S(1)} %stack.295.place_ref, bf16[256,8192]{1,0:T(8,128)(2,1)} %bitcast.133, bf16[256,512]{1,0:T(8,128)(2,1)S(1)} %bitcast.127, bf16[512,512]{1,0:T(8,128)(2,1)S(1)} %pad_maximum_fusion.refs_0_, bf16[512,512]{1,0:T(8,128)(2,1)S(1)} %pad_maximum_fusion.1.refs_1_), custom_call_target="tpu_custom_call" | custom-call | flops 536870912 | bytes 2097152 | tf_op jit(solution)/shard_map/project/pallas_call | solution.py:201
  56.9 4.1 %project.6 = (f32[256,512]{1,0:T(8,128)S(1)}, bf16[256,8192]{1,0:T(8,128)(2,1)}) custom-call(s32[16]{0:T(128)S(1)} %stack.286.place_ref, bf16[256,8192]{1,0:T(8,128)(2,1)} %bitcast.134, bf16[256,512]{1,0:T(8,128)(2,1)S(1)} %bitcast.128, bf16[512,512]{1,0:T(8,128)(2,1)S(1)} %collective-permute-done.7.refs_0_, ...), custom_call_target="tpu_custom_call", output_to_operand_aliasing={{1}: (8, {})} | custom-call | flops 5368709120 | bytes 4194304 | tf_op jit(solution)/shard_map/project/pallas_call | solution.py:201
  63.3 7.0 %collective-permute-done.14.refs_3_ = bf16[512,512]{1,0:T(8,128)(2,1)} collective-permute-done((bf16[512,512]{1,0:T(8,128)(2,1)S(1)}, bf16[512,512]{1,0:T(8,128)(2,1)}, u32[]{:S(2)}, u32[]{:S(2)}) %collective-permute-start.14) | collective-permute-done | bytes 524320 | tf_op jit(solution)/shard_map/ppermute | solution.py:24
  70.2 3.5 %collective-permute-start.19 = (bf16[512,512]{1,0:T(8,128)(2,1)}, bf16[512,512]{1,0:T(8,128)(2,1)S(1)}, u32[]{:S(2)}, u32[]{:S(2)}) collective-permute-start(bf16[512,512]{1,0:T(8,128)(2,1)} %collective-permute-done.14.refs_3_), channel_id=1, source_target_pairs={{0,7},{1,0},{2,1},{3,2},{4,3},{5,4},{6,5},{7,6},{8,15},{9,8},{10,9... | collective-permute-start | bytes 1572872 | tf_op jit(solution)/shard_map/ppermute | solution.py:24
  74.7 2.8 %all-to-all-done.grads_ref.tokens_ref = bf16[8,256,1152]{2,1,0:T(8,128)(2,1)} async-done(((bf16[8,256,1152]{2,1,0:T(8,128)(2,1)}), bf16[8,256,1152]{2,1,0:T(8,128)(2,1)}, u32[]{:S(2)}, u32[]{:S(2)}) %all-to-all-start) | async-done | bytes 4718624 | tf_op jit(solution)/shard_map/all_to_all | solution.py:288
  77.5 5.6 %all-to-all-start.1 = ((bf16[8,256,384]{2,1,0:T(8,128)(2,1)}), bf16[8,256,384]{2,1,0:T(8,128)(2,1)S(1)}, u32[]{:S(2)}, u32[]{:S(2)}) async-start(bf16[8,256,384]{2,1,0:T(8,128)(2,1)} %get-tuple-element.54), calls=%async_computation.1 | async-start | bytes 3145728 | tf_op jit(solution)/shard_map/all_to_all | solution.py:313
  83.1 3.8 %partial_grad.4 = f32[3,128,512]{2,1,0:T(8,128)S(1)} custom-call(bf16[8,256,1152]{2,1,0:T(8,128)(2,1)} %all-to-all-done.grads_ref.tokens_ref, bf16[8,256,1152]{2,1,0:T(8,128)(2,1)} %all-to-all-done.grads_ref.tokens_ref), custom_call_target="tpu_custom_call" | custom-call | flops 4026531840 | tf_op jit(solution)/shard_map/partial_grad/pallas_call | solution.py:120
  86.9 5.7 %collective-permute-start.16 = (f32[64,512]{1,0:T(8,128)S(1)}, f32[64,512]{1,0:T(8,128)S(1)}, u32[]{:S(2)}, u32[]{:S(2)}) collective-permute-start(f32[64,512]{1,0:T(8,128)S(1)} %get-tuple-element.89), channel_id=1, source_target_pairs={{0,7},{1,0},{2,1},{3,2},{4,3},{5,4},{6,5},{7,6},{8,15},{9,8},{10,9... | collective-permute-start | bytes 393224 | tf_op jit(solution)/shard_map/ppermute | solution.py:24
  94.5 3.4 %collective-permute-done.15 = f32[64,512]{1,0:T(8,128)S(1)} collective-permute-done((f32[64,512]{1,0:T(8,128)S(1)}, f32[64,512]{1,0:T(8,128)S(1)}, u32[]{:S(2)}, u32[]{:S(2)}) %collective-permute-start.15) | collective-permute-done | bytes 131104 | tf_op jit(solution)/shard_map/ppermute | solution.py:24
  100.5 2.7 %collective-permute-start.26 = (bf16[512,512]{1,0:T(8,128)(2,1)}, bf16[512,512]{1,0:T(8,128)(2,1)}, u32[]{:S(2)}, u32[]{:S(2)}) collective-permute-start(bf16[512,512]{1,0:T(8,128)(2,1)} %collective-permute-done.13.refs_2_), channel_id=1, source_target_pairs={{0,7},{1,0},{2,1},{3,2},{4,3},{5,4},{6,5},{7,6},{8,15},{9,8},{10,9... | collective-permute-start | bytes 1572872 | tf_op jit(solution)/shard_map/ppermute | solution.py:24
  103.1 2.7 %partial_grad.5 = f32[2,128,512]{2,1,0:T(8,128)S(1)} custom-call(bf16[8,256,1152]{2,1,0:T(8,128)(2,1)} %all-to-all-done.grads_ref.tokens_ref, bf16[8,256,1152]{2,1,0:T(8,128)(2,1)} %all-to-all-done.grads_ref.tokens_ref), custom_call_target="tpu_custom_call" | custom-call | flops 2684354560 | tf_op jit(solution)/shard_map/partial_grad/pallas_call | solution.py:120
  111.6 3.3 %partial_grad.3 = f32[3,128,512]{2,1,0:T(8,128)S(1)} custom-call(bf16[8,256,384]{2,1,0:T(8,128)(2,1)S(1)} %all-to-all-done.1.tokens_ref, bf16[8,256,1152]{2,1,0:T(8,128)(2,1)} %all-to-all-done.grads_ref.tokens_ref), custom_call_target="tpu_custom_call" | custom-call | flops 4026531840 | tf_op jit(solution)/shard_map/partial_grad/pallas_call | solution.py:120
  114.9 5.8 %collective-permute-done.23 = f32[128,512]{1,0:T(8,128)} collective-permute-done((f32[128,512]{1,0:T(8,128)}, f32[128,512]{1,0:T(8,128)}, u32[]{:S(2)}, u32[]{:S(2)}) %collective-permute-start.23) | collective-permute-done | bytes 262176 | tf_op jit(solution)/shard_map/ppermute | solution.py:24
  125.5 4.5 %project.7 = (f32[256,512]{1,0:T(8,128)S(1)}, bf16[256,8192]{1,0:T(8,128)(2,1)}) custom-call(s32[16]{0:T(128)S(1)} %stack.335.place_ref, bf16[256,8192]{1,0:T(8,128)(2,1)} %bitcast.135, bf16[256,512]{1,0:T(8,128)(2,1)S(1)} %bitcast.129, bf16[512,512]{1,0:T(8,128)(2,1)} %collective-permute-done.11.refs_0_, ...), custom_call_target="tpu_custom_call", output_to_operand_aliasing={{1}: (8, {})} | custom-call | flops 3221225472 | bytes 4194304 | tf_op jit(solution)/shard_map/project/pallas_call | solution.py:201
  130.0 2.7 %collective-permute-start.28 = (bf16[512,512]{1,0:T(8,128)(2,1)S(1)}, bf16[512,512]{1,0:T(8,128)(2,1)}, u32[]{:S(2)}, u32[]{:S(2)}) collective-permute-start(bf16[512,512]{1,0:T(8,128)(2,1)S(1)} %collective-permute-done.19.refs_3_), channel_id=1, source_target_pairs={{0,7},{1,0},{2,1},{3,2},{4,3},{5,4},{6,5},{7,6},{8,15},{9,8},{10,9... | collective-permute-start | bytes 1572872 | tf_op jit(solution)/shard_map/ppermute | solution.py:24
  132.8 5.7 %collective-permute-start.31 = (f32[128,512]{1,0:T(8,128)S(1)}, f32[128,512]{1,0:T(8,128)S(1)}, u32[]{:S(2)}, u32[]{:S(2)}) collective-permute-start(f32[128,512]{1,0:T(8,128)S(1)} %fusion.3.inner_ref), channel_id=1, source_target_pairs={{0,64},{64,0},{1,65},{65,1},{2,66},{66,2},{3,67},{67,3},{4,68},{68... | collective-permute-start | bytes 786440 | tf_op jit(solution)/shard_map/ppermute | solution.py:36
  142.4 4.3 %project.8 = (f32[256,512]{1,0:T(8,128)S(1)}, bf16[256,8192]{1,0:T(8,128)(2,1)}) custom-call(s32[16]{0:T(128)S(1)} %stack.318.place_ref, bf16[256,8192]{1,0:T(8,128)(2,1)} %bitcast.136, bf16[256,512]{1,0:T(8,128)(2,1)S(1)} %bitcast.130, bf16[512,512]{1,0:T(8,128)(2,1)S(1)} %collective-permute-done.18.refs_0_, ...), custom_call_target="tpu_custom_call", output_to_operand_aliasing={{1}: (8, {})} | custom-call | flops 1073741824 | bytes 4194304 | tf_op jit(solution)/shard_map/project/pallas_call | solution.py:201
  146.7 3.9 %project.9 = (bf16[256,512]{1,0:T(8,128)(2,1)}, bf16[256,8192]{1,0:T(8,128)(2,1)}) custom-call(s32[8]{0:T(128)S(1)} %stack.260.place_ref, bf16[256,8192]{1,0:T(8,128)(2,1)} %bitcast.137, bf16[256,512]{1,0:T(8,128)(2,1)S(1)} %bitcast.131, bf16[512,512]{1,0:T(8,128)(2,1)S(1)} %collective-permute-done.27.refs_0_, ...), custom_call_target="tpu_custom_call", output_to_operand_aliasing={{1}: (6, {})} | custom-call | flops 536870912 | bytes 2097152 | tf_op jit(solution)/shard_map/project/pallas_call | solution.py:201
  (93 shorter events, 43.9 us)
Async XLA Ops:
  5.3 12.1 %collective-permute-start.2 = (bf16[128,512]{1,0:T(8,128)(2,1)S(1)}, bf16[128,512]{1,0:T(8,128)(2,1)S(1)}, u32[]{:S(2)}, u32[]{:S(2)}) collective-permute-start(bf16[128,512]{1,0:T(8,128)(2,1)S(1)} %collective-permute-done), channel_id=1, source_target_pairs={{0,16},{16,32},{32,48},{48,0},{1,17},{17,33},{33,49},{49,1},{2,18}... | collective-permute-start | bytes 393224 | tf_op jit(solution)/shard_map/ppermute | solution.py:28
  7.4 10.1 %collective-permute-start.5 = (bf16[128,512]{1,0:T(8,128)(2,1)}, bf16[128,512]{1,0:T(8,128)(2,1)S(1)}, u32[]{:S(2)}, u32[]{:S(2)}) collective-permute-start(bf16[128,512]{1,0:T(8,128)(2,1)} %bitcast.142), channel_id=1, source_target_pairs={{0,48},{16,0},{32,16},{48,32},{1,49},{17,1},{33,17},{49,33},{2,50}... | collective-permute-start | bytes 393224 | tf_op jit(solution)/shard_map/ppermute | solution.py:28
  17.8 59.7 %all-to-all-start = ((bf16[8,256,1152]{2,1,0:T(8,128)(2,1)}), bf16[8,256,1152]{2,1,0:T(8,128)(2,1)}, u32[]{:S(2)}, u32[]{:S(2)}) async-start(bf16[8,256,1152]{2,1,0:T(8,128)(2,1)} %get-tuple-element.47), calls=%async_computation | async-start | bytes 9437184 | tf_op jit(solution)/shard_map/all_to_all | solution.py:288
  25.0 15.2 %collective-permute-start.7 = (bf16[512,512]{1,0:T(8,128)(2,1)S(1)}, bf16[512,512]{1,0:T(8,128)(2,1)S(1)}, u32[]{:S(2)}, u32[]{:S(2)}) collective-permute-start(bf16[512,512]{1,0:T(8,128)(2,1)S(1)} %pad_maximum_fusion.refs_0_), channel_id=1, source_target_pairs={{0,1},{1,2},{2,3},{3,4},{4,5},{5,6},{6,7},{7,0},{8,9},{9,10},{10,1... | collective-permute-start | bytes 1572872 | tf_op jit(solution)/shard_map/ppermute | solution.py:24
  26.7 24.8 %collective-permute-start.8 = (bf16[512,512]{1,0:T(8,128)(2,1)S(1)}, bf16[512,512]{1,0:T(8,128)(2,1)S(1)}, u32[]{:S(2)}, u32[]{:S(2)}) collective-permute-start(bf16[512,512]{1,0:T(8,128)(2,1)S(1)} %pad_maximum_fusion.1.refs_1_), channel_id=1, source_target_pairs={{0,1},{1,2},{2,3},{3,4},{4,5},{5,6},{6,7},{7,0},{8,9},{9,10},{10,1... | collective-permute-start | bytes 1572872 | tf_op jit(solution)/shard_map/ppermute | solution.py:24
  28.3 23.1 %collective-permute-start.9 = (bf16[512,512]{1,0:T(8,128)(2,1)S(1)}, bf16[512,512]{1,0:T(8,128)(2,1)}, u32[]{:S(2)}, u32[]{:S(2)}) collective-permute-start(bf16[512,512]{1,0:T(8,128)(2,1)S(1)} %pad_maximum_fusion.refs_0_), channel_id=1, source_target_pairs={{0,7},{1,0},{2,1},{3,2},{4,3},{5,4},{6,5},{7,6},{8,15},{9,8},{10,9... | collective-permute-start | bytes 1572872 | tf_op jit(solution)/shard_map/ppermute | solution.py:24
  30.8 23.3 %collective-permute-start.10 = (bf16[512,512]{1,0:T(8,128)(2,1)S(1)}, bf16[512,512]{1,0:T(8,128)(2,1)S(1)}, u32[]{:S(2)}, u32[]{:S(2)}) collective-permute-start(bf16[512,512]{1,0:T(8,128)(2,1)S(1)} %pad_maximum_fusion.1.refs_1_), channel_id=1, source_target_pairs={{0,7},{1,0},{2,1},{3,2},{4,3},{5,4},{6,5},{7,6},{8,15},{9,8},{10,9... | collective-permute-start | bytes 1572872 | tf_op jit(solution)/shard_map/ppermute | solution.py:24
  32.2 60.4 %collective-permute-start.17 = (f32[2,128,128]{2,1,0:T(8,128)S(1)}, f32[2,128,128]{2,1,0:T(8,128)}, u32[]{:S(2)}, u32[]{:S(2)}) collective-permute-start(f32[2,128,128]{2,1,0:T(8,128)S(1)} %pad_maximum_fusion.5), channel_id=1, source_target_pairs={{0,64},{64,0},{1,65},{65,1},{2,66},{66,2},{3,67},{67,3},{4,68},{68... | collective-permute-start | bytes 393224 | tf_op jit(solution)/shard_map/ppermute | solution.py:36
  40.2 22.5 %collective-permute-start.11 = (bf16[512,512]{1,0:T(8,128)(2,1)S(1)}, bf16[512,512]{1,0:T(8,128)(2,1)}, u32[]{:S(2)}, u32[]{:S(2)}) collective-permute-start(bf16[512,512]{1,0:T(8,128)(2,1)S(1)} %collective-permute-done.7.refs_0_), channel_id=1, source_target_pairs={{0,1},{1,2},{2,3},{3,4},{4,5},{5,6},{6,7},{7,0},{8,9},{9,10},{10,1... | collective-permute-start | bytes 1572872 | tf_op jit(solution)/shard_map/ppermute | solution.py:24
  51.4 22.5 %collective-permute-start.12 = (bf16[512,512]{1,0:T(8,128)(2,1)S(1)}, bf16[512,512]{1,0:T(8,128)(2,1)S(1)}, u32[]{:S(2)}, u32[]{:S(2)}) collective-permute-start(bf16[512,512]{1,0:T(8,128)(2,1)S(1)} %collective-permute-done.8.refs_1_), channel_id=1, source_target_pairs={{0,1},{1,2},{2,3},{3,4},{4,5},{5,6},{6,7},{7,0},{8,9},{9,10},{10,1... | collective-permute-start | bytes 1572872 | tf_op jit(solution)/shard_map/ppermute | solution.py:24
  51.5 23.3 %collective-permute-start.13 = (bf16[512,512]{1,0:T(8,128)(2,1)}, bf16[512,512]{1,0:T(8,128)(2,1)}, u32[]{:S(2)}, u32[]{:S(2)}) collective-permute-start(bf16[512,512]{1,0:T(8,128)(2,1)} %collective-permute-done.9.refs_2_), channel_id=1, source_target_pairs={{0,7},{1,0},{2,1},{3,2},{4,3},{5,4},{6,5},{7,6},{8,15},{9,8},{10,9... | collective-permute-start | bytes 1572872 | tf_op jit(solution)/shard_map/ppermute | solution.py:24
  54.1 16.1 %collective-permute-start.14 = (bf16[512,512]{1,0:T(8,128)(2,1)S(1)}, bf16[512,512]{1,0:T(8,128)(2,1)}, u32[]{:S(2)}, u32[]{:S(2)}) collective-permute-start(bf16[512,512]{1,0:T(8,128)(2,1)S(1)} %collective-permute-done.10.refs_3_), channel_id=1, source_target_pairs={{0,7},{1,0},{2,1},{3,2},{4,3},{5,4},{6,5},{7,6},{8,15},{9,8},{10,9... | collective-permute-start | bytes 1572872 | tf_op jit(solution)/shard_map/ppermute | solution.py:24
  62.7 36.1 %collective-permute-start.18 = (bf16[512,512]{1,0:T(8,128)(2,1)}, bf16[512,512]{1,0:T(8,128)(2,1)S(1)}, u32[]{:S(2)}, u32[]{:S(2)}) collective-permute-start(bf16[512,512]{1,0:T(8,128)(2,1)} %collective-permute-done.11.refs_0_), channel_id=1, source_target_pairs={{0,1},{1,2},{2,3},{3,4},{4,5},{5,6},{6,7},{7,0},{8,9},{9,10},{10,1... | collective-permute-start | bytes 1572872 | tf_op jit(solution)/shard_map/ppermute | solution.py:24
  70.2 28.5 %collective-permute-start.19 = (bf16[512,512]{1,0:T(8,128)(2,1)}, bf16[512,512]{1,0:T(8,128)(2,1)S(1)}, u32[]{:S(2)}, u32[]{:S(2)}) collective-permute-start(bf16[512,512]{1,0:T(8,128)(2,1)} %collective-permute-done.14.refs_3_), channel_id=1, source_target_pairs={{0,7},{1,0},{2,1},{3,2},{4,3},{5,4},{6,5},{7,6},{8,15},{9,8},{10,9... | collective-permute-start | bytes 1572872 | tf_op jit(solution)/shard_map/ppermute | solution.py:24
  77.5 34.1 %all-to-all-start.1 = ((bf16[8,256,384]{2,1,0:T(8,128)(2,1)}), bf16[8,256,384]{2,1,0:T(8,128)(2,1)S(1)}, u32[]{:S(2)}, u32[]{:S(2)}) async-start(bf16[8,256,384]{2,1,0:T(8,128)(2,1)} %get-tuple-element.54), calls=%async_computation.1 | async-start | bytes 3145728 | tf_op jit(solution)/shard_map/all_to_all | solution.py:313
  100.4 22.3 %collective-permute-start.25 = (bf16[512,512]{1,0:T(8,128)(2,1)}, bf16[512,512]{1,0:T(8,128)(2,1)}, u32[]{:S(2)}, u32[]{:S(2)}) collective-permute-start(bf16[512,512]{1,0:T(8,128)(2,1)} %copy-done.2), channel_id=1, source_target_pairs={{0,1},{1,2},{2,3},{3,4},{4,5},{5,6},{6,7},{7,0},{8,9},{9,10},{10,1... | collective-permute-start | bytes 1572872 | tf_op jit(solution)/shard_map/ppermute | solution.py:24
  100.5 22.2 %collective-permute-start.26 = (bf16[512,512]{1,0:T(8,128)(2,1)}, bf16[512,512]{1,0:T(8,128)(2,1)}, u32[]{:S(2)}, u32[]{:S(2)}) collective-permute-start(bf16[512,512]{1,0:T(8,128)(2,1)} %collective-permute-done.13.refs_2_), channel_id=1, source_target_pairs={{0,7},{1,0},{2,1},{3,2},{4,3},{5,4},{6,5},{7,6},{8,15},{9,8},{10,9... | collective-permute-start | bytes 1572872 | tf_op jit(solution)/shard_map/ppermute | solution.py:24
  107.7 13.0 %collective-permute-start.23 = (f32[128,512]{1,0:T(8,128)}, f32[128,512]{1,0:T(8,128)}, u32[]{:S(2)}, u32[]{:S(2)}) collective-permute-start(f32[128,512]{1,0:T(8,128)} %get-tuple-element.94), channel_id=1, source_target_pairs={{0,7},{1,0},{2,1},{3,2},{4,3},{5,4},{6,5},{7,6},{8,15},{9,8},{10,9... | collective-permute-start | bytes 786440 | tf_op jit(solution)/shard_map/ppermute | solution.py:24
  107.8 13.7 %collective-permute-start.21 = (f32[128,512]{1,0:T(8,128)}, f32[128,512]{1,0:T(8,128)}, u32[]{:S(2)}, u32[]{:S(2)}) collective-permute-start(f32[128,512]{1,0:T(8,128)} %get-tuple-element.95), channel_id=1, source_target_pairs={{0,1},{1,2},{2,3},{3,4},{4,5},{5,6},{6,7},{7,0},{8,9},{9,10},{10,1... | collective-permute-start | bytes 786440 | tf_op jit(solution)/shard_map/ppermute | solution.py:24
  109.2 13.5 %collective-permute-start.24 = (f32[2,2,128,128]{3,2,1,0:T(8,128)S(1)}, f32[2,2,128,128]{3,2,1,0:T(8,128)S(1)}, u32[]{:S(2)}, u32[]{:S(2)}) collective-permute-start(f32[2,2,128,128]{3,2,1,0:T(8,128)S(1)} %pad_maximum_fusion.4.refs_0_), channel_id=1, source_target_pairs={{0,128},{128,0},{1,129},{129,1},{2,130},{130,2},{3,131},{131,3},{4... | collective-permute-start | bytes 786440 | tf_op jit(solution)/shard_map/ppermute | solution.py:40
  122.7 10.0 %collective-permute-start.29 = (f32[128,512]{1,0:T(8,128)S(1)}, f32[128,512]{1,0:T(8,128)S(1)}, u32[]{:S(2)}, u32[]{:S(2)}) collective-permute-start(f32[128,512]{1,0:T(8,128)S(1)} %get-tuple-element.79), channel_id=1, source_target_pairs={{0,1},{1,2},{2,3},{3,4},{4,5},{5,6},{6,7},{7,0},{8,9},{9,10},{10,1... | collective-permute-start | bytes 786440 | tf_op jit(solution)/shard_map/ppermute | solution.py:24
  129.9 16.8 %collective-permute-start.27 = (bf16[512,512]{1,0:T(8,128)(2,1)S(1)}, bf16[512,512]{1,0:T(8,128)(2,1)S(1)}, u32[]{:S(2)}, u32[]{:S(2)}) collective-permute-start(bf16[512,512]{1,0:T(8,128)(2,1)S(1)} %collective-permute-done.18.refs_0_), channel_id=1, source_target_pairs={{0,1},{1,2},{2,3},{3,4},{4,5},{5,6},{6,7},{7,0},{8,9},{9,10},{10,1... | collective-permute-start | bytes 1572872 | tf_op jit(solution)/shard_map/ppermute | solution.py:24
  130.0 16.7 %collective-permute-start.28 = (bf16[512,512]{1,0:T(8,128)(2,1)S(1)}, bf16[512,512]{1,0:T(8,128)(2,1)}, u32[]{:S(2)}, u32[]{:S(2)}) collective-permute-start(bf16[512,512]{1,0:T(8,128)(2,1)S(1)} %collective-permute-done.19.refs_3_), channel_id=1, source_target_pairs={{0,7},{1,0},{2,1},{3,2},{4,3},{5,4},{6,5},{7,6},{8,15},{9,8},{10,9... | collective-permute-start | bytes 1572872 | tf_op jit(solution)/shard_map/ppermute | solution.py:24
  139.7 11.0 %collective-permute-start.32 = (f32[128,512]{1,0:T(8,128)S(1)}, f32[128,512]{1,0:T(8,128)}, u32[]{:S(2)}, u32[]{:S(2)}) collective-permute-start(f32[128,512]{1,0:T(8,128)S(1)} %add.613.near_ref), channel_id=1, source_target_pairs={{0,128},{128,0},{1,129},{129,1},{2,130},{130,2},{3,131},{131,3},{4... | collective-permute-start | bytes 786440 | tf_op jit(solution)/shard_map/ppermute | solution.py:40
  (21 other events, 201.7 us)

commit v6 on v5

--- a/solution.py
+++ b/solution.py
@@ -308,7 +308,7 @@
         if k == 1:
             carry = add(carry, 1, pieces, 5)
     step3 = [None] * 4
-    step3[0], step3[3] = shift_z(pieces[0], 1), shift_z(pieces[3], -1)
+    step3[0], step3[2] = shift_z(pieces[0], 1), shift_z(pieces[2], -1)
     first, _, pieces = lax.optimization_barrier((first, carry[0], pieces))
     second = lax.all_to_all(after(second, first), sub, 0, 0)
 
@@ -326,7 +326,7 @@
     down = jnp.concatenate([back[:half], back[half:] + down])
     up, down, states, step3 = lax.optimization_barrier((up, down, states, step3))
     step3[1] = shift_z(after(pieces[1], up), 1)
-    step3[2] = shift_z(after(pieces[2], down), -1)
+    step3[3] = shift_z(after(pieces[3], down), -1)
     ahead, back = terms(after(first, up, down), 5, 2, 6)
     up, down = shift_z(up, 1), shift_z(down, -1)
     up, down = ahead + up, back + down

time: 154 us -> 154 us (level)
  transfers between devices with their start and end apart: 35 -> 35, of which waited for: 14 -> 13; matrix products, arithmetic and copies ran while one was open for 4% -> 4% of each run, Pallas kernels for 22% -> 22%
where the time goes in v6:
time: 154 us; the launch traced here: 152 us
  starting transfers between devices  67.9 us (44%)
  waiting for transfers between devices  40.6 us (26%)
  Pallas kernels  35.8 us (23%)
  other arithmetic  4.94 us (3%)
  local copies, waits for them, and re-layouts  2.21 us (1%)
    ppermute x22, waiting for transfers between devices, shift_z(): return lax.ppermute(x, 'z', [(i, (i + dz) % NZ) for i in range(NZ)])  35.2 us
    ppermute x22, starting transfers between devices, shift_z(): return lax.ppermute(x, 'z', [(i, (i + dz) % NZ) for i in range(NZ)])  30.1 us
    pallas_call x5, Pallas kernels, project(): pl.pallas_call(functools.partial(project_kernel, sizes, first), in_specs=...  19.6 us
    pallas_call x3, Pallas kernels, partial_grad(): pl.pallas_call(grad_kernel, grid=(count,), in_specs=[pl.BlockSpec((member...  9.8 us
    ppermute x2, starting transfers between devices, shift_core(): return lax.ppermute(x, 'core', [(0, 1), (1, 0)])  9.28 us
    ppermute x6, starting transfers between devices, shift_y(): return lax.ppermute(x, 'y', [(i, (i + dy) % NY) for i in range(NY)])  8.66 us
    all_to_all x1, starting transfers between devices, local(): first = lax.all_to_all(first, sub, 0, 0)  7.2 us
    all_to_all x1, starting transfers between devices, local(): second = lax.all_to_all(after(second, first), sub, 0, 0)  5.58 us
  transfers between devices with their start and end apart: 35, of which 13 were waited for; matrix products, arithmetic and copies ran while one was open for 4% of the time, Pallas kernels for 22%

profile of v6, /device:TPU:1, one launch (start us, length us, event | category | flops | bytes accessed | tf_op | source)
XLA Modules:
  0.0 152.5 jit_solution(17104863144407279061)
XLA Ops:
  12.8 4.7 %sort_tokens.1 = (bf16[8,256,1152]{2,1,0:T(8,128)(2,1)}, bf16[8,256,384]{2,1,0:T(8,128)(2,1)}) custom-call(s32[8]{0:T(128)S(1)} %stack.269.place_ref, bf16[256,8192]{1,0:T(8,128)(2,1)} %bitcast.132, bf16[256,512]{1,0:T(8,128)(2,1)} %bitcast.126), custom_call_target="tpu_custom_call" | custom-call | bytes 17825792 | tf_op jit(solution)/shard_map/sort_tokens/pallas_call | solution.py:87
  17.8 7.2 %all-to-all-start = ((bf16[8,256,1152]{2,1,0:T(8,128)(2,1)}), bf16[8,256,1152]{2,1,0:T(8,128)(2,1)}, u32[]{:S(2)}, u32[]{:S(2)}) async-start(bf16[8,256,1152]{2,1,0:T(8,128)(2,1)} %get-tuple-element.47), calls=%async_computation | async-start | bytes 9437184 | tf_op jit(solution)/shard_map/all_to_all | solution.py:288
  32.2 3.7 %collective-permute-start.17 = (f32[2,128,128]{2,1,0:T(8,128)S(1)}, f32[2,128,128]{2,1,0:T(8,128)}, u32[]{:S(2)}, u32[]{:S(2)}) collective-permute-start(f32[2,128,128]{2,1,0:T(8,128)S(1)} %pad_maximum_fusion.5), channel_id=1, source_target_pairs={{0,64},{64,0},{1,65},{65,1},{2,66},{66,2},{3,67},{67,3},{4,68},{68... | collective-permute-start | bytes 393224 | tf_op jit(solution)/shard_map/ppermute | solution.py:36
  36.0 4.2 %collective-permute-done.7.refs_0_ = bf16[512,512]{1,0:T(8,128)(2,1)S(1)} collective-permute-done((bf16[512,512]{1,0:T(8,128)(2,1)S(1)}, bf16[512,512]{1,0:T(8,128)(2,1)S(1)}, u32[]{:S(2)}, u32[]{:S(2)}) %collective-permute-start.7) | collective-permute-done | bytes 524320 | tf_op jit(solution)/shard_map/ppermute | solution.py:24
  40.2 11.2 %collective-permute-done.8.refs_1_ = bf16[512,512]{1,0:T(8,128)(2,1)S(1)} collective-permute-done((bf16[512,512]{1,0:T(8,128)(2,1)S(1)}, bf16[512,512]{1,0:T(8,128)(2,1)S(1)}, u32[]{:S(2)}, u32[]{:S(2)}) %collective-permute-start.8) | collective-permute-done | bytes 524320 | tf_op jit(solution)/shard_map/ppermute | solution.py:24
  51.5 2.7 %collective-permute-start.13 = (bf16[512,512]{1,0:T(8,128)(2,1)S(1)}, bf16[512,512]{1,0:T(8,128)(2,1)}, u32[]{:S(2)}, u32[]{:S(2)}) collective-permute-start(bf16[512,512]{1,0:T(8,128)(2,1)S(1)} %collective-permute-done.9.refs_2_), channel_id=1, source_target_pairs={{0,7},{1,0},{2,1},{3,2},{4,3},{5,4},{6,5},{7,6},{8,15},{9,8},{10,9... | collective-permute-start | bytes 1572872 | tf_op jit(solution)/shard_map/ppermute | solution.py:24
  54.2 2.7 %project.5 = (f32[256,512]{1,0:T(8,128)S(1)}, bf16[256,8192]{1,0:T(8,128)(2,1)}) custom-call(s32[8]{0:T(128)S(1)} %stack.295.place_ref, bf16[256,8192]{1,0:T(8,128)(2,1)} %bitcast.133, bf16[256,512]{1,0:T(8,128)(2,1)S(1)} %bitcast.127, bf16[512,512]{1,0:T(8,128)(2,1)S(1)} %pad_maximum_fusion.refs_0_, bf16[512,512]{1,0:T(8,128)(2,1)S(1)} %pad_maximum_fusion.1.refs_1_), custom_call_target="tpu_custom_call" | custom-call | flops 536870912 | bytes 2097152 | tf_op jit(solution)/shard_map/project/pallas_call | solution.py:201
  56.9 4.1 %project.6 = (f32[256,512]{1,0:T(8,128)S(1)}, bf16[256,8192]{1,0:T(8,128)(2,1)}) custom-call(s32[16]{0:T(128)S(1)} %stack.286.place_ref, bf16[256,8192]{1,0:T(8,128)(2,1)} %bitcast.134, bf16[256,512]{1,0:T(8,128)(2,1)S(1)} %bitcast.128, bf16[512,512]{1,0:T(8,128)(2,1)S(1)} %collective-permute-done.7.refs_0_, ...), custom_call_target="tpu_custom_call", output_to_operand_aliasing={{1}: (8, {})} | custom-call | flops 5368709120 | bytes 4194304 | tf_op jit(solution)/shard_map/project/pallas_call | solution.py:201
  65.4 8.6 %collective-permute-done.12.refs_1_ = bf16[512,512]{1,0:T(8,128)(2,1)S(1)} collective-permute-done((bf16[512,512]{1,0:T(8,128)(2,1)S(1)}, bf16[512,512]{1,0:T(8,128)(2,1)S(1)}, u32[]{:S(2)}, u32[]{:S(2)}) %collective-permute-start.12) | collective-permute-done | bytes 524320 | tf_op jit(solution)/shard_map/ppermute | solution.py:24
  74.7 2.8 %all-to-all-done.grads_ref.tokens_ref = bf16[8,256,1152]{2,1,0:T(8,128)(2,1)} async-done(((bf16[8,256,1152]{2,1,0:T(8,128)(2,1)}), bf16[8,256,1152]{2,1,0:T(8,128)(2,1)}, u32[]{:S(2)}, u32[]{:S(2)}) %all-to-all-start) | async-done | bytes 4718624 | tf_op jit(solution)/shard_map/all_to_all | solution.py:288
  77.5 5.6 %all-to-all-start.1 = ((bf16[8,256,384]{2,1,0:T(8,128)(2,1)}), bf16[8,256,384]{2,1,0:T(8,128)(2,1)S(1)}, u32[]{:S(2)}, u32[]{:S(2)}) async-start(bf16[8,256,384]{2,1,0:T(8,128)(2,1)} %get-tuple-element.54), calls=%async_computation.1 | async-start | bytes 3145728 | tf_op jit(solution)/shard_map/all_to_all | solution.py:313
  83.1 3.8 %partial_grad.4 = f32[3,128,512]{2,1,0:T(8,128)S(1)} custom-call(bf16[8,256,1152]{2,1,0:T(8,128)(2,1)} %all-to-all-done.grads_ref.tokens_ref, bf16[8,256,1152]{2,1,0:T(8,128)(2,1)} %all-to-all-done.grads_ref.tokens_ref), custom_call_target="tpu_custom_call" | custom-call | flops 4026531840 | tf_op jit(solution)/shard_map/partial_grad/pallas_call | solution.py:120
  86.9 5.7 %collective-permute-start.16 = (f32[64,512]{1,0:T(8,128)S(1)}, f32[64,512]{1,0:T(8,128)S(1)}, u32[]{:S(2)}, u32[]{:S(2)}) collective-permute-start(f32[64,512]{1,0:T(8,128)S(1)} %get-tuple-element.89), channel_id=1, source_target_pairs={{0,7},{1,0},{2,1},{3,2},{4,3},{5,4},{6,5},{7,6},{8,15},{9,8},{10,9... | collective-permute-start | bytes 393224 | tf_op jit(solution)/shard_map/ppermute | solution.py:24
  94.5 3.4 %collective-permute-done.15 = f32[64,512]{1,0:T(8,128)S(1)} collective-permute-done((f32[64,512]{1,0:T(8,128)S(1)}, f32[64,512]{1,0:T(8,128)S(1)}, u32[]{:S(2)}, u32[]{:S(2)}) %collective-permute-start.15) | collective-permute-done | bytes 131104 | tf_op jit(solution)/shard_map/ppermute | solution.py:24
  100.5 2.7 %collective-permute-start.26 = (bf16[512,512]{1,0:T(8,128)(2,1)}, bf16[512,512]{1,0:T(8,128)(2,1)}, u32[]{:S(2)}, u32[]{:S(2)}) collective-permute-start(bf16[512,512]{1,0:T(8,128)(2,1)} %collective-permute-done.14.refs_3_), channel_id=1, source_target_pairs={{0,7},{1,0},{2,1},{3,2},{4,3},{5,4},{6,5},{7,6},{8,15},{9,8},{10,9... | collective-permute-start | bytes 1572872 | tf_op jit(solution)/shard_map/ppermute | solution.py:24
  103.1 2.7 %partial_grad.5 = f32[2,128,512]{2,1,0:T(8,128)S(1)} custom-call(bf16[8,256,1152]{2,1,0:T(8,128)(2,1)} %all-to-all-done.grads_ref.tokens_ref, bf16[8,256,1152]{2,1,0:T(8,128)(2,1)} %all-to-all-done.grads_ref.tokens_ref), custom_call_target="tpu_custom_call" | custom-call | flops 2684354560 | tf_op jit(solution)/shard_map/partial_grad/pallas_call | solution.py:120
  111.6 3.3 %partial_grad.3 = f32[3,128,512]{2,1,0:T(8,128)S(1)} custom-call(bf16[8,256,384]{2,1,0:T(8,128)(2,1)S(1)} %all-to-all-done.1.tokens_ref, bf16[8,256,1152]{2,1,0:T(8,128)(2,1)} %all-to-all-done.grads_ref.tokens_ref), custom_call_target="tpu_custom_call" | custom-call | flops 4026531840 | tf_op jit(solution)/shard_map/partial_grad/pallas_call | solution.py:120
  114.9 5.8 %collective-permute-done.23 = f32[128,512]{1,0:T(8,128)} collective-permute-done((f32[128,512]{1,0:T(8,128)}, f32[128,512]{1,0:T(8,128)}, u32[]{:S(2)}, u32[]{:S(2)}) %collective-permute-start.23) | collective-permute-done | bytes 262176 | tf_op jit(solution)/shard_map/ppermute | solution.py:24
  122.2 3.3 %collective-permute-start.30 = (f32[128,512]{1,0:T(8,128)S(1)}, f32[128,512]{1,0:T(8,128)S(1)}, u32[]{:S(2)}, u32[]{:S(2)}) collective-permute-start(f32[128,512]{1,0:T(8,128)S(1)} %get-tuple-element.80), channel_id=1, source_target_pairs={{0,7},{1,0},{2,1},{3,2},{4,3},{5,4},{6,5},{7,6},{8,15},{9,8},{10,9... | collective-permute-start | bytes 786440 | tf_op jit(solution)/shard_map/ppermute | solution.py:24
  125.5 4.5 %project.7 = (f32[256,512]{1,0:T(8,128)S(1)}, bf16[256,8192]{1,0:T(8,128)(2,1)}) custom-call(s32[16]{0:T(128)S(1)} %stack.335.place_ref, bf16[256,8192]{1,0:T(8,128)(2,1)} %bitcast.135, bf16[256,512]{1,0:T(8,128)(2,1)S(1)} %bitcast.129, bf16[512,512]{1,0:T(8,128)(2,1)} %collective-permute-done.11.refs_0_, ...), custom_call_target="tpu_custom_call", output_to_operand_aliasing={{1}: (8, {})} | custom-call | flops 3221225472 | bytes 4194304 | tf_op jit(solution)/shard_map/project/pallas_call | solution.py:201
  130.1 2.7 %collective-permute-start.28 = (bf16[512,512]{1,0:T(8,128)(2,1)}, bf16[512,512]{1,0:T(8,128)(2,1)}, u32[]{:S(2)}, u32[]{:S(2)}) collective-permute-start(bf16[512,512]{1,0:T(8,128)(2,1)} %collective-permute-done.26.refs_3_), channel_id=1, source_target_pairs={{0,7},{1,0},{2,1},{3,2},{4,3},{5,4},{6,5},{7,6},{8,15},{9,8},{10,9... | collective-permute-start | bytes 1572872 | tf_op jit(solution)/shard_map/ppermute | solution.py:24
  132.8 5.6 %collective-permute-start.31 = (f32[128,512]{1,0:T(8,128)S(1)}, f32[128,512]{1,0:T(8,128)S(1)}, u32[]{:S(2)}, u32[]{:S(2)}) collective-permute-start(f32[128,512]{1,0:T(8,128)S(1)} %fusion.3.inner_ref), channel_id=1, source_target_pairs={{0,64},{64,0},{1,65},{65,1},{2,66},{66,2},{3,67},{67,3},{4,68},{68... | collective-permute-start | bytes 786440 | tf_op jit(solution)/shard_map/ppermute | solution.py:36
  142.4 4.3 %project.8 = (f32[256,512]{1,0:T(8,128)S(1)}, bf16[256,8192]{1,0:T(8,128)(2,1)}) custom-call(s32[16]{0:T(128)S(1)} %stack.318.place_ref, bf16[256,8192]{1,0:T(8,128)(2,1)} %bitcast.136, bf16[256,512]{1,0:T(8,128)(2,1)S(1)} %bitcast.130, bf16[512,512]{1,0:T(8,128)(2,1)S(1)} %collective-permute-done.18.refs_0_, ...), custom_call_target="tpu_custom_call", output_to_operand_aliasing={{1}: (8, {})} | custom-call | flops 1073741824 | bytes 4194304 | tf_op jit(solution)/shard_map/project/pallas_call | solution.py:201
  146.7 3.9 %project.9 = (bf16[256,512]{1,0:T(8,128)(2,1)}, bf16[256,8192]{1,0:T(8,128)(2,1)}) custom-call(s32[8]{0:T(128)S(1)} %stack.260.place_ref, bf16[256,8192]{1,0:T(8,128)(2,1)} %bitcast.137, bf16[256,512]{1,0:T(8,128)(2,1)S(1)} %bitcast.131, bf16[512,512]{1,0:T(8,128)(2,1)S(1)} %collective-permute-done.27.refs_0_, ...), custom_call_target="tpu_custom_call", output_to_operand_aliasing={{1}: (6, {})} | custom-call | flops 536870912 | bytes 2097152 | tf_op jit(solution)/shard_map/project/pallas_call | solution.py:201
  (93 shorter events, 42.5 us)
Async XLA Ops:
  5.3 12.1 %collective-permute-start.2 = (bf16[128,512]{1,0:T(8,128)(2,1)S(1)}, bf16[128,512]{1,0:T(8,128)(2,1)S(1)}, u32[]{:S(2)}, u32[]{:S(2)}) collective-permute-start(bf16[128,512]{1,0:T(8,128)(2,1)S(1)} %collective-permute-done), channel_id=1, source_target_pairs={{0,16},{16,32},{32,48},{48,0},{1,17},{17,33},{33,49},{49,1},{2,18}... | collective-permute-start | bytes 393224 | tf_op jit(solution)/shard_map/ppermute | solution.py:28
  17.8 59.7 %all-to-all-start = ((bf16[8,256,1152]{2,1,0:T(8,128)(2,1)}), bf16[8,256,1152]{2,1,0:T(8,128)(2,1)}, u32[]{:S(2)}, u32[]{:S(2)}) async-start(bf16[8,256,1152]{2,1,0:T(8,128)(2,1)} %get-tuple-element.47), calls=%async_computation | async-start | bytes 9437184 | tf_op jit(solution)/shard_map/all_to_all | solution.py:288
  25.0 15.2 %collective-permute-start.7 = (bf16[512,512]{1,0:T(8,128)(2,1)S(1)}, bf16[512,512]{1,0:T(8,128)(2,1)S(1)}, u32[]{:S(2)}, u32[]{:S(2)}) collective-permute-start(bf16[512,512]{1,0:T(8,128)(2,1)S(1)} %pad_maximum_fusion.refs_0_), channel_id=1, source_target_pairs={{0,1},{1,2},{2,3},{3,4},{4,5},{5,6},{6,7},{7,0},{8,9},{9,10},{10,1... | collective-permute-start | bytes 1572872 | tf_op jit(solution)/shard_map/ppermute | solution.py:24
  26.7 24.8 %collective-permute-start.8 = (bf16[512,512]{1,0:T(8,128)(2,1)S(1)}, bf16[512,512]{1,0:T(8,128)(2,1)S(1)}, u32[]{:S(2)}, u32[]{:S(2)}) collective-permute-start(bf16[512,512]{1,0:T(8,128)(2,1)S(1)} %pad_maximum_fusion.1.refs_1_), channel_id=1, source_target_pairs={{0,1},{1,2},{2,3},{3,4},{4,5},{5,6},{6,7},{7,0},{8,9},{9,10},{10,1... | collective-permute-start | bytes 1572872 | tf_op jit(solution)/shard_map/ppermute | solution.py:24
  28.3 23.1 %collective-permute-start.9 = (bf16[512,512]{1,0:T(8,128)(2,1)S(1)}, bf16[512,512]{1,0:T(8,128)(2,1)S(1)}, u32[]{:S(2)}, u32[]{:S(2)}) collective-permute-start(bf16[512,512]{1,0:T(8,128)(2,1)S(1)} %pad_maximum_fusion.refs_0_), channel_id=1, source_target_pairs={{0,7},{1,0},{2,1},{3,2},{4,3},{5,4},{6,5},{7,6},{8,15},{9,8},{10,9... | collective-permute-start | bytes 1572872 | tf_op jit(solution)/shard_map/ppermute | solution.py:24
  30.8 23.3 %collective-permute-start.10 = (bf16[512,512]{1,0:T(8,128)(2,1)S(1)}, bf16[512,512]{1,0:T(8,128)(2,1)}, u32[]{:S(2)}, u32[]{:S(2)}) collective-permute-start(bf16[512,512]{1,0:T(8,128)(2,1)S(1)} %pad_maximum_fusion.1.refs_1_), channel_id=1, source_target_pairs={{0,7},{1,0},{2,1},{3,2},{4,3},{5,4},{6,5},{7,6},{8,15},{9,8},{10,9... | collective-permute-start | bytes 1572872 | tf_op jit(solution)/shard_map/ppermute | solution.py:24
  32.2 60.4 %collective-permute-start.17 = (f32[2,128,128]{2,1,0:T(8,128)S(1)}, f32[2,128,128]{2,1,0:T(8,128)}, u32[]{:S(2)}, u32[]{:S(2)}) collective-permute-start(f32[2,128,128]{2,1,0:T(8,128)S(1)} %pad_maximum_fusion.5), channel_id=1, source_target_pairs={{0,64},{64,0},{1,65},{65,1},{2,66},{66,2},{3,67},{67,3},{4,68},{68... | collective-permute-start | bytes 393224 | tf_op jit(solution)/shard_map/ppermute | solution.py:36
  40.2 22.5 %collective-permute-start.11 = (bf16[512,512]{1,0:T(8,128)(2,1)S(1)}, bf16[512,512]{1,0:T(8,128)(2,1)}, u32[]{:S(2)}, u32[]{:S(2)}) collective-permute-start(bf16[512,512]{1,0:T(8,128)(2,1)S(1)} %collective-permute-done.7.refs_0_), channel_id=1, source_target_pairs={{0,1},{1,2},{2,3},{3,4},{4,5},{5,6},{6,7},{7,0},{8,9},{9,10},{10,1... | collective-permute-start | bytes 1572872 | tf_op jit(solution)/shard_map/ppermute | solution.py:24
  51.4 22.5 %collective-permute-start.12 = (bf16[512,512]{1,0:T(8,128)(2,1)S(1)}, bf16[512,512]{1,0:T(8,128)(2,1)S(1)}, u32[]{:S(2)}, u32[]{:S(2)}) collective-permute-start(bf16[512,512]{1,0:T(8,128)(2,1)S(1)} %collective-permute-done.8.refs_1_), channel_id=1, source_target_pairs={{0,1},{1,2},{2,3},{3,4},{4,5},{5,6},{6,7},{7,0},{8,9},{9,10},{10,1... | collective-permute-start | bytes 1572872 | tf_op jit(solution)/shard_map/ppermute | solution.py:24
  51.5 11.8 %collective-permute-start.13 = (bf16[512,512]{1,0:T(8,128)(2,1)S(1)}, bf16[512,512]{1,0:T(8,128)(2,1)}, u32[]{:S(2)}, u32[]{:S(2)}) collective-permute-start(bf16[512,512]{1,0:T(8,128)(2,1)S(1)} %collective-permute-done.9.refs_2_), channel_id=1, source_target_pairs={{0,7},{1,0},{2,1},{3,2},{4,3},{5,4},{6,5},{7,6},{8,15},{9,8},{10,9... | collective-permute-start | bytes 1572872 | tf_op jit(solution)/shard_map/ppermute | solution.py:24
  54.1 20.6 %collective-permute-start.14 = (bf16[512,512]{1,0:T(8,128)(2,1)}, bf16[512,512]{1,0:T(8,128)(2,1)}, u32[]{:S(2)}, u32[]{:S(2)}) collective-permute-start(bf16[512,512]{1,0:T(8,128)(2,1)} %collective-permute-done.10.refs_3_), channel_id=1, source_target_pairs={{0,7},{1,0},{2,1},{3,2},{4,3},{5,4},{6,5},{7,6},{8,15},{9,8},{10,9... | collective-permute-start | bytes 1572872 | tf_op jit(solution)/shard_map/ppermute | solution.py:24
  62.7 36.1 %collective-permute-start.18 = (bf16[512,512]{1,0:T(8,128)(2,1)}, bf16[512,512]{1,0:T(8,128)(2,1)S(1)}, u32[]{:S(2)}, u32[]{:S(2)}) collective-permute-start(bf16[512,512]{1,0:T(8,128)(2,1)} %collective-permute-done.11.refs_0_), channel_id=1, source_target_pairs={{0,1},{1,2},{2,3},{3,4},{4,5},{5,6},{6,7},{7,0},{8,9},{9,10},{10,1... | collective-permute-start | bytes 1572872 | tf_op jit(solution)/shard_map/ppermute | solution.py:24
  63.3 35.5 %collective-permute-start.19 = (bf16[512,512]{1,0:T(8,128)(2,1)}, bf16[512,512]{1,0:T(8,128)(2,1)S(1)}, u32[]{:S(2)}, u32[]{:S(2)}) collective-permute-start(bf16[512,512]{1,0:T(8,128)(2,1)} %collective-permute-done.13.refs_2_), channel_id=1, source_target_pairs={{0,7},{1,0},{2,1},{3,2},{4,3},{5,4},{6,5},{7,6},{8,15},{9,8},{10,9... | collective-permute-start | bytes 1572872 | tf_op jit(solution)/shard_map/ppermute | solution.py:24
  77.5 34.1 %all-to-all-start.1 = ((bf16[8,256,384]{2,1,0:T(8,128)(2,1)}), bf16[8,256,384]{2,1,0:T(8,128)(2,1)S(1)}, u32[]{:S(2)}, u32[]{:S(2)}) async-start(bf16[8,256,384]{2,1,0:T(8,128)(2,1)} %get-tuple-element.54), calls=%async_computation.1 | async-start | bytes 3145728 | tf_op jit(solution)/shard_map/all_to_all | solution.py:313
  100.4 21.7 %collective-permute-start.25 = (bf16[512,512]{1,0:T(8,128)(2,1)}, bf16[512,512]{1,0:T(8,128)(2,1)}, u32[]{:S(2)}, u32[]{:S(2)}) collective-permute-start(bf16[512,512]{1,0:T(8,128)(2,1)} %copy-done.2), channel_id=1, source_target_pairs={{0,1},{1,2},{2,3},{3,4},{4,5},{5,6},{6,7},{7,0},{8,9},{9,10},{10,1... | collective-permute-start | bytes 1572872 | tf_op jit(solution)/shard_map/ppermute | solution.py:24
  100.5 21.6 %collective-permute-start.26 = (bf16[512,512]{1,0:T(8,128)(2,1)}, bf16[512,512]{1,0:T(8,128)(2,1)}, u32[]{:S(2)}, u32[]{:S(2)}) collective-permute-start(bf16[512,512]{1,0:T(8,128)(2,1)} %collective-permute-done.14.refs_3_), channel_id=1, source_target_pairs={{0,7},{1,0},{2,1},{3,2},{4,3},{5,4},{6,5},{7,6},{8,15},{9,8},{10,9... | collective-permute-start | bytes 1572872 | tf_op jit(solution)/shard_map/ppermute | solution.py:24
  107.7 13.1 %collective-permute-start.23 = (f32[128,512]{1,0:T(8,128)}, f32[128,512]{1,0:T(8,128)}, u32[]{:S(2)}, u32[]{:S(2)}) collective-permute-start(f32[128,512]{1,0:T(8,128)} %get-tuple-element.94), channel_id=1, source_target_pairs={{0,7},{1,0},{2,1},{3,2},{4,3},{5,4},{6,5},{7,6},{8,15},{9,8},{10,9... | collective-permute-start | bytes 786440 | tf_op jit(solution)/shard_map/ppermute | solution.py:24
  107.8 13.1 %collective-permute-start.21 = (f32[128,512]{1,0:T(8,128)}, f32[128,512]{1,0:T(8,128)}, u32[]{:S(2)}, u32[]{:S(2)}) collective-permute-start(f32[128,512]{1,0:T(8,128)} %get-tuple-element.95), channel_id=1, source_target_pairs={{0,1},{1,2},{2,3},{3,4},{4,5},{5,6},{6,7},{7,0},{8,9},{9,10},{10,1... | collective-permute-start | bytes 786440 | tf_op jit(solution)/shard_map/ppermute | solution.py:24
  109.2 12.9 %collective-permute-start.24 = (f32[2,2,128,128]{3,2,1,0:T(8,128)S(1)}, f32[2,2,128,128]{3,2,1,0:T(8,128)S(1)}, u32[]{:S(2)}, u32[]{:S(2)}) collective-permute-start(f32[2,2,128,128]{3,2,1,0:T(8,128)S(1)} %pad_maximum_fusion.4.refs_0_), channel_id=1, source_target_pairs={{0,128},{128,0},{1,129},{129,1},{2,130},{130,2},{3,131},{131,3},{4... | collective-permute-start | bytes 786440 | tf_op jit(solution)/shard_map/ppermute | solution.py:40
  122.1 10.7 %collective-permute-start.29 = (f32[128,512]{1,0:T(8,128)S(1)}, f32[128,512]{1,0:T(8,128)S(1)}, u32[]{:S(2)}, u32[]{:S(2)}) collective-permute-start(f32[128,512]{1,0:T(8,128)S(1)} %get-tuple-element.79), channel_id=1, source_target_pairs={{0,1},{1,2},{2,3},{3,4},{4,5},{5,6},{6,7},{7,0},{8,9},{9,10},{10,1... | collective-permute-start | bytes 786440 | tf_op jit(solution)/shard_map/ppermute | solution.py:24
  122.2 10.6 %collective-permute-start.30 = (f32[128,512]{1,0:T(8,128)S(1)}, f32[128,512]{1,0:T(8,128)S(1)}, u32[]{:S(2)}, u32[]{:S(2)}) collective-permute-start(f32[128,512]{1,0:T(8,128)S(1)} %get-tuple-element.80), channel_id=1, source_target_pairs={{0,7},{1,0},{2,1},{3,2},{4,3},{5,4},{6,5},{7,6},{8,15},{9,8},{10,9... | collective-permute-start | bytes 786440 | tf_op jit(solution)/shard_map/ppermute | solution.py:24
  130.0 16.7 %collective-permute-start.27 = (bf16[512,512]{1,0:T(8,128)(2,1)S(1)}, bf16[512,512]{1,0:T(8,128)(2,1)S(1)}, u32[]{:S(2)}, u32[]{:S(2)}) collective-permute-start(bf16[512,512]{1,0:T(8,128)(2,1)S(1)} %collective-permute-done.18.refs_0_), channel_id=1, source_target_pairs={{0,1},{1,2},{2,3},{3,4},{4,5},{5,6},{6,7},{7,0},{8,9},{9,10},{10,1... | collective-permute-start | bytes 1572872 | tf_op jit(solution)/shard_map/ppermute | solution.py:24
  130.1 16.6 %collective-permute-start.28 = (bf16[512,512]{1,0:T(8,128)(2,1)}, bf16[512,512]{1,0:T(8,128)(2,1)}, u32[]{:S(2)}, u32[]{:S(2)}) collective-permute-start(bf16[512,512]{1,0:T(8,128)(2,1)} %collective-permute-done.26.refs_3_), channel_id=1, source_target_pairs={{0,7},{1,0},{2,1},{3,2},{4,3},{5,4},{6,5},{7,6},{8,15},{9,8},{10,9... | collective-permute-start | bytes 1572872 | tf_op jit(solution)/shard_map/ppermute | solution.py:24
  139.7 11.0 %collective-permute-start.32 = (f32[128,512]{1,0:T(8,128)S(1)}, f32[128,512]{1,0:T(8,128)}, u32[]{:S(2)}, u32[]{:S(2)}) collective-permute-start(f32[128,512]{1,0:T(8,128)S(1)} %add.613.near_ref), channel_id=1, source_target_pairs={{0,128},{128,0},{1,129},{129,1},{2,130},{130,2},{3,131},{131,3},{4... | collective-permute-start | bytes 786440 | tf_op jit(solution)/shard_map/ppermute | solution.py:40
  (21 other events, 202.1 us)
